TPU v7x, 128 devices: a whole 4x4x4 slice. The times are simulated.
128 devices in a mesh: grp: 4 (over y), blk: 32 (over x, z, core).
Axes of the slice: x: 4, y: 4, z: 4, core: 2. Of those that a mesh axis runs over, the one named last changes fastest.
Arguments:
- mass_per_volume: float32 [512, 64, 128], P('blk', 'grp'), may hold values from 0.5 to 2
- flow_vector: float32 [3, 512, 64, 128], P(None, 'blk', 'grp'), may hold values from -4 to 4
- magnetic_vector: float32 [3, 512, 64, 128], P(None, 'blk', 'grp'), may hold values from -4 to 4
- thermal_push: float32 [512, 64, 128], P('blk', 'grp'), may hold values from 1 to 4
- gradient_clipping_flags: int32 [512, 64, 128], P('blk', 'grp'), may hold values 0 or 1
- tracer_launch_volume: int32 [65536, 1], P(('grp', 'blk')), may hold values from 0 to 32767
- tracer_holder_tile: int32 [65536, 1], P(('grp', 'blk')), may hold values from 0 to 31; in each aligned block of 512 rows (0 to 511, 512 to 1023, ...) at most 32 rows name the same one
- holder_local_offset: int32 [65536, 1], P(('grp', 'blk')), may hold values from 0 to 1023
- neutral_thermal_field: float32 [50, 64, 512], P(None, 'blk'), may hold values from 0.5 to 2
- electric_voltage: float32 [64, 512], P('blk'), may hold values from -4 to 4
- reciprocal_operators: float32 [8, 50, 50], replicated, may hold values from 0 to 1
- warming_by_height: float32 [50], replicated, may hold values from 0.005 to 0.05
- pedersen_by_height: float32 [50], replicated, may hold values from 0.005 to 0.02
Outputs:
- conserved_quantities: float32 [8, 512, 64, 128], P(None, 'blk', 'grp')
- ending_thermal_state: float32 [50, 64, 512], P(None, 'blk', 'grp')
- ending_electric_voltage: float32 [64, 512], P('blk', 'grp')
Inputs may be any that keep to these rules, and one draw needn't show every extreme that they name: `tracer_holder_tile`: among the 512 lines of one device at most 32 name the same owner. `tracer_launch_volume`: a cell of the sending device's own region. `holder_local_offset`: lon * 512 + lat inside the owner's 2 longitudes.
All inputs are finite; a program needn't handle non-finite values. No bound on the sum of `gradient_clipping_flags` on one device may be relied on, other than what follows from the above.
Results may differ from a plain program's by a relative error of at most 0.0003.
Values sent between devices are 32-bit elements; how exact they have to be, the bound alone decides.
No kernel may reach another device: no remote copies, remote signals or barrier semaphores. Data moves between devices by JAX's collectives and lax.ppermute only.
A program may use at most 128 MiB of HBM per device.

v0:
```python
import jax
import jax.numpy as jnp
from jax import lax
from jax.sharding import PartitionSpec as P

SUBSTEPS = 2
COUPLINGS = 2
SWEEPS = 4


HEAT_RATIO = 5.0 / 3.0
TIME_STEP = 0.02
DRAG_RATE = 0.5


def padded(block, sides, width):
    for axis, dim in sides:
        count = lax.axis_size(axis)
        forward = [(i, i + 1) for i in range(count - 1)]
        forward.append((count - 1, 0))
        backward = [(target, source) for source, target in forward]
        low = lax.ppermute(
            lax.slice_in_dim(block, block.shape[dim] - width, None, axis=dim), axis, forward
        )
        high = lax.ppermute(lax.slice_in_dim(block, 0, width, axis=dim), axis, backward)
        block = jnp.concatenate([low, block, high], axis=dim)
    return block


def to_conserved(fluid):
    mass_per_volume = fluid[0]
    flow_vector = fluid[1:4]
    magnetic_vector = fluid[4:7]
    thermal_push = fluid[7]
    energy = (
        thermal_push / (HEAT_RATIO - 1.0)
        + 0.5 * mass_per_volume * jnp.sum(flow_vector * flow_vector, axis=0)
        + 0.5 * jnp.sum(magnetic_vector * magnetic_vector, axis=0)
    )
    return jnp.concatenate(
        [mass_per_volume[None], mass_per_volume[None] * flow_vector, magnetic_vector, energy[None]],
        axis=0,
    )


def to_primitive(conserved_quantities):
    mass_per_volume = conserved_quantities[0]
    momentum = conserved_quantities[1:4]
    magnetic_vector = conserved_quantities[4:7]
    thermal_push = (HEAT_RATIO - 1.0) * (
        conserved_quantities[7]
        - 0.5 * jnp.sum(momentum * momentum, axis=0) / mass_per_volume
        - 0.5 * jnp.sum(magnetic_vector * magnetic_vector, axis=0)
    )
    return jnp.concatenate(
        [
            mass_per_volume[None],
            momentum / mass_per_volume[None],
            magnetic_vector,
            thermal_push[None],
        ],
        axis=0,
    )


def physical_flux(fluid, direction):
    mass_per_volume = fluid[0]
    flow_vector = fluid[1:4]
    magnetic_vector = fluid[4:7]
    thermal_push = fluid[7]
    shape = (3,) + (1,) * (fluid.ndim - 1)
    normal = (jnp.arange(3) == direction).astype(jnp.float32).reshape(shape)
    normal_speed = flow_vector[direction]
    normal_field = magnetic_vector[direction]
    field_square = jnp.sum(magnetic_vector * magnetic_vector, axis=0)
    across = jnp.sum(magnetic_vector * magnetic_vector * (1.0 - normal), axis=0)
    total_pressure = thermal_push + 0.5 * field_square
    energy = (
        thermal_push / (HEAT_RATIO - 1.0)
        + 0.5 * mass_per_volume * jnp.sum(flow_vector * flow_vector, axis=0)
        + 0.5 * field_square
    )
    mass_flux = mass_per_volume * normal_speed
    momentum_flux = (
        mass_per_volume * flow_vector * normal_speed
        - normal_field * magnetic_vector
        + total_pressure * normal
    )
    field_flux = normal_speed * magnetic_vector - normal_field * flow_vector
    energy_flux = (energy + total_pressure) * normal_speed - normal_field * jnp.sum(
        flow_vector * magnetic_vector, axis=0
    )
    flux = jnp.concatenate([mass_flux[None], momentum_flux, field_flux, energy_flux[None]], axis=0)
    conserved_quantities = jnp.concatenate(
        [mass_per_volume[None], mass_per_volume[None] * flow_vector, magnetic_vector, energy[None]],
        axis=0,
    )
    sound = HEAT_RATIO * thermal_push / mass_per_volume
    alfven = field_square / mass_per_volume
    transverse = across / mass_per_volume
    fast = 0.5 * (sound + alfven + jnp.sqrt((sound - alfven) ** 2 + 4.0 * sound * transverse))
    return (flux, conserved_quantities, jnp.abs(normal_speed) + jnp.sqrt(fast))


def face_flux(left, right, direction):
    flux_left, state_left, speed_left = physical_flux(left, direction)
    flux_right, state_right, speed_right = physical_flux(right, direction)
    return 0.5 * (flux_left + flux_right) - 0.5 * jnp.maximum(speed_left, speed_right)[None] * (
        state_right - state_left
    )


def limited(forward, backward):
    return (
        0.5
        * (jnp.sign(forward) + jnp.sign(backward))
        * jnp.minimum(jnp.abs(forward), jnp.abs(backward))
    )


def piece_of(values, start, stop, axis):
    return lax.slice_in_dim(values, start, stop, axis=axis)


def sliced_divergence(fluid, limiter, axis):
    count = fluid.shape[axis]
    forward = piece_of(fluid, 1, count, axis) - piece_of(fluid, 0, count - 1, axis)
    slope = (
        limited(piece_of(forward, 1, count - 1, axis), piece_of(forward, 0, count - 2, axis))
        * piece_of(limiter, 1, count - 1, axis - 1)[None]
    )
    centre = piece_of(fluid, 1, count - 1, axis)
    left = piece_of(centre + 0.5 * slope, 0, count - 3, axis)
    right = piece_of(centre - 0.5 * slope, 1, count - 2, axis)
    flux = face_flux(left, right, axis - 1)
    return piece_of(flux, 1, count - 3, axis) - piece_of(flux, 0, count - 4, axis)


def rolled_divergence(fluid, limiter, axis):
    forward = jnp.roll(fluid, -1, axis) - fluid
    slope = limited(forward, jnp.roll(forward, 1, axis)) * limiter[None]
    left = fluid + 0.5 * slope
    right = jnp.roll(fluid - 0.5 * slope, -1, axis)
    flux = face_flux(left, right, axis - 1)
    return flux - jnp.roll(flux, 1, axis)


def advance(extended):
    fluid = extended[:8]
    limiter = extended[8]
    along_x = sliced_divergence(fluid[:, :, 2:-2], limiter[:, 2:-2], 1)
    along_y = sliced_divergence(fluid[:, 2:-2], limiter[2:-2], 2)
    inner = fluid[:, 2:-2, 2:-2]
    inner_limiter = limiter[2:-2, 2:-2]
    along_z = rolled_divergence(inner, inner_limiter, 3)
    return (to_conserved(inner) - TIME_STEP * (along_x + along_y + along_z), inner_limiter)


def halo_cells(fluid, limiter):
    return padded(jnp.concatenate([fluid, limiter[None]], axis=0), (("grp", 2), ("blk", 1)), 2)


def line_payload(extended, margin, fluid, sources, columns):
    size_x = fluid.shape[1]
    size_y = fluid.shape[2]
    field_x = extended[4]
    field_y = extended[5]
    east = field_y[margin + 1 : margin + 1 + size_x, margin : margin + size_y]
    west = field_y[margin - 1 : margin - 1 + size_x, margin : margin + size_y]
    north = field_x[margin : margin + size_x, margin + 1 : margin + 1 + size_y]
    south = field_x[margin : margin + size_x, margin - 1 : margin - 1 + size_y]
    current = 0.5 * (east - west) - 0.5 * (north - south)
    precipitation = fluid[7] * jnp.sqrt(fluid[7] / fluid[0])
    return jnp.stack(
        [
            columns.astype(jnp.float32),
            current.reshape(-1)[sources],
            precipitation.reshape(-1)[sources],
        ],
        axis=0,
    )


def vertical_tridiagonal_update(
    neutral_thermal_field, warming_speed, warming_by_height, reciprocal_operators
):
    forcing_vector_combined = (
        neutral_thermal_field + warming_by_height[:, None, None] * warming_speed[None]
    )
    levels, longs, lats = forcing_vector_combined.shape
    bands = reciprocal_operators.shape[0]
    grouped = forcing_vector_combined.reshape(levels, longs, bands, lats // bands)
    solved = jnp.einsum(
        "bzy,ylbk->zlbk", reciprocal_operators, grouped, precision=lax.Precision.HIGHEST
    )
    return solved.reshape(levels, longs, lats)


def relax(extended, source):
    integrated_pedersen = extended[0]
    electric_voltage = extended[1]
    centre = integrated_pedersen[1:-1, 1:-1]
    east = 0.5 * (centre + integrated_pedersen[2:, 1:-1])
    west = 0.5 * (centre + integrated_pedersen[:-2, 1:-1])
    north = 0.5 * (centre + integrated_pedersen[1:-1, 2:])
    south = 0.5 * (centre + integrated_pedersen[1:-1, :-2])
    total = (
        east * electric_voltage[2:, 1:-1]
        + west * electric_voltage[:-2, 1:-1]
        + north * electric_voltage[1:-1, 2:]
        + south * electric_voltage[1:-1, :-2]
    )
    return (total - source) / (east + west + north + south)


def cycle_margin(integrated_pedersen, electric_voltage):
    extended = padded(jnp.stack([integrated_pedersen, electric_voltage], axis=0), (("blk", 1),), 1)
    return jnp.pad(extended, ((0, 0), (0, 0), (1, 1)))


def apply_drag(conserved_quantities, cells, line_potential, line_conductance):
    flat = conserved_quantities.reshape(conserved_quantities.shape[0], -1)
    push = DRAG_RATE * line_conductance * (flat[0][cells] * line_potential - flat[2][cells])
    added = jax.ops.segment_sum(push, cells, num_segments=flat.shape[1])
    new_energy = flat[7] + (flat[2] * added + 0.5 * added * added) / flat[0]
    flat = flat.at[2].set(flat[2] + added).at[7].set(new_energy)
    return flat.reshape(conserved_quantities.shape)


def table_product(left, right):
    return jnp.dot(left, right, precision=lax.Precision.HIGHEST, preferred_element_type=jnp.float32)


def table_product_back(left, right):
    return lax.dot_general(
        left,
        right,
        (((1,), (1,)), ((), ())),
        precision=lax.Precision.HIGHEST,
        preferred_element_type=jnp.float32,
    )


def body(
    mass_per_volume,
    flow_vector,
    magnetic_vector,
    thermal_push,
    gradient_clipping_flags,
    tracer_launch_volume,
    tracer_holder_tile,
    holder_local_offset,
    neutral_thermal_field,
    electric_voltage,
    reciprocal_operators,
    warming_by_height,
    pedersen_by_height,
):
    groups = lax.axis_size("grp")
    blocks = lax.axis_size("blk")
    group_position = lax.axis_index("grp")
    limiter = gradient_clipping_flags.astype(jnp.float32)
    fluid = jnp.concatenate(
        [mass_per_volume[None], flow_vector, magnetic_vector, thermal_push[None]], axis=0
    )
    sources = tracer_launch_volume[:, 0]
    owners = tracer_holder_tile[:, 0]
    columns = holder_local_offset[:, 0]
    lines = owners.shape[0]
    capacity = 2 * lines // blocks
    slot_count = blocks * capacity
    one_hot = (owners[:, None] == jnp.arange(blocks, dtype=jnp.int32)[None]).astype(jnp.int32)
    rank = jnp.sum((jnp.cumsum(one_hot, axis=0) - one_hot) * one_hot, axis=1)
    slots = owners * capacity + rank
    slot_table = (slots[:, None] == jnp.arange(slot_count, dtype=jnp.int32)[None]).astype(
        jnp.float32
    )
    lon_count, lat_count = electric_voltage.shape
    quarter_factor = lat_count // groups
    warming_map = neutral_thermal_field
    field_potential = electric_voltage
    conserved_quantities = to_conserved(fluid)
    for coupling in range(COUPLINGS):
        margin = 2
        extended = halo_cells(fluid, limiter)
        payload = line_payload(extended, margin, fluid, sources, columns)
        outgoing = table_product(payload, slot_table).reshape(3, blocks, capacity)
        incoming = lax.all_to_all(outgoing, "blk", split_axis=1, concat_axis=1, tiled=True)
        for substep in range(SUBSTEPS):
            if substep > 0:
                extended = halo_cells(to_primitive(conserved_quantities), limiter)
            conserved_quantities, inner_limiter = advance(extended)
        arrived = incoming.reshape(3, slot_count)
        arrived_columns = arrived[0].astype(jnp.int32)
        column_table = (
            arrived_columns[:, None] == jnp.arange(lon_count * lat_count, dtype=jnp.int32)[None]
        ).astype(jnp.float32)
        deposit_table = table_product(arrived[1:3], column_table).reshape(2, lon_count, lat_count)
        arrivals = lax.psum(deposit_table, "grp")
        warming_map = vertical_tridiagonal_update(
            warming_map, arrivals[1], warming_by_height, reciprocal_operators
        )
        integrated_pedersen = jnp.einsum(
            "k,krb->rb", pedersen_by_height, warming_map, precision=lax.Precision.HIGHEST
        )
        for sweep in range(SWEEPS):
            grid_extended = cycle_margin(integrated_pedersen, field_potential)
            field_potential = relax(grid_extended, arrivals[0])
        whole = jnp.stack([field_potential, integrated_pedersen], axis=0)
        answer = table_product_back(whole.reshape(2, -1), column_table).reshape(2, blocks, capacity)
        returned = lax.all_to_all(answer, "blk", split_axis=1, concat_axis=1, tiled=True)
        reply_pair = table_product_back(returned.reshape(2, slot_count), slot_table)
        conserved_quantities = apply_drag(
            conserved_quantities, sources, reply_pair[0], reply_pair[1]
        )
        fluid = to_primitive(conserved_quantities)
    ending_thermal_state = lax.dynamic_slice_in_dim(
        warming_map, group_position * quarter_factor, quarter_factor, 2
    )
    ending_electric_voltage = lax.dynamic_slice_in_dim(
        field_potential, group_position * quarter_factor, quarter_factor, 1
    )
    return (conserved_quantities, ending_thermal_state, ending_electric_voltage)


def solution(mesh):
    in_specs = (
        P("blk", "grp", None),
        P(None, "blk", "grp", None),
        P(None, "blk", "grp", None),
        P("blk", "grp", None),
        P("blk", "grp", None),
        P(("grp", "blk"), None),
        P(("grp", "blk"), None),
        P(("grp", "blk"), None),
        P(None, "blk", None),
        P("blk", None),
        P(),
        P(),
        P(),
    )
    out_specs = (P(None, "blk", "grp", None), P(None, "blk", "grp"), P("blk", "grp"))
    return jax.shard_map(body, mesh=mesh, in_specs=in_specs, out_specs=out_specs, check_vma=False)
```

profile of v0, /device:TPU:0, one launch (start us, length us, event | category | flops | bytes accessed | tf_op | source)
XLA Modules:
  0.0 319.4 jit_solution(18091782720974786370)
XLA Ops:
  23.5 5.5 %collective-permute-start.3 = (f32[9,2,20,128]{3,2,1,0:T(8,128)S(1)}, f32[9,2,20,128]{3,2,1,0:T(8,128)S(1)}, u32[]{:S(2)}, u32[]{:S(2)}) collective-permute-start(f32[9,2,20,128]{3,2,1,0:T(8,128)S(1)} %get-tuple-element.473), channel_id=1, source_target_pairs={{1,0},{2,1},{3,2},{4,3},{5,4},{6,5},{7,6},{8,7},{9,8},{10,9},{11,1... | collective-permute-start | bytes 552968 | tf_op jit(solution)/shard_map/ppermute | solution.py:25
  32.9 4.9 %collective-permute-done.2 = f32[9,2,20,128]{3,2,1,0:T(8,128)S(1)} collective-permute-done((f32[9,2,20,128]{3,2,1,0:T(8,128)S(1)}, f32[9,2,20,128]{3,2,1,0:T(8,128)S(1)}, u32[]{:S(2)}, u32[]{:S(2)}) %collective-permute-start.2) | collective-permute-done | bytes 184352 | tf_op jit(solution)/shard_map/ppermute | solution.py:22
  55.3 4.3 %all-to-all-start = ((f32[3,32,32]{2,0,1:T(4,128)}), f32[3,32,32]{2,0,1:T(4,128)S(1)}, u32[]{:S(2)}, u32[]{:S(2)}) async-start(f32[3,32,32]{2,0,1:T(4,128)} %copy.32), calls=%async_computation | async-start | bytes 131072 | tf_op jit(solution)/shard_map/all_to_all | solution.py:288
  59.6 7.5 %all-to-all-done = f32[3,32,32]{2,0,1:T(4,128)S(1)} async-done(((f32[3,32,32]{2,0,1:T(4,128)}), f32[3,32,32]{2,0,1:T(4,128)S(1)}, u32[]{:S(2)}, u32[]{:S(2)}) %all-to-all-start) | async-done | bytes 12320 | tf_op jit(solution)/shard_map/all_to_all | solution.py:288
  69.3 10.8 %psum.14 = f32[2,2,512]{2,0,1:T(2,128)S(1)} all-reduce(f32[2,2,512]{2,0,1:T(2,128)S(1)} %fusion.4), channel_id=1, replica_groups=mesh['grp'=4,'blk'=32] {'grp'}, use_global_device_ids=true, to_apply=%region_56.57 | all-reduce | flops 2048 | bytes 16384 | tf_op jit(solution)/shard_map/psum | solution.py:299
  83.9 5.1 %collective-permute-done.8 = f32[2,1,512]{2,1,0:T(1,128)S(1)} collective-permute-done((f32[2,1,512]{2,1,0:T(1,128)S(1)}, f32[2,1,512]{2,1,0:T(1,128)S(1)}, u32[]{:S(2)}, u32[]{:S(2)}) %collective-permute-start.8) | collective-permute-done | bytes 4128 | tf_op jit(solution)/shard_map/ppermute | solution.py:22
  99.4 4.0 %collective-permute-done.12 = f32[2,1,512]{2,1,0:T(1,128)S(1)} collective-permute-done((f32[2,1,512]{2,1,0:T(1,128)S(1)}, f32[2,1,512]{2,1,0:T(1,128)S(1)}, u32[]{:S(2)}, u32[]{:S(2)}) %collective-permute-start.12) | collective-permute-done | bytes 4128 | tf_op jit(solution)/shard_map/ppermute | solution.py:22
  106.1 5.0 %collective-permute-done.14 = f32[2,1,512]{2,1,0:T(1,128)S(1)} collective-permute-done((f32[2,1,512]{2,1,0:T(1,128)S(1)}, f32[2,1,512]{2,1,0:T(1,128)S(1)}, u32[]{:S(2)}, u32[]{:S(2)}) %collective-permute-start.14) | collective-permute-done | bytes 4128 | tf_op jit(solution)/shard_map/ppermute | solution.py:22
  111.4 4.9 %fusion = f32[2,32,32]{2,0,1:T(2,128)} fusion(s32[32,32]{1,0:T(8,128)S(1)} %bitcast.1711, f32[1,1024]{1,0:T(1,128)S(1)} %bitcast.1720, f32[1,1024]{1,0:T(1,128)S(1)} %bitcast.1722), kind=kOutput, calls=%fused_computation.12 | convolution fusion | flops 26216448 | bytes 20480 | tf_op jit(solution)/shard_map/dot_general | solution.py:235
  116.2 4.7 %all-to-all-start.1 = ((f32[2,32,32]{2,0,1:T(2,128)}), f32[2,32,32]{2,0,1:T(2,128)}, u32[]{:S(2)}, u32[]{:S(2)}) async-start(f32[2,32,32]{2,0,1:T(2,128)} %fusion), calls=%async_computation.1 | async-start | bytes 65536 | tf_op jit(solution)/shard_map/all_to_all | solution.py:311
  124.2 4.1 %all-to-all-done.1 = f32[2,32,32]{2,0,1:T(2,128)} async-done(((f32[2,32,32]{2,0,1:T(2,128)}), f32[2,32,32]{2,0,1:T(2,128)}, u32[]{:S(2)}, u32[]{:S(2)}) %all-to-all-start.1) | async-done | bytes 8224 | tf_op jit(solution)/shard_map/all_to_all | solution.py:311
  141.7 5.2 %collective-permute-done.6 = f32[9,2,20,128]{3,2,1,0:T(8,128)S(1)} collective-permute-done((f32[9,2,20,128]{3,2,1,0:T(8,128)S(1)}, f32[9,2,20,128]{3,2,1,0:T(8,128)S(1)}, u32[]{:S(2)}, u32[]{:S(2)}) %collective-permute-start.6) | collective-permute-done | bytes 184352 | tf_op jit(solution)/shard_map/ppermute | solution.py:22
  186.6 5.7 %collective-permute-done.18 = f32[9,2,20,128]{3,2,1,0:T(8,128)S(1)} collective-permute-done((f32[9,2,20,128]{3,2,1,0:T(8,128)S(1)}, f32[9,2,20,128]{3,2,1,0:T(8,128)S(1)}, u32[]{:S(2)}, u32[]{:S(2)}) %collective-permute-start.18) | collective-permute-done | bytes 184352 | tf_op jit(solution)/shard_map/ppermute | solution.py:22
  207.6 3.9 %all-to-all-start.2 = ((f32[3,32,32]{2,0,1:T(4,128)}), f32[3,32,32]{2,0,1:T(4,128)S(1)}, u32[]{:S(2)}, u32[]{:S(2)}) async-start(f32[3,32,32]{2,0,1:T(4,128)} %copy.38), calls=%async_computation.2 | async-start | bytes 131072 | tf_op jit(solution)/shard_map/all_to_all | solution.py:288
  214.5 4.5 %all-to-all-done.2 = f32[3,32,32]{2,0,1:T(4,128)S(1)} async-done(((f32[3,32,32]{2,0,1:T(4,128)}), f32[3,32,32]{2,0,1:T(4,128)S(1)}, u32[]{:S(2)}, u32[]{:S(2)}) %all-to-all-start.2) | async-done | bytes 12320 | tf_op jit(solution)/shard_map/all_to_all | solution.py:288
  221.1 9.8 %psum.15 = f32[2,2,512]{2,1,0:T(2,128)S(1)} all-reduce(f32[2,2,512]{2,1,0:T(2,128)S(1)} %copy.40), channel_id=1, replica_groups=mesh['grp'=4,'blk'=32] {'grp'}, use_global_device_ids=true, to_apply=%region_112.113 | all-reduce | flops 2048 | bytes 16384 | tf_op jit(solution)/shard_map/psum | solution.py:299
  234.4 5.1 %collective-permute-done.24 = f32[2,1,512]{2,1,0:T(1,128)S(1)} collective-permute-done((f32[2,1,512]{2,1,0:T(1,128)S(1)}, f32[2,1,512]{2,1,0:T(1,128)S(1)}, u32[]{:S(2)}, u32[]{:S(2)}) %collective-permute-start.24) | collective-permute-done | bytes 4128 | tf_op jit(solution)/shard_map/ppermute | solution.py:22
  242.0 4.2 %collective-permute-done.26 = f32[2,1,512]{2,1,0:T(1,128)S(1)} collective-permute-done((f32[2,1,512]{2,1,0:T(1,128)S(1)}, f32[2,1,512]{2,1,0:T(1,128)S(1)}, u32[]{:S(2)}, u32[]{:S(2)}) %collective-permute-start.26) | collective-permute-done | bytes 4128 | tf_op jit(solution)/shard_map/ppermute | solution.py:22
  248.3 5.0 %collective-permute-done.28 = f32[2,1,512]{2,1,0:T(1,128)S(1)} collective-permute-done((f32[2,1,512]{2,1,0:T(1,128)S(1)}, f32[2,1,512]{2,1,0:T(1,128)S(1)}, u32[]{:S(2)}, u32[]{:S(2)}) %collective-permute-start.28) | collective-permute-done | bytes 4128 | tf_op jit(solution)/shard_map/ppermute | solution.py:22
  255.5 4.5 %collective-permute-done.30 = f32[2,1,512]{2,1,0:T(1,128)S(1)} collective-permute-done((f32[2,1,512]{2,1,0:T(1,128)S(1)}, f32[2,1,512]{2,1,0:T(1,128)S(1)}, u32[]{:S(2)}, u32[]{:S(2)}) %collective-permute-start.30) | collective-permute-done | bytes 4128 | tf_op jit(solution)/shard_map/ppermute | solution.py:22
  260.2 4.8 %fusion.1 = f32[2,32,32]{2,0,1:T(2,128)} fusion(s32[32,32]{1,0:T(8,128)S(1)} %bitcast.1710, f32[1,1024]{1,0:T(1,128)S(1)} %bitcast.1721, f32[1,1024]{1,0:T(1,128)S(1)} %bitcast.1723), kind=kOutput, calls=%fused_computation.13 | convolution fusion | flops 26216448 | bytes 20480 | tf_op jit(solution)/shard_map/dot_general | solution.py:235
  265.1 4.6 %all-to-all-start.3 = ((f32[2,32,32]{2,0,1:T(2,128)}), f32[2,32,32]{2,0,1:T(2,128)}, u32[]{:S(2)}, u32[]{:S(2)}) async-start(f32[2,32,32]{2,0,1:T(2,128)} %fusion.1), calls=%async_computation.3 | async-start | bytes 65536 | tf_op jit(solution)/shard_map/all_to_all | solution.py:311
  270.2 6.7 %all-to-all-done.3 = f32[2,32,32]{2,0,1:T(2,128)} async-done(((f32[2,32,32]{2,0,1:T(2,128)}), f32[2,32,32]{2,0,1:T(2,128)}, u32[]{:S(2)}, u32[]{:S(2)}) %all-to-all-start.3) | async-done | bytes 8224 | tf_op jit(solution)/shard_map/all_to_all | solution.py:311
  290.3 5.4 %collective-permute-done.22 = f32[9,2,20,128]{3,2,1,0:T(8,128)S(1)} collective-permute-done((f32[9,2,20,128]{3,2,1,0:T(8,128)S(1)}, f32[9,2,20,128]{3,2,1,0:T(8,128)S(1)}, u32[]{:S(2)}, u32[]{:S(2)}) %collective-permute-start.22) | collective-permute-done | bytes 184352 | tf_op jit(solution)/shard_map/ppermute | solution.py:22
  (480 shorter events, 186.3 us)
Async XLA Ops:
  5.8 14.5 %collective-permute-start.1 = (f32[9,16,2,128]{3,2,1,0:T(2,128)}, f32[9,16,2,128]{3,2,1,0:T(2,128)}, u32[]{:S(2)}, u32[]{:S(2)}) collective-permute-start(f32[9,16,2,128]{3,2,1,0:T(2,128)} %get-tuple-element.585), channel_id=1, source_target_pairs={{32,0},{64,32},{96,64},{0,96},{33,1},{65,33},{97,65},{1,97},{34,2}... | collective-permute-start | bytes 442376 | tf_op jit(solution)/shard_map/ppermute | solution.py:25
  8.9 11.4 %collective-permute-start = (f32[9,16,2,128]{3,2,1,0:T(2,128)}, f32[9,16,2,128]{3,2,1,0:T(2,128)}, u32[]{:S(2)}, u32[]{:S(2)}) collective-permute-start(f32[9,16,2,128]{3,2,1,0:T(2,128)} %get-tuple-element.584), channel_id=1, source_target_pairs={{0,32},{32,64},{64,96},{96,0},{1,33},{33,65},{65,97},{97,1},{2,34}... | collective-permute-start | bytes 442376 | tf_op jit(solution)/shard_map/ppermute | solution.py:22
  23.5 9.4 %collective-permute-start.3 = (f32[9,2,20,128]{3,2,1,0:T(8,128)S(1)}, f32[9,2,20,128]{3,2,1,0:T(8,128)S(1)}, u32[]{:S(2)}, u32[]{:S(2)}) collective-permute-start(f32[9,2,20,128]{3,2,1,0:T(8,128)S(1)} %get-tuple-element.473), channel_id=1, source_target_pairs={{1,0},{2,1},{3,2},{4,3},{5,4},{6,5},{7,6},{8,7},{9,8},{10,9},{11,1... | collective-permute-start | bytes 552968 | tf_op jit(solution)/shard_map/ppermute | solution.py:25
  28.9 8.8 %collective-permute-start.2 = (f32[9,2,20,128]{3,2,1,0:T(8,128)S(1)}, f32[9,2,20,128]{3,2,1,0:T(8,128)S(1)}, u32[]{:S(2)}, u32[]{:S(2)}) collective-permute-start(f32[9,2,20,128]{3,2,1,0:T(8,128)S(1)} %get-tuple-element.472), channel_id=1, source_target_pairs={{0,1},{1,2},{2,3},{3,4},{4,5},{5,6},{6,7},{7,8},{8,9},{9,10},{10,1... | collective-permute-start | bytes 552968 | tf_op jit(solution)/shard_map/ppermute | solution.py:22
  55.3 11.8 %all-to-all-start = ((f32[3,32,32]{2,0,1:T(4,128)}), f32[3,32,32]{2,0,1:T(4,128)S(1)}, u32[]{:S(2)}, u32[]{:S(2)}) async-start(f32[3,32,32]{2,0,1:T(4,128)} %copy.32), calls=%async_computation | async-start | bytes 131072 | tf_op jit(solution)/shard_map/all_to_all | solution.py:288
  82.6 6.4 %collective-permute-start.8 = (f32[2,1,512]{2,1,0:T(1,128)S(1)}, f32[2,1,512]{2,1,0:T(1,128)S(1)}, u32[]{:S(2)}, u32[]{:S(2)}) collective-permute-start(f32[2,1,512]{2,1,0:T(1,128)S(1)} %get-tuple-element.685), channel_id=1, source_target_pairs={{0,1},{1,2},{2,3},{3,4},{4,5},{5,6},{6,7},{7,8},{8,9},{9,10},{10,1... | collective-permute-start | bytes 12296 | tf_op jit(solution)/shard_map/ppermute | solution.py:22
  89.3 6.4 %collective-permute-start.10 = (f32[2,1,512]{2,1,0:T(1,128)S(1)}, f32[2,1,512]{2,1,0:T(1,128)S(1)}, u32[]{:S(2)}, u32[]{:S(2)}) collective-permute-start(f32[2,1,512]{2,1,0:T(1,128)S(1)} %get-tuple-element.681), channel_id=1, source_target_pairs={{0,1},{1,2},{2,3},{3,4},{4,5},{5,6},{6,7},{7,8},{8,9},{9,10},{10,1... | collective-permute-start | bytes 12296 | tf_op jit(solution)/shard_map/ppermute | solution.py:22
  90.7 40.9 %collective-permute-start.5 = (f32[9,16,2,128]{3,2,1,0:T(2,128)}, f32[9,16,2,128]{3,2,1,0:T(2,128)S(1)}, u32[]{:S(2)}, u32[]{:S(2)}) collective-permute-start(f32[9,16,2,128]{3,2,1,0:T(2,128)} %get-tuple-element.564), channel_id=1, source_target_pairs={{32,0},{64,32},{96,64},{0,96},{33,1},{65,33},{97,65},{1,97},{34,2}... | collective-permute-start | bytes 442376 | tf_op jit(solution)/shard_map/ppermute | solution.py:25
  90.7 40.9 %collective-permute-start.4 = (f32[9,16,2,128]{3,2,1,0:T(2,128)}, f32[9,16,2,128]{3,2,1,0:T(2,128)}, u32[]{:S(2)}, u32[]{:S(2)}) collective-permute-start(f32[9,16,2,128]{3,2,1,0:T(2,128)} %get-tuple-element.563), channel_id=1, source_target_pairs={{0,32},{32,64},{64,96},{96,0},{1,33},{33,65},{65,97},{97,1},{2,34}... | collective-permute-start | bytes 442376 | tf_op jit(solution)/shard_map/ppermute | solution.py:22
  104.8 6.4 %collective-permute-start.14 = (f32[2,1,512]{2,1,0:T(1,128)S(1)}, f32[2,1,512]{2,1,0:T(1,128)S(1)}, u32[]{:S(2)}, u32[]{:S(2)}) collective-permute-start(f32[2,1,512]{2,1,0:T(1,128)S(1)} %get-tuple-element.677), channel_id=1, source_target_pairs={{0,1},{1,2},{2,3},{3,4},{4,5},{5,6},{6,7},{7,8},{8,9},{9,10},{10,1... | collective-permute-start | bytes 12296 | tf_op jit(solution)/shard_map/ppermute | solution.py:22
  116.2 12.1 %all-to-all-start.1 = ((f32[2,32,32]{2,0,1:T(2,128)}), f32[2,32,32]{2,0,1:T(2,128)}, u32[]{:S(2)}, u32[]{:S(2)}) async-start(f32[2,32,32]{2,0,1:T(2,128)} %fusion), calls=%async_computation.1 | async-start | bytes 65536 | tf_op jit(solution)/shard_map/all_to_all | solution.py:311
  138.2 8.7 %collective-permute-start.6 = (f32[9,2,20,128]{3,2,1,0:T(8,128)S(1)}, f32[9,2,20,128]{3,2,1,0:T(8,128)S(1)}, u32[]{:S(2)}, u32[]{:S(2)}) collective-permute-start(f32[9,2,20,128]{3,2,1,0:T(8,128)S(1)} %get-tuple-element.470), channel_id=1, source_target_pairs={{0,1},{1,2},{2,3},{3,4},{4,5},{5,6},{6,7},{7,8},{8,9},{9,10},{10,1... | collective-permute-start | bytes 552968 | tf_op jit(solution)/shard_map/ppermute | solution.py:22
  172.5 7.3 %collective-permute-start.17 = (f32[9,16,2,128]{3,2,1,0:T(2,128)}, f32[9,16,2,128]{3,2,1,0:T(2,128)S(1)}, u32[]{:S(2)}, u32[]{:S(2)}) collective-permute-start(f32[9,16,2,128]{3,2,1,0:T(2,128)} %get-tuple-element.543), channel_id=1, source_target_pairs={{32,0},{64,32},{96,64},{0,96},{33,1},{65,33},{97,65},{1,97},{34,2}... | collective-permute-start | bytes 442376 | tf_op jit(solution)/shard_map/ppermute | solution.py:25
  174.0 6.6 %collective-permute-start.16 = (f32[9,16,2,128]{3,2,1,0:T(2,128)}, f32[9,16,2,128]{3,2,1,0:T(2,128)S(1)}, u32[]{:S(2)}, u32[]{:S(2)}) collective-permute-start(f32[9,16,2,128]{3,2,1,0:T(2,128)} %get-tuple-element.542), channel_id=1, source_target_pairs={{0,32},{32,64},{64,96},{96,0},{1,33},{33,65},{65,97},{97,1},{2,34}... | collective-permute-start | bytes 442376 | tf_op jit(solution)/shard_map/ppermute | solution.py:22
  183.2 9.2 %collective-permute-start.18 = (f32[9,2,20,128]{3,2,1,0:T(8,128)S(1)}, f32[9,2,20,128]{3,2,1,0:T(8,128)S(1)}, u32[]{:S(2)}, u32[]{:S(2)}) collective-permute-start(f32[9,2,20,128]{3,2,1,0:T(8,128)S(1)} %get-tuple-element.468), channel_id=1, source_target_pairs={{0,1},{1,2},{2,3},{3,4},{4,5},{5,6},{6,7},{7,8},{8,9},{9,10},{10,1... | collective-permute-start | bytes 552968 | tf_op jit(solution)/shard_map/ppermute | solution.py:22
  207.6 11.4 %all-to-all-start.2 = ((f32[3,32,32]{2,0,1:T(4,128)}), f32[3,32,32]{2,0,1:T(4,128)S(1)}, u32[]{:S(2)}, u32[]{:S(2)}) async-start(f32[3,32,32]{2,0,1:T(4,128)} %copy.38), calls=%async_computation.2 | async-start | bytes 131072 | tf_op jit(solution)/shard_map/all_to_all | solution.py:288
  212.3 67.9 %collective-permute-start.21 = (f32[9,16,2,128]{3,2,1,0:T(2,128)}, f32[9,16,2,128]{3,2,1,0:T(2,128)S(1)}, u32[]{:S(2)}, u32[]{:S(2)}) collective-permute-start(f32[9,16,2,128]{3,2,1,0:T(2,128)} %get-tuple-element.522), channel_id=1, source_target_pairs={{32,0},{64,32},{96,64},{0,96},{33,1},{65,33},{97,65},{1,97},{34,2}... | collective-permute-start | bytes 442376 | tf_op jit(solution)/shard_map/ppermute | solution.py:25
  214.3 65.9 %collective-permute-start.20 = (f32[9,16,2,128]{3,2,1,0:T(2,128)}, f32[9,16,2,128]{3,2,1,0:T(2,128)}, u32[]{:S(2)}, u32[]{:S(2)}) collective-permute-start(f32[9,16,2,128]{3,2,1,0:T(2,128)} %get-tuple-element.521), channel_id=1, source_target_pairs={{0,32},{32,64},{64,96},{96,0},{1,33},{33,65},{65,97},{97,1},{2,34}... | collective-permute-start | bytes 442376 | tf_op jit(solution)/shard_map/ppermute | solution.py:22
  233.0 6.4 %collective-permute-start.24 = (f32[2,1,512]{2,1,0:T(1,128)S(1)}, f32[2,1,512]{2,1,0:T(1,128)S(1)}, u32[]{:S(2)}, u32[]{:S(2)}) collective-permute-start(f32[2,1,512]{2,1,0:T(1,128)S(1)} %get-tuple-element.675), channel_id=1, source_target_pairs={{0,1},{1,2},{2,3},{3,4},{4,5},{5,6},{6,7},{7,8},{8,9},{9,10},{10,1... | collective-permute-start | bytes 12296 | tf_op jit(solution)/shard_map/ppermute | solution.py:22
  239.8 6.4 %collective-permute-start.26 = (f32[2,1,512]{2,1,0:T(1,128)S(1)}, f32[2,1,512]{2,1,0:T(1,128)S(1)}, u32[]{:S(2)}, u32[]{:S(2)}) collective-permute-start(f32[2,1,512]{2,1,0:T(1,128)S(1)} %get-tuple-element.673), channel_id=1, source_target_pairs={{0,1},{1,2},{2,3},{3,4},{4,5},{5,6},{6,7},{7,8},{8,9},{9,10},{10,1... | collective-permute-start | bytes 12296 | tf_op jit(solution)/shard_map/ppermute | solution.py:22
  246.9 6.4 %collective-permute-start.28 = (f32[2,1,512]{2,1,0:T(1,128)S(1)}, f32[2,1,512]{2,1,0:T(1,128)S(1)}, u32[]{:S(2)}, u32[]{:S(2)}) collective-permute-start(f32[2,1,512]{2,1,0:T(1,128)S(1)} %get-tuple-element.671), channel_id=1, source_target_pairs={{0,1},{1,2},{2,3},{3,4},{4,5},{5,6},{6,7},{7,8},{8,9},{9,10},{10,1... | collective-permute-start | bytes 12296 | tf_op jit(solution)/shard_map/ppermute | solution.py:22
  253.6 6.4 %collective-permute-start.30 = (f32[2,1,512]{2,1,0:T(1,128)S(1)}, f32[2,1,512]{2,1,0:T(1,128)S(1)}, u32[]{:S(2)}, u32[]{:S(2)}) collective-permute-start(f32[2,1,512]{2,1,0:T(1,128)S(1)} %get-tuple-element.669), channel_id=1, source_target_pairs={{0,1},{1,2},{2,3},{3,4},{4,5},{5,6},{6,7},{7,8},{8,9},{9,10},{10,1... | collective-permute-start | bytes 12296 | tf_op jit(solution)/shard_map/ppermute | solution.py:22
  265.1 11.8 %all-to-all-start.3 = ((f32[2,32,32]{2,0,1:T(2,128)}), f32[2,32,32]{2,0,1:T(2,128)}, u32[]{:S(2)}, u32[]{:S(2)}) async-start(f32[2,32,32]{2,0,1:T(2,128)} %fusion.1), calls=%async_computation.3 | async-start | bytes 65536 | tf_op jit(solution)/shard_map/all_to_all | solution.py:311
  286.8 8.9 %collective-permute-start.22 = (f32[9,2,20,128]{3,2,1,0:T(8,128)S(1)}, f32[9,2,20,128]{3,2,1,0:T(8,128)S(1)}, u32[]{:S(2)}, u32[]{:S(2)}) collective-permute-start(f32[9,2,20,128]{3,2,1,0:T(8,128)S(1)} %get-tuple-element.466), channel_id=1, source_target_pairs={{0,1},{1,2},{2,3},{3,4},{4,5},{5,6},{6,7},{7,8},{8,9},{9,10},{10,1... | collective-permute-start | bytes 552968 | tf_op jit(solution)/shard_map/ppermute | solution.py:22
  (67 other events, 562.5 us)
where the time goes:
time: 325 us; the launch traced here: 319 us
  waiting for transfers between devices  86.5 us (27%)
  other arithmetic  82.6 us (25%)
  local copies, waits for them, and re-layouts  63.1 us (19%)
  starting transfers between devices  42.5 us (13%)
  matrix products  21.1 us (6%)
  blocking collectives  20.6 us (6%)
    ppermute x16, waiting for transfers between devices, padded(): lax.ppermute(lax.slice_in_dim(block, block.shape[dim] - width, None, axis...  58 us
    psum x2, blocking collectives, body(): arrivals = lax.psum(deposit_table, 'grp')  20.6 us
    ppermute x16, starting transfers between devices, padded(): lax.ppermute(lax.slice_in_dim(block, 0, width, axis=dim), axis, backward)  18.6 us
    dot_general x4, matrix products, table_product_back(): lax.dot_general(left, right, (((1,), (1,)), ((), ())), precision=lax.Prec...  13.3 us
    all_to_all x2, waiting for transfers between devices, body(): lax.all_to_all(outgoing, 'blk', split_axis=1, concat_axis=1, tiled=True)  12 us
    unnamed x128, local copies, waits for them, and re-layouts  11.6 us
    all_to_all x2, waiting for transfers between devices, body(): lax.all_to_all(answer, 'blk', split_axis=1, concat_axis=1, tiled=True)  10.7 us
    all_to_all x2, starting transfers between devices, body(): lax.all_to_all(answer, 'blk', split_axis=1, concat_axis=1, tiled=True)  9.3 us
  transfers between devices with their start and end apart: 36, of which 24 were waited for; matrix products, arithmetic and copies ran while one was open for 19% of the time, Pallas kernels for 0%

commit v1 on v0

v1 whole, which is shorter than its diff:
```python
import functools

import jax
import jax.numpy as jnp
from jax import lax
from jax.experimental import pallas as pl
from jax.experimental.pallas import tpu as pltpu
from jax.sharding import PartitionSpec as P

SWEEPS = 4
HEAT_RATIO = 5.0 / 3.0
TIME_STEP = 0.02
DRAG_RATE = 0.5
CX = 16
CY = 16
CZ = 128
BLOCKS = 32
CAP = 32
SLOTS = BLOCKS * CAP
LATS = 512
BANDS = 8
F32 = jnp.float32
BF16 = jnp.bfloat16
HIGHEST = lax.Precision.HIGHEST
VMEM_LIMIT = 40 * 1024 * 1024


def shape(*dims):
    return jax.ShapeDtypeStruct(dims, F32)


def kernel_call(body, outs, microseconds, scratch=()):
    return pl.pallas_call(
        body,
        out_shape=outs,
        scratch_shapes=list(scratch),
        compiler_params=pltpu.CompilerParams(vmem_limit_bytes=VMEM_LIMIT),
        cost_estimate=pl.CostEstimate(
            flops=0, bytes_accessed=int(microseconds * 3.3e6), transcendentals=0
        ),
    )


def half_slope(before, centre, after, half_limiter):
    forward = after - centre
    backward = centre - before
    low = jnp.minimum(forward, backward)
    high = jnp.maximum(forward, backward)
    return half_limiter * (jnp.maximum(low, 0.0) + jnp.minimum(high, 0.0))


def side(w, d):
    rho, ux, uy, uz, bx, by, bz, p = w
    u = (ux, uy, uz)
    b = (bx, by, bz)
    e, f = [k for k in range(3) if k != d]
    inverse = 1.0 / rho
    m = [rho * c for c in u]
    across = b[e] * b[e] + b[f] * b[f]
    square = across + b[d] * b[d]
    kinetic = m[0] * ux + m[1] * uy + m[2] * uz
    total = p + 0.5 * square
    energy = 1.5 * p + 0.5 * (kinetic + square)
    along = ux * bx + uy * by + uz * bz
    flux = [None] * 8
    flux[0] = m[d]
    for k in range(3):
        flux[1 + k] = m[k] * u[d] - b[d] * b[k]
        if k != d:
            flux[4 + k] = u[d] * b[k] - b[d] * u[k]
    flux[1 + d] = flux[1 + d] + total
    flux[7] = (energy + total) * u[d] - b[d] * along
    sound = (HEAT_RATIO * p) * inverse
    alfven = square * inverse
    transverse = across * inverse
    gap = sound - alfven
    fast = 0.5 * (sound + alfven + jnp.sqrt(gap * gap + 4.0 * sound * transverse))
    speed = jnp.abs(u[d]) + jnp.sqrt(fast)
    return flux, [rho, m[0], m[1], m[2], bx, by, bz, energy], speed


def face_flux(left, right, d):
    flux_l, state_l, speed_l = side(left, d)
    flux_r, state_r, speed_r = side(right, d)
    speed = 0.5 * jnp.maximum(speed_l, speed_r)
    out = []
    for k in range(8):
        jump = speed * (state_r[k] - state_l[k])
        if flux_l[k] is None:
            out.append(-jump)
        else:
            out.append(0.5 * (flux_l[k] + flux_r[k]) - jump)
    return out


def substep_kernel(mode, split, refs):
    refs = list(refs)
    w_ref, lim_ref = refs[:2]
    faces = refs[2:6]
    lims = refs[6:10]
    refs = refs[10:]
    if split:
        uy_ref = refs[0]
        uy_faces = refs[1:5]
        refs = refs[5:]
    if mode == "final":
        push_ref = refs[0]
        refs = refs[1:]
        out_ref = refs[0]
        outs = ()
        refs = refs[1:]
    else:
        out_ref = refs[0]
        outs = refs[1:9]
        refs = refs[9:]
    ext, lim_ext, lx, hx, lb, ht = refs
    iota = lax.broadcasted_iota(jnp.int32, (CY, CZ), 0)
    first_row = iota == 0
    last_row = iota == CY - 1

    def halo(which, f, r):
        if split:
            if f == 2:
                return uy_faces[which][r]
            f = f if f < 2 else f - 1
        return faces[which][2 * f + r]

    for f in range(8):
        ext[f, 0] = halo(2, f, 0)
        ext[f, 1] = halo(2, f, 1)
        if split and f == 2:
            ext[f, 2 : 2 + CX] = uy_ref[...]
        else:
            ext[f, 2 : 2 + CX] = w_ref[f]
        ext[f, 2 + CX] = halo(3, f, 0)
        ext[f, 3 + CX] = halo(3, f, 1)
    lim_ext[0] = 0.5 * lims[2][...]
    lim_ext[1 : 1 + CX] = 0.5 * lim_ref[...]
    lim_ext[1 + CX] = 0.5 * lims[3][...]

    def row(f, r):
        return ext[f, 2 : 2 + CX, r, :]

    lim_low = 0.5 * lims[0][...]
    lim_high = 0.5 * lims[1][...]
    lim_last = lim_ext[1 : 1 + CX, CY - 1, :]
    left = []
    right = []
    for f in range(8):
        low0, low1 = halo(0, f, 0), halo(0, f, 1)
        high0, high1 = halo(1, f, 0), halo(1, f, 1)
        lb[f] = low1 + half_slope(low0, low1, row(f, 0), lim_low)
        last = row(f, CY - 1)
        left.append(last + half_slope(row(f, CY - 2), last, high0, lim_last))
        right.append(high0 - half_slope(last, high0, high1, lim_high))
    for f, value in enumerate(face_flux(left, right, 1)):
        ht[f] = value

    left = []
    right = []
    for f in range(8):
        a, b, c, d = ext[f, 0], ext[f, 1], ext[f, 2], ext[f, 3]
        left.append(b + half_slope(a, b, c, lim_ext[0]))
        s = half_slope(b, c, d, lim_ext[1])
        right.append(c - s)
        lx[f] = c + s
    for f, value in enumerate(face_flux(left, right, 0)):
        hx[f] = value

    def plane(i, carry):
        lim = lim_ext[i + 1]
        lim_next = lim_ext[i + 2]
        w = [ext[f, i + 2] for f in range(8)]
        left = [lx[f] for f in range(8)]
        right = []
        for f in range(8):
            after = ext[f, i + 3]
            s = half_slope(w[f], after, ext[f, i + 4], lim_next)
            right.append(after - s)
            lx[f] = after + s
        flux = face_flux(left, right, 0)
        total = []
        for f in range(8):
            total.append(flux[f] - hx[f])
            hx[f] = flux[f]
        left = []
        right = []
        for f in range(8):
            before = jnp.where(first_row, halo_row(f, i, 1), pltpu.roll(w[f], 1, 0))
            after = jnp.where(last_row, halo_row(f, i, 2), pltpu.roll(w[f], CY - 1, 0))
            s = half_slope(before, w[f], after, lim)
            right.append(w[f] - s)
            left.append(
                jnp.where(first_row, lb[f, pl.ds(i, 1), :], pltpu.roll(w[f] + s, 1, 0))
            )
        flux = face_flux(left, right, 1)
        for f in range(8):
            upper = jnp.where(
                last_row, ht[f, pl.ds(i, 1), :], pltpu.roll(flux[f], CY - 1, 0)
            )
            total[f] = total[f] + (upper - flux[f])
        left = []
        right = []
        for f in range(8):
            s = half_slope(pltpu.roll(w[f], 1, 1), w[f], pltpu.roll(w[f], CZ - 1, 1), lim)
            left.append(w[f] + s)
            right.append(pltpu.roll(w[f] - s, CZ - 1, 1))
        flux = face_flux(left, right, 2)
        for f in range(8):
            total[f] = total[f] + (flux[f] - pltpu.roll(flux[f], 1, 1))
        rho, ux, uy, uz, bx, by, bz, p = w
        m = [rho * ux, rho * uy, rho * uz]
        energy = 1.5 * p + 0.5 * (
            m[0] * ux + m[1] * uy + m[2] * uz + bx * bx + by * by + bz * bz
        )
        state = [rho, m[0], m[1], m[2], bx, by, bz, energy]
        state = [state[f] - TIME_STEP * total[f] for f in range(8)]
        rho, mx, my, mz, bx, by, bz, energy = state
        if mode == "final":
            added = rho * push_ref[0, i] - my * push_ref[1, i]
            energy = energy + (my * added + 0.5 * added * added) / rho
            result = [rho, mx, my + added, mz, bx, by, bz, energy]
        else:
            inverse = 1.0 / rho
            p = (HEAT_RATIO - 1.0) * (
                energy
                - 0.5 * (mx * mx + my * my + mz * mz) * inverse
                - 0.5 * (bx * bx + by * by + bz * bz)
            )
            result = [rho, mx * inverse, my * inverse, mz * inverse, bx, by, bz, p]
        for f in range(8):
            out_ref[f, i] = result[f]
        return carry

    def halo_row(f, i, which):
        if split and f == 2:
            return uy_faces[0][1, pl.ds(i, 1), :] if which == 1 else uy_faces[1][0, pl.ds(i, 1), :]
        g = (f if f < 2 else f - 1) if split else f
        if which == 1:
            return faces[0][2 * g + 1, pl.ds(i, 1), :]
        return faces[1][2 * g, pl.ds(i, 1), :]

    lax.fori_loop(0, CX, plane, 0)
    if mode != "final":
        write_faces(out_ref, outs, mode == "late")


def write_faces(w_ref, outs, late):
    y_low, y_high, x_low, x_high, bx_low, bx_high, by_low, by_high = outs
    fields = [f for f in range(8) if not (late and f == 2)]
    for g, f in enumerate(fields):
        for r in range(2):
            y_low[2 * g + r] = w_ref[f, :, r, :]
            y_high[2 * g + r] = w_ref[f, :, CY - 2 + r, :]
            x_low[2 * g + r] = w_ref[f, r]
            x_high[2 * g + r] = w_ref[f, CX - 2 + r]
    bx_low[...] = w_ref[4, :, 0, :]
    bx_high[...] = w_ref[4, :, CY - 1, :]
    by_low[...] = w_ref[5, 0]
    by_high[...] = w_ref[5, CX - 1]


def face_shapes(fields):
    return [shape(2 * fields, CX, CZ)] * 4 + [shape(CX, CZ)] * 4


def pack_kernel(rho, u, b, p, flags, w_ref, lim_ref, *outs):
    w_ref[0] = rho[...]
    w_ref[1:4] = u[...]
    w_ref[4:7] = b[...]
    w_ref[7] = p[...]
    lim_ref[...] = flags[...].astype(F32)
    faces, lims = outs[:8], outs[8:]
    write_faces(w_ref, faces, False)
    lims[0][...] = lim_ref[:, 0, :]
    lims[1][...] = lim_ref[:, CY - 1, :]
    lims[2][...] = lim_ref[0]
    lims[3][...] = lim_ref[CX - 1]


def substep(mode, split, args):
    scratch = [
        pltpu.VMEM((8, CX + 4, CY, CZ), F32),
        pltpu.VMEM((CX + 2, CY, CZ), F32),
        pltpu.VMEM((8, CY, CZ), F32),
        pltpu.VMEM((8, CY, CZ), F32),
        pltpu.VMEM((8, CX, CZ), F32),
        pltpu.VMEM((8, CX, CZ), F32),
    ]
    outs = [shape(8, CX, CY, CZ)]
    if mode == "all":
        outs += face_shapes(8)
    elif mode == "late":
        outs += face_shapes(7)

    def body(*refs):
        substep_kernel(mode, split, refs)

    return kernel_call(body, outs, 5.0, scratch)(*args)


def rounded_parts(value, count):
    parts = []
    for _ in range(count):
        part = value.astype(BF16).astype(F32)
        parts.append(part)
        value = value - part
    return parts


def one_hot(positions, extent):
    rows = lax.broadcasted_iota(jnp.int32, (extent, SLOTS), 0)
    return rows == positions.astype(jnp.int32)


def spread(rows, out_ref):
    for t in range(SLOTS // CZ):
        tile = rows[:, t * CZ : (t + 1) * CZ]
        for j in range(CZ // CAP):
            moved = tile if j == 0 else pltpu.roll(tile, CZ - CAP * j, 1)
            out_ref[t * (CZ // CAP) + j] = moved[0:4]


def collect(block_ref, rows_ref):
    lane = lax.broadcasted_iota(jnp.int32, (8, CZ), 1) // CAP
    per = CZ // CAP
    for t in range(SLOTS // CZ):
        total = jnp.zeros((8, CZ), F32)
        for j in range(per):
            block = block_ref[t * per + j]
            block = jnp.concatenate([block, block], axis=0)
            moved = block if j == 0 else pltpu.roll(block, CAP * j, 1)
            total = jnp.where(lane == j, moved, total)
        rows_ref[:, t * CZ : (t + 1) * CZ] = total


def slot_kernel(owner_ref, rows_ref, out_ref):
    count = owner_ref.shape[0]
    owner = owner_ref[...]
    others = rows_ref[4:5, :].astype(jnp.int32)
    here = lax.broadcasted_iota(jnp.int32, (count, count), 0)
    there = lax.broadcasted_iota(jnp.int32, (count, count), 1)
    earlier = jnp.where((owner == others) & (there < here), 1.0, 0.0)
    rank = jnp.sum(earlier, axis=1, keepdims=True)
    slot = owner * CAP + rank.astype(jnp.int32)
    lanes = lax.broadcasted_iota(jnp.int32, (count, SLOTS), 1)
    table = jnp.where(lanes == slot, 1.0, 0.0).astype(BF16)
    found = jnp.dot(rows_ref[...].astype(BF16), table, preferred_element_type=F32)
    out_ref[...] = found
    out_ref[0:1, :] = found[0:1] + found[5:6] - 1.0
    out_ref[2:3, :] = found[2:3] * CZ + found[3:4]


def payload_kernel(w_ref, bx_low, bx_high, by_low, by_high, slot_ref, out_ref, fields, rows):
    iota = lax.broadcasted_iota(jnp.int32, (CY, CZ), 0)
    for x in range(CX):
        east = by_high[...] if x == CX - 1 else w_ref[5, x + 1]
        west = by_low[...] if x == 0 else w_ref[5, x - 1]
        bx = w_ref[4, x]
        north = jnp.where(iota == CY - 1, bx_high[x : x + 1, :], pltpu.roll(bx, CY - 1, 0))
        south = jnp.where(iota == 0, bx_low[x : x + 1, :], pltpu.roll(bx, 1, 0))
        p = w_ref[7, x]
        fields[x * CY : (x + 1) * CY, 0:CZ] = 0.5 * (east - west) - 0.5 * (north - south)
        fields[x * CY : (x + 1) * CY, CZ : 2 * CZ] = p * jnp.sqrt(p / w_ref[0, x])
    cells = one_hot(slot_ref[0:1, :], CX * CY).astype(F32).astype(BF16)
    levels = one_hot(slot_ref[1:2, :], CZ)
    across = fields[...].T
    found = jnp.zeros((2 * CZ, SLOTS), F32)
    for part in rounded_parts(across, 3):
        found = found + jnp.dot(part.astype(BF16), cells, preferred_element_type=F32)
    rows[...] = slot_ref[...]
    for v in range(2):
        kept = jnp.where(levels, found[v * CZ : (v + 1) * CZ], 0.0)
        rows[v : v + 1, :] = jnp.sum(kept, axis=0, keepdims=True)
    spread(rows[...], out_ref)


def deposit(rows, column, out_ref, stack):
    upper = column >= float(LATS)
    place = one_hot(jnp.where(upper, column - LATS, column), LATS).astype(F32).astype(BF16)
    for v in range(2):
        for lon in range(2):
            kept = jnp.where(upper == (lon == 1), rows[v : v + 1, :], 0.0)
            for k, part in enumerate(rounded_parts(kept, 3)):
                at = 4 * k + 2 * v + lon
                stack[at : at + 1, :] = part
    stack[12:16, :] = jnp.zeros((4, SLOTS), F32)
    total = lax.dot_general(
        stack[...].astype(BF16), place, (((1,), (1,)), ((), ())), preferred_element_type=F32
    )
    out_ref[...] = total[0:4] + total[4:8] + total[8:12]


def deposit_first_kernel(block_ref, out_ref, column_ref, rows, stack):
    collect(block_ref, rows)
    column_ref[...] = rows[...]
    deposit(rows[...], rows[2:3, :], out_ref, stack)


def deposit_next_kernel(block_ref, column_ref, out_ref, rows, stack):
    collect(block_ref, rows)
    deposit(rows[...], column_ref[2:3, :], out_ref, stack)


def scatter(block_ref, slot_ref, rows, parts):
    collect(block_ref, rows)
    weight = DRAG_RATE * rows[1:2, :]
    cells = one_hot(slot_ref[0:1, :], CX * CY).astype(F32).astype(BF16)
    levels = one_hot(slot_ref[1:2, :], CZ)
    for v, value in enumerate((weight * rows[0:1, :], weight)):
        for k, part in enumerate(rounded_parts(value, 2)):
            at = (2 * v + k) * CZ
            parts[at : at + CZ, :] = jnp.where(levels, part, 0.0).astype(BF16)
    total = lax.dot_general(
        cells, parts[...], (((1,), (1,)), ((), ())), preferred_element_type=F32
    )
    first = total[:, 0:CZ] + total[:, CZ : 2 * CZ]
    second = total[:, 2 * CZ : 3 * CZ] + total[:, 3 * CZ :]
    return first.reshape(CX, CY, CZ), second.reshape(CX, CY, CZ)


def drag_kernel(block_ref, slot_ref, w_ref, out_ref, y_low, y_high, x_low, x_high, rows, parts):
    first, second = scatter(block_ref, slot_ref, rows, parts)
    out_ref[...] = w_ref[2] * (1.0 - second) + first
    for r in range(2):
        y_low[r] = out_ref[:, r, :]
        y_high[r] = out_ref[:, CY - 2 + r, :]
        x_low[r] = out_ref[r]
        x_high[r] = out_ref[CX - 2 + r]


def scatter_kernel(block_ref, slot_ref, out_ref, rows, parts):
    first, second = scatter(block_ref, slot_ref, rows, parts)
    out_ref[0] = first
    out_ref[1] = second


def base_kernel(inverse_ref, pedersen_ref, warming_ref, thermal_ref, out_ref, factors):
    levels = pedersen_ref.shape[0]
    for band in range(BANDS):
        factors[band : band + 1, :] = jnp.sum(
            pedersen_ref[...] * inverse_ref[band], axis=0, keepdims=True
        )
    once = factors[0:BANDS, :]
    for band in range(BANDS):
        twice = jnp.dot(once, inverse_ref[band], precision=HIGHEST, preferred_element_type=F32)
        factors[BANDS + band : BANDS + band + 1, :] = twice[band : band + 1, :]
    both = factors[...]
    lane_band = lax.broadcasted_iota(jnp.int32, (BANDS, LATS), 1) // (LATS // BANDS)
    own = lane_band == lax.broadcasted_iota(jnp.int32, (BANDS, LATS), 0)

    def pick(values):
        return jnp.sum(jnp.where(own, values, 0.0), axis=0, keepdims=True)

    for lon in range(2):
        field = thermal_ref[:, lon, :]
        found = jnp.dot(both, field, precision=HIGHEST, preferred_element_type=F32)
        out_ref[lon : lon + 1, :] = pick(found[0:BANDS])
        out_ref[2 + lon : 3 + lon, :] = pick(found[BANDS:])
    response = jnp.sum(both * warming_ref[...], axis=1, keepdims=True)
    out_ref[4:5, :] = pick(jnp.broadcast_to(response[0:BANDS], (BANDS, LATS)))
    out_ref[5:6, :] = pick(jnp.broadcast_to(response[BANDS:], (BANDS, LATS)))
    out_ref[6:8, :] = jnp.zeros((2, LATS), F32)


def gather_kernel(at, a, b, c, d, potential, base, out_ref):
    out_ref[0:4, :] = (a[...] + b[...]) + (c[...] + d[...])
    out_ref[4:6, :] = potential[...]
    out_ref[6:8, :] = base[at : at + 2, :]


def sweep_kernel(m2, m1, here, p1, p2, base, column_ref, out_v, out_block, out_base, ext, table):
    for k in range(4):
        for at, ref in enumerate((m2, m1, here, p1, p2)):
            ext[k, 2 * at : 2 * at + 2, :] = ref[2 * k : 2 * k + 2, :]
        ext[k, 10:16, :] = jnp.ones((6, LATS), F32)
    source = ext[0]
    heat = ext[1]
    potential = ext[2]
    conductance = ext[3] + base[4:5, :] * heat
    lane = lax.broadcasted_iota(jnp.int32, (16, LATS), 1)
    first = lane == 0
    last = lane == LATS - 1

    def up(v):
        return jnp.where(last, 0.0, pltpu.roll(v, LATS - 1, 1))

    def down(v):
        return jnp.where(first, 0.0, pltpu.roll(v, 1, 1))

    east = 0.5 * (conductance + pltpu.roll(conductance, 15, 0))
    west = 0.5 * (conductance + pltpu.roll(conductance, 1, 0))
    north = 0.5 * (conductance + up(conductance))
    south = 0.5 * (conductance + down(conductance))
    inverse = 1.0 / (east + west + north + south)
    for _ in range(SWEEPS):
        potential = (
            east * pltpu.roll(potential, 15, 0)
            + west * pltpu.roll(potential, 1, 0)
            + north * up(potential)
            + south * down(potential)
            - source
        ) * inverse
    ext[2] = potential
    ext[3] = conductance
    out_v[...] = ext[2, 4:6, :]
    out_base[...] = base[...]
    out_base[2:4, :] = base[2:4, :] + base[5:6, :] * here[2:4, :]
    for v in range(2):
        for k, part in enumerate(rounded_parts(ext[2 + v, 4:6, :], 3)):
            table[4 * k + 2 * v : 4 * k + 2 * v + 2, :] = part
    table[12:16, :] = jnp.zeros((4, LATS), F32)
    column = column_ref[2:3, :]
    upper = column >= float(LATS)
    place = one_hot(jnp.where(upper, column - LATS, column), LATS).astype(F32).astype(BF16)
    found = jnp.dot(table[...].astype(BF16), place, preferred_element_type=F32)
    found = found[0:4] + found[4:8] + found[8:12]
    voltage = jnp.where(upper, found[1:2], found[0:1])
    weight = jnp.where(upper, found[3:4], found[2:3])
    sub = lax.broadcasted_iota(jnp.int32, (8, SLOTS), 0)
    spread(jnp.where(sub == 0, voltage, weight), out_block)


def thermal_kernel(thermal_ref, inverse_ref, warming_ref, one_ref, two_ref, out_ref):
    low_band = lax.broadcasted_iota(jnp.int32, (thermal_ref.shape[0], CZ), 1) < CZ // 2
    for lon in range(2):
        field = thermal_ref[:, lon, :]
        for sums in (one_ref, two_ref):
            forced = field + warming_ref[...] * sums[2 + lon : 3 + lon, :]
            low = jnp.dot(inverse_ref[0], forced, precision=HIGHEST, preferred_element_type=F32)
            high = jnp.dot(inverse_ref[1], forced, precision=HIGHEST, preferred_element_type=F32)
            field = jnp.where(low_band, low, high)
        out_ref[:, lon, :] = field


def shifted(value, axis, by):
    count = lax.axis_size(axis)
    return lax.ppermute(value, axis, [(i, (i + by) % count) for i in range(count)])


def halos(faces):
    y_low, y_high, x_low, x_high = faces
    return (
        shifted(y_high, "grp", 1),
        shifted(y_low, "grp", -1),
        shifted(x_high, "blk", 1),
        shifted(x_low, "blk", -1),
    )


def body(
    mass_per_volume,
    flow_vector,
    magnetic_vector,
    thermal_push,
    gradient_clipping_flags,
    tracer_launch_volume,
    tracer_holder_tile,
    holder_local_offset,
    neutral_thermal_field,
    electric_voltage,
    reciprocal_operators,
    warming_by_height,
    pedersen_by_height,
):
    group = lax.axis_index("grp")
    lines = tracer_launch_volume.shape[0]
    sources = tracer_launch_volume[:, 0]
    columns = holder_local_offset[:, 0]
    zero = jnp.zeros_like(sources)
    line_rows = jnp.stack(
        [
            sources // CZ,
            sources % CZ,
            columns // CZ,
            columns % CZ,
            tracer_holder_tile[:, 0],
            zero + 1,
            zero,
            zero,
        ],
        axis=0,
    ).astype(F32)
    quarter = LATS // 4

    packed = kernel_call(
        pack_kernel,
        [shape(8, CX, CY, CZ), shape(CX, CY, CZ)] + face_shapes(8) + [shape(CX, CZ)] * 4,
        1.0,
    )(mass_per_volume, flow_vector, magnetic_vector, thermal_push, gradient_clipping_flags)
    fluid, limiter = packed[:2]
    faces, field_faces, limit_faces = packed[2:6], packed[6:10], packed[10:14]
    field_halos = halos(field_faces)
    all_halos = halos(faces)
    limit_halos = halos(limit_faces)

    slots = kernel_call(slot_kernel, shape(8, SLOTS), 1.0)(tracer_holder_tile, line_rows)
    base = kernel_call(
        base_kernel, shape(8, LATS), 2.0, [pltpu.VMEM((2 * BANDS, 50), F32)]
    )(
        reciprocal_operators,
        pedersen_by_height[:, None],
        warming_by_height[None, :],
        neutral_thermal_field,
    )

    rows_scratch = pltpu.VMEM((8, SLOTS), F32)
    stack_scratch = pltpu.VMEM((16, SLOTS), F32)
    parts_scratch = pltpu.VMEM((4 * CZ, SLOTS), BF16)

    def payload(w, near):
        return kernel_call(
            payload_kernel,
            shape(BLOCKS, 4, CZ),
            2.0,
            [pltpu.VMEM((CX * CY, 2 * CZ), F32), rows_scratch],
        )(w, *near, slots)

    def exchange(blocks):
        return lax.all_to_all(blocks, "blk", split_axis=0, concat_axis=0, tiled=True)

    def ionosphere(at, sums, potential, base_now, column):
        terms = [sums] + [shifted(sums, "grp", k) for k in range(1, 4)]
        here = kernel_call(
            functools.partial(gather_kernel, at), shape(8, LATS), 0.3
        )(*terms, potential, base_now)
        around = [shifted(here, "blk", k) for k in (2, 1)]
        around += [here]
        around += [shifted(here, "blk", k) for k in (-1, -2)]
        voltage, reply, base_next = kernel_call(
            sweep_kernel,
            [shape(2, LATS), shape(BLOCKS, 4, CZ), shape(8, LATS)],
            2.0,
            [pltpu.VMEM((4, 16, LATS), F32), pltpu.VMEM((16, LATS), F32)],
        )(*around, base_now, column)
        return here, voltage, exchange(reply), base_next

    arrived = exchange(payload(fluid, field_halos))
    middle = substep("all", False, (fluid, limiter, *all_halos, *limit_halos))
    sums, column = kernel_call(
        deposit_first_kernel,
        [shape(4, LATS), shape(8, SLOTS)],
        1.5,
        [rows_scratch, stack_scratch],
    )(arrived)
    here_one, voltage, returned, base_next = ionosphere(
        0, sums, electric_voltage, base, column
    )
    ended = substep("late", False, (middle[0], limiter, *halos(middle[1:5]), *limit_halos))
    fluid = ended[0]
    late_halos = halos(ended[1:5])
    arrived = exchange(payload(fluid, halos(ended[5:9])))
    dragged = kernel_call(
        drag_kernel,
        [shape(CX, CY, CZ)] + [shape(2, CX, CZ)] * 4,
        2.0,
        [rows_scratch, parts_scratch],
    )(returned, slots, fluid)
    speed, speed_halos = dragged[0], halos(dragged[1:5])
    sums = kernel_call(
        deposit_next_kernel, shape(4, LATS), 1.5, [rows_scratch, stack_scratch]
    )(arrived, column)
    here_two, voltage, returned, base_next = ionosphere(2, sums, voltage, base_next, column)
    middle = substep(
        "all", True, (fluid, limiter, *late_halos, *limit_halos, speed, *speed_halos)
    )
    push = kernel_call(
        scatter_kernel, shape(2, CX, CY, CZ), 2.0, [rows_scratch, parts_scratch]
    )(returned, slots)
    (conserved_quantities,) = substep(
        "final", False, (middle[0], limiter, *halos(middle[1:5]), *limit_halos, push)
    )

    start = group * quarter
    ending_thermal_state = kernel_call(
        thermal_kernel, shape(50, 2, quarter), 2.0
    )(
        lax.dynamic_slice_in_dim(neutral_thermal_field, start, quarter, 2),
        lax.dynamic_slice_in_dim(reciprocal_operators, group * 2, 2, 0),
        warming_by_height[:, None],
        lax.dynamic_slice_in_dim(here_one, start, quarter, 1),
        lax.dynamic_slice_in_dim(here_two, start, quarter, 1),
    )
    ending_electric_voltage = lax.dynamic_slice_in_dim(voltage, start, quarter, 1)
    return (conserved_quantities, ending_thermal_state, ending_electric_voltage)


def solution(mesh):
    in_specs = (
        P("blk", "grp", None),
        P(None, "blk", "grp", None),
        P(None, "blk", "grp", None),
        P("blk", "grp", None),
        P("blk", "grp", None),
        P(("grp", "blk"), None),
        P(("grp", "blk"), None),
        P(("grp", "blk"), None),
        P(None, "blk", None),
        P("blk", None),
        P(),
        P(),
        P(),
    )
    out_specs = (P(None, "blk", "grp", None), P(None, "blk", "grp"), P("blk", "grp"))
    return jax.shard_map(body, mesh=mesh, in_specs=in_specs, out_specs=out_specs, check_vma=False)
```

time: 325 us -> 186 us (0.57); the launches traced: 319 us -> 185 us
  other arithmetic: 82.6 us -> 0.04 us
  local copies, waits for them, and re-layouts: 63.1 us -> 9.97 us
  starting transfers between devices: 42.5 us -> 82.8 us
  Pallas kernels: 0 us -> 39.4 us
  waiting for transfers between devices: 86.5 us -> 51.4 us
  matrix products: 21.1 us -> 0 us
  blocking collectives: 20.6 us -> 0 us
    ppermute x32 -> x46, starting transfers between devices: 25.1 us -> 64.5 us  [shifted(): lax.ppermute(value, axis, [(i, (i + by) % count) for i in range(count)])]
    pallas_call x0 -> x18, Pallas kernels: none -> 39.4 us  [the longest x4 28.6 us: substep(): return kernel_call(body, outs, 5.0, scratch)(*args)]
    sub x52 -> x0, other arithmetic: 26.1 us -> none  [the longest x8 8.58 us: sliced_divergence(): right = piece_of(centre - 0.5 * slope, 1, count - 2, axis)]
    gather x8 -> x0, local copies, waits for them, and re-layouts: 25.1 us -> none  [the longest x2 6.29 us: apply_drag(): flat[0][cells] * line_potential - flat[2][cells]]
    dot_general x12 -> x0, matrix products: 21.1 us -> none  [the longest x4 13.3 us: table_product_back(): lax.dot_general(left, right, (((1,), (1,)), ((), ())), precision=lax.Prec...]
    psum x2 -> x0, blocking collectives: 20.6 us -> none  [body(): arrivals = lax.psum(deposit_table, 'grp')]
    ppermute x32 -> x46, waiting for transfers between devices: 63.7 us -> 44.1 us  [shifted(): lax.ppermute(value, axis, [(i, (i + by) % count) for i in range(count)])]
    all_to_all x4, waiting for transfers between devices: 22.7 us -> 7.28 us  [exchange(): lax.all_to_all(blocks, 'blk', split_axis=0, concat_axis=0, tiled=True)]
  transfers between devices with their start and end apart: 36 -> 50, of which waited for: 24 -> 16; matrix products, arithmetic and copies ran while one was open for 19% -> 1% of each run, Pallas kernels for 0% -> 17%
where the time goes in v1:
time: 186 us; the launch traced here: 185 us
  starting transfers between devices  82.8 us (45%)
  waiting for transfers between devices  51.4 us (28%)
  Pallas kernels  39.4 us (21%)
  local copies, waits for them, and re-layouts  9.97 us (5%)
    ppermute x46, starting transfers between devices, shifted(): lax.ppermute(value, axis, [(i, (i + by) % count) for i in range(count)])  64.5 us
    ppermute x46, waiting for transfers between devices, shifted(): lax.ppermute(value, axis, [(i, (i + by) % count) for i in range(count)])  44.1 us
    pallas_call x4, Pallas kernels, substep(): return kernel_call(body, outs, 5.0, scratch)(*args)  28.6 us
    all_to_all x4, starting transfers between devices, exchange(): lax.all_to_all(blocks, 'blk', split_axis=0, concat_axis=0, tiled=True)  18.3 us
    unnamed x38, local copies, waits for them, and re-layouts  9.12 us
    all_to_all x4, waiting for transfers between devices, exchange(): lax.all_to_all(blocks, 'blk', split_axis=0, concat_axis=0, tiled=True)  7.28 us
  transfers between devices with their start and end apart: 50, of which 16 were waited for; matrix products, arithmetic and copies ran while one was open for 1% of the time, Pallas kernels for 17%

profile of v1, /device:TPU:0, one launch (start us, length us, event | category | flops | bytes accessed | tf_op | source)
XLA Modules:
  0.0 184.6 jit_solution(5178835162716552596)
XLA Ops:
  8.9 5.3 %collective-permute-start.19 = (f32[16,128]{1,0:T(8,128)S(1)}, f32[16,128]{1,0:T(8,128)S(1)}, u32[]{:S(2)}, u32[]{:S(2)}) collective-permute-start(f32[16,128]{1,0:T(8,128)S(1)} %get-tuple-element.71), channel_id=1, source_target_pairs={{0,31},{1,0},{2,1},{3,2},{4,3},{5,4},{6,5},{7,6},{8,7},{9,8},{10,9... | collective-permute-start | bytes 24584 | tf_op jit(solution)/shard_map/ppermute | solution.py:538
  17.6 5.1 %collective-permute-start.3 = (f32[16,16,128]{2,1,0:T(8,128)S(1)}, f32[16,16,128]{2,1,0:T(8,128)S(1)}, u32[]{:S(2)}, u32[]{:S(2)}) collective-permute-start(f32[16,16,128]{2,1,0:T(8,128)S(1)} %get-tuple-element.53), channel_id=1, source_target_pairs={{0,31},{1,0},{2,1},{3,2},{4,3},{5,4},{6,5},{7,6},{8,7},{9,8},{10,9... | collective-permute-start | bytes 393224 | tf_op jit(solution)/shard_map/ppermute | solution.py:538
  25.6 3.9 %all-to-all-start = ((f32[32,4,128]{2,1,0:T(4,128)}), f32[32,4,128]{2,1,0:T(4,128)S(1)}, u32[]{:S(2)}, u32[]{:S(2)}) async-start(f32[32,4,128]{2,1,0:T(4,128)} %shard_map.152), calls=%async_computation | async-start | bytes 131072 | tf_op jit(solution)/shard_map/all_to_all | solution.py:620
  29.6 4.8 %collective-permute-done.4.refs_6_ = f32[16,128]{1,0:T(8,128)S(1)} collective-permute-done((f32[16,128]{1,0:T(8,128)S(1)}, f32[16,128]{1,0:T(8,128)S(1)}, u32[]{:S(2)}, u32[]{:S(2)}) %collective-permute-start.4) | collective-permute-done | bytes 8224 | tf_op jit(solution)/shard_map/ppermute | solution.py:538
  34.4 3.6 %collective-permute-done.5.refs_7_ = f32[16,128]{1,0:T(8,128)S(1)} collective-permute-done((f32[16,128]{1,0:T(8,128)S(1)}, f32[16,128]{1,0:T(8,128)S(1)}, u32[]{:S(2)}, u32[]{:S(2)}) %collective-permute-start.5) | collective-permute-done | bytes 8224 | tf_op jit(solution)/shard_map/ppermute | solution.py:538
  38.1 6.4 %collective-permute-done.6.refs_8_ = f32[16,128]{1,0:T(8,128)S(1)} collective-permute-done((f32[16,128]{1,0:T(8,128)S(1)}, f32[16,128]{1,0:T(8,128)S(1)}, u32[]{:S(2)}, u32[]{:S(2)}) %collective-permute-start.6) | collective-permute-done | bytes 8224 | tf_op jit(solution)/shard_map/ppermute | solution.py:538
  47.7 7.3 %shard_map.149 = (f32[8,16,16,128]{3,2,1,0:T(8,128)S(1)}, f32[16,16,128]{2,1,0:T(8,128)}, f32[16,16,128]{2,1,0:T(8,128)}, f32[16,16,128]{2,1,0:T(8,128)S(1)}, f3...) custom-call(f32[8,16,16,128]{3,2,1,0:T(8,128)S(1)} %get-tuple-elemen, ...), custom_call_target="tpu_custom_call" | custom-call | bytes 16500000 | tf_op jit(solution)/shard_map/pallas_call | solution.py:299
  58.3 5.1 %collective-permute-start.11 = (f32[16,16,128]{2,1,0:T(8,128)S(1)}, f32[16,16,128]{2,1,0:T(8,128)S(1)}, u32[]{:S(2)}, u32[]{:S(2)}) collective-permute-start(f32[16,16,128]{2,1,0:T(8,128)S(1)} %get-tuple-element.62), channel_id=1, source_target_pairs={{0,31},{1,0},{2,1},{3,2},{4,3},{5,4},{6,5},{7,6},{8,7},{9,8},{10,9... | collective-permute-start | bytes 393224 | tf_op jit(solution)/shard_map/ppermute | solution.py:538
  68.3 3.7 %collective-permute-done.26.p2 = f32[8,512]{1,0:T(8,128)S(1)} collective-permute-done((f32[8,512]{1,0:T(8,128)S(1)}, f32[8,512]{1,0:T(8,128)S(1)}, u32[]{:S(2)}, u32[]{:S(2)}) %collective-permute-start.26) | collective-permute-done | bytes 16416 | tf_op jit(solution)/shard_map/ppermute | solution.py:538
  74.7 6.5 %collective-permute-done.24.m1 = f32[8,512]{1,0:T(8,128)S(1)} collective-permute-done((f32[8,512]{1,0:T(8,128)S(1)}, f32[8,512]{1,0:T(8,128)S(1)}, u32[]{:S(2)}, u32[]{:S(2)}) %collective-permute-start.24) | collective-permute-done | bytes 16416 | tf_op jit(solution)/shard_map/ppermute | solution.py:538
  81.2 7.1 %collective-permute-done.23.m2 = f32[8,512]{1,0:T(8,128)S(1)} collective-permute-done((f32[8,512]{1,0:T(8,128)S(1)}, f32[8,512]{1,0:T(8,128)S(1)}, u32[]{:S(2)}, u32[]{:S(2)}) %collective-permute-start.23) | collective-permute-done | bytes 16416 | tf_op jit(solution)/shard_map/ppermute | solution.py:538
  89.6 3.8 %all-to-all-start.1 = ((f32[32,4,128]{2,1,0:T(4,128)}), f32[32,4,128]{2,1,0:T(4,128)S(1)}, u32[]{:S(2)}, u32[]{:S(2)}) async-start(f32[32,4,128]{2,1,0:T(4,128)} %get-tuple-element.74), calls=%async_computation.1 | async-start | bytes 131072 | tf_op jit(solution)/shard_map/all_to_all | solution.py:620
  93.5 6.6 %shard_map.150 = (f32[8,16,16,128]{3,2,1,0:T(8,128)S(1)}, f32[14,16,128]{2,1,0:T(8,128)S(1)}, f32[14,16,128]{2,1,0:T(8,128)S(1)}, f32[14,16,128]{2,1,0:T(8,128)S...) custom-call(f32[8,16,16,128]{3,2,1,0:T(8,128)S(1)} %get-tuple-elemen, ...), custom_call_target="tpu_custom_call" | custom-call | bytes 16500000 | tf_op jit(solution)/shard_map/pallas_call | solution.py:299
  105.2 5.1 %collective-permute-start.38 = (f32[16,128]{1,0:T(8,128)S(1)}, f32[16,128]{1,0:T(8,128)S(1)}, u32[]{:S(2)}, u32[]{:S(2)}) collective-permute-start(f32[16,128]{1,0:T(8,128)S(1)} %get-tuple-element.88), channel_id=1, source_target_pairs={{0,31},{1,0},{2,1},{3,2},{4,3},{5,4},{6,5},{7,6},{8,7},{9,8},{10,9... | collective-permute-start | bytes 24584 | tf_op jit(solution)/shard_map/ppermute | solution.py:538
  113.1 6.8 %all-to-all-start.2 = ((f32[32,4,128]{2,1,0:T(4,128)}), f32[32,4,128]{2,1,0:T(4,128)S(1)}, u32[]{:S(2)}, u32[]{:S(2)}) async-start(f32[32,4,128]{2,1,0:T(4,128)} %shard_map.159), calls=%async_computation.2 | async-start | bytes 131072 | tf_op jit(solution)/shard_map/all_to_all | solution.py:620
  120.6 3.2 %collective-permute-start.28 = (f32[2,16,128]{2,1,0:T(8,128)S(1)}, f32[2,16,128]{2,1,0:T(8,128)S(1)}, u32[]{:S(2)}, u32[]{:S(2)}) collective-permute-start(f32[2,16,128]{2,1,0:T(8,128)S(1)} %get-tuple-element.77), channel_id=1, source_target_pairs={{0,96},{32,0},{64,32},{96,64},{1,97},{33,1},{65,33},{97,65},{2,98}... | collective-permute-start | bytes 49160 | tf_op jit(solution)/shard_map/ppermute | solution.py:538
  123.8 3.2 %collective-permute-start.13 = (f32[14,16,128]{2,1,0:T(8,128)S(1)}, f32[14,16,128]{2,1,0:T(8,128)S(1)}, u32[]{:S(2)}, u32[]{:S(2)}) collective-permute-start(f32[14,16,128]{2,1,0:T(8,128)S(1)} %copy-done.11), channel_id=1, source_target_pairs={{0,96},{32,0},{64,32},{96,64},{1,97},{33,1},{65,33},{97,65},{2,98}... | collective-permute-start | bytes 344072 | tf_op jit(solution)/shard_map/ppermute | solution.py:538
  133.5 3.2 %collective-permute-start.15 = (f32[14,16,128]{2,1,0:T(8,128)S(1)}, f32[14,16,128]{2,1,0:T(8,128)S(1)}, u32[]{:S(2)}, u32[]{:S(2)}) collective-permute-start(f32[14,16,128]{2,1,0:T(8,128)S(1)} %get-tuple-element.67), channel_id=1, source_target_pairs={{0,31},{1,0},{2,1},{3,2},{4,3},{5,4},{6,5},{7,6},{8,7},{9,8},{10,9... | collective-permute-start | bytes 344072 | tf_op jit(solution)/shard_map/ppermute | solution.py:538
  140.8 4.0 %collective-permute-start.44 = (f32[8,512]{1,0:T(8,128)S(1)}, f32[8,512]{1,0:T(8,128)S(1)}, u32[]{:S(2)}, u32[]{:S(2)}) collective-permute-start(f32[8,512]{1,0:T(8,128)S(1)} %shard_map.161.here), channel_id=1, source_target_pairs={{0,31},{1,0},{2,1},{3,2},{4,3},{5,4},{6,5},{7,6},{8,7},{9,8},{10,9... | collective-permute-start | bytes 49160 | tf_op jit(solution)/shard_map/ppermute | solution.py:538
  146.7 7.3 %shard_map.158 = (f32[8,16,16,128]{3,2,1,0:T(8,128)S(1)}, f32[16,16,128]{2,1,0:T(8,128)}, f32[16,16,128]{2,1,0:T(8,128)}, f32[16,16,128]{2,1,0:T(8,128)S(1)}, f3...) custom-call(f32[8,16,16,128]{3,2,1,0:T(8,128)S(1)} %get-tuple-elemen, ...), custom_call_target="tpu_custom_call" | custom-call | bytes 16500000 | tf_op jit(solution)/shard_map/pallas_call | solution.py:299
  157.3 5.1 %collective-permute-start.34 = (f32[16,16,128]{2,1,0:T(8,128)S(1)}, f32[16,16,128]{2,1,0:T(8,128)S(1)}, u32[]{:S(2)}, u32[]{:S(2)}) collective-permute-start(f32[16,16,128]{2,1,0:T(8,128)S(1)} %get-tuple-element.84), channel_id=1, source_target_pairs={{0,31},{1,0},{2,1},{3,2},{4,3},{5,4},{6,5},{7,6},{8,7},{9,8},{10,9... | collective-permute-start | bytes 393224 | tf_op jit(solution)/shard_map/ppermute | solution.py:538
  165.2 3.8 %all-to-all-start.3 = ((f32[32,4,128]{2,1,0:T(4,128)}), f32[32,4,128]{2,1,0:T(4,128)S(1)}, u32[]{:S(2)}, u32[]{:S(2)}) async-start(f32[32,4,128]{2,1,0:T(4,128)} %get-tuple-element.91), calls=%async_computation.3 | async-start | bytes 131072 | tf_op jit(solution)/shard_map/all_to_all | solution.py:620
  169.6 7.0 %all-to-all-done.3.block_ref = f32[32,4,128]{2,1,0:T(4,128)S(1)} async-done(((f32[32,4,128]{2,1,0:T(4,128)}), f32[32,4,128]{2,1,0:T(4,128)S(1)}, u32[]{:S(2)}, u32[]{:S(2)}) %all-to-all-start.3) | async-done | bytes 65568 | tf_op jit(solution)/shard_map/all_to_all | solution.py:620
  177.2 7.3 %shard_map.164 = f32[8,16,16,128]{3,2,1,0:T(8,128)} custom-call(f32[8,16,16,128]{3,2,1,0:T(8,128)S(1)} %get-tuple-element.80.refs_0_, f32[16,16,128]{2,1,0:T(8,128)S(1)} %get-tuple-element.49.refs_1_, f32[16,16,128]{2,1,0:T(8,128)S(1)} %collective-permute-done.31.refs_2_, f32[16,16,128]{2,1,0:T(8,128)S(1)} %collective-permute-done.32.refs_3_, ...), custom_call_target="tpu_custom_call" | custom-call | bytes 16500000 | tf_op jit(solution)/shard_map/pallas_call | solution.py:299
  (146 shorter events, 58.4 us)
Async XLA Ops:
  8.9 15.3 %collective-permute-start.19 = (f32[16,128]{1,0:T(8,128)S(1)}, f32[16,128]{1,0:T(8,128)S(1)}, u32[]{:S(2)}, u32[]{:S(2)}) collective-permute-start(f32[16,128]{1,0:T(8,128)S(1)} %get-tuple-element.71), channel_id=1, source_target_pairs={{0,31},{1,0},{2,1},{3,2},{4,3},{5,4},{6,5},{7,6},{8,7},{9,8},{10,9... | collective-permute-start | bytes 24584 | tf_op jit(solution)/shard_map/ppermute | solution.py:538
  14.2 32.8 %collective-permute-start = (f32[16,16,128]{2,1,0:T(8,128)S(1)}, f32[16,16,128]{2,1,0:T(8,128)S(1)}, u32[]{:S(2)}, u32[]{:S(2)}) collective-permute-start(f32[16,16,128]{2,1,0:T(8,128)S(1)} %get-tuple-element.50), channel_id=1, source_target_pairs={{0,32},{32,64},{64,96},{96,0},{1,33},{33,65},{65,97},{97,1},{2,34}... | collective-permute-start | bytes 393224 | tf_op jit(solution)/shard_map/ppermute | solution.py:538
  14.5 33.1 %collective-permute-start.1 = (f32[16,16,128]{2,1,0:T(8,128)S(1)}, f32[16,16,128]{2,1,0:T(8,128)S(1)}, u32[]{:S(2)}, u32[]{:S(2)}) collective-permute-start(f32[16,16,128]{2,1,0:T(8,128)S(1)} %get-tuple-element.51), channel_id=1, source_target_pairs={{0,96},{32,0},{64,32},{96,64},{1,97},{33,1},{65,33},{97,65},{2,98}... | collective-permute-start | bytes 393224 | tf_op jit(solution)/shard_map/ppermute | solution.py:538
  17.6 30.1 %collective-permute-start.2 = (f32[16,16,128]{2,1,0:T(8,128)S(1)}, f32[16,16,128]{2,1,0:T(8,128)S(1)}, u32[]{:S(2)}, u32[]{:S(2)}) collective-permute-start(f32[16,16,128]{2,1,0:T(8,128)S(1)} %get-tuple-element.52), channel_id=1, source_target_pairs={{0,1},{1,2},{2,3},{3,4},{4,5},{5,6},{6,7},{7,8},{8,9},{9,10},{10,1... | collective-permute-start | bytes 393224 | tf_op jit(solution)/shard_map/ppermute | solution.py:538
  17.6 30.1 %collective-permute-start.3 = (f32[16,16,128]{2,1,0:T(8,128)S(1)}, f32[16,16,128]{2,1,0:T(8,128)S(1)}, u32[]{:S(2)}, u32[]{:S(2)}) collective-permute-start(f32[16,16,128]{2,1,0:T(8,128)S(1)} %get-tuple-element.53), channel_id=1, source_target_pairs={{0,31},{1,0},{2,1},{3,2},{4,3},{5,4},{6,5},{7,6},{8,7},{9,8},{10,9... | collective-permute-start | bytes 393224 | tf_op jit(solution)/shard_map/ppermute | solution.py:538
  25.6 18.8 %all-to-all-start = ((f32[32,4,128]{2,1,0:T(4,128)}), f32[32,4,128]{2,1,0:T(4,128)S(1)}, u32[]{:S(2)}, u32[]{:S(2)}) async-start(f32[32,4,128]{2,1,0:T(4,128)} %shard_map.152), calls=%async_computation | async-start | bytes 131072 | tf_op jit(solution)/shard_map/all_to_all | solution.py:620
  47.1 16.3 %collective-permute-start.21 = (f32[4,512]{1,0:T(4,128)S(1)}, f32[4,512]{1,0:T(4,128)S(1)}, u32[]{:S(2)}, u32[]{:S(2)}) collective-permute-start(f32[4,512]{1,0:T(4,128)S(1)} %get-tuple-element.72.a), channel_id=1, source_target_pairs={{0,64},{32,96},{64,0},{96,32},{1,65},{33,97},{65,1},{97,33},{2,66}... | collective-permute-start | bytes 24584 | tf_op jit(solution)/shard_map/ppermute | solution.py:538
  55.0 38.4 %collective-permute-start.8 = (f32[16,16,128]{2,1,0:T(8,128)}, f32[16,16,128]{2,1,0:T(8,128)S(1)}, u32[]{:S(2)}, u32[]{:S(2)}) collective-permute-start(f32[16,16,128]{2,1,0:T(8,128)} %get-tuple-element.59), channel_id=1, source_target_pairs={{0,32},{32,64},{64,96},{96,0},{1,33},{33,65},{65,97},{97,1},{2,34}... | collective-permute-start | bytes 393224 | tf_op jit(solution)/shard_map/ppermute | solution.py:538
  55.3 38.1 %collective-permute-start.9 = (f32[16,16,128]{2,1,0:T(8,128)}, f32[16,16,128]{2,1,0:T(8,128)S(1)}, u32[]{:S(2)}, u32[]{:S(2)}) collective-permute-start(f32[16,16,128]{2,1,0:T(8,128)} %get-tuple-element.60), channel_id=1, source_target_pairs={{0,96},{32,0},{64,32},{96,64},{1,97},{33,1},{65,33},{97,65},{2,98}... | collective-permute-start | bytes 393224 | tf_op jit(solution)/shard_map/ppermute | solution.py:538
  58.3 35.2 %collective-permute-start.10 = (f32[16,16,128]{2,1,0:T(8,128)}, f32[16,16,128]{2,1,0:T(8,128)S(1)}, u32[]{:S(2)}, u32[]{:S(2)}) collective-permute-start(f32[16,16,128]{2,1,0:T(8,128)} %get-tuple-element.61), channel_id=1, source_target_pairs={{0,1},{1,2},{2,3},{3,4},{4,5},{5,6},{6,7},{7,8},{8,9},{9,10},{10,1... | collective-permute-start | bytes 393224 | tf_op jit(solution)/shard_map/ppermute | solution.py:538
  58.3 35.2 %collective-permute-start.11 = (f32[16,16,128]{2,1,0:T(8,128)S(1)}, f32[16,16,128]{2,1,0:T(8,128)S(1)}, u32[]{:S(2)}, u32[]{:S(2)}) collective-permute-start(f32[16,16,128]{2,1,0:T(8,128)S(1)} %get-tuple-element.62), channel_id=1, source_target_pairs={{0,31},{1,0},{2,1},{3,2},{4,3},{5,4},{6,5},{7,6},{8,7},{9,8},{10,9... | collective-permute-start | bytes 393224 | tf_op jit(solution)/shard_map/ppermute | solution.py:538
  89.6 23.5 %all-to-all-start.1 = ((f32[32,4,128]{2,1,0:T(4,128)}), f32[32,4,128]{2,1,0:T(4,128)S(1)}, u32[]{:S(2)}, u32[]{:S(2)}) async-start(f32[32,4,128]{2,1,0:T(4,128)} %get-tuple-element.74), calls=%async_computation.1 | async-start | bytes 131072 | tf_op jit(solution)/shard_map/all_to_all | solution.py:620
  113.1 14.3 %all-to-all-start.2 = ((f32[32,4,128]{2,1,0:T(4,128)}), f32[32,4,128]{2,1,0:T(4,128)S(1)}, u32[]{:S(2)}, u32[]{:S(2)}) async-start(f32[32,4,128]{2,1,0:T(4,128)} %shard_map.159), calls=%async_computation.2 | async-start | bytes 131072 | tf_op jit(solution)/shard_map/all_to_all | solution.py:620
  123.8 16.9 %collective-permute-start.12 = (f32[14,16,128]{2,1,0:T(8,128)S(1)}, f32[14,16,128]{2,1,0:T(8,128)S(1)}, u32[]{:S(2)}, u32[]{:S(2)}) collective-permute-start(f32[14,16,128]{2,1,0:T(8,128)S(1)} %copy-done.13), channel_id=1, source_target_pairs={{0,32},{32,64},{64,96},{96,0},{1,33},{33,65},{65,97},{97,1},{2,34}... | collective-permute-start | bytes 344072 | tf_op jit(solution)/shard_map/ppermute | solution.py:538
  123.8 20.9 %collective-permute-start.13 = (f32[14,16,128]{2,1,0:T(8,128)S(1)}, f32[14,16,128]{2,1,0:T(8,128)S(1)}, u32[]{:S(2)}, u32[]{:S(2)}) collective-permute-start(f32[14,16,128]{2,1,0:T(8,128)S(1)} %copy-done.11), channel_id=1, source_target_pairs={{0,96},{32,0},{64,32},{96,64},{1,97},{33,1},{65,33},{97,65},{2,98}... | collective-permute-start | bytes 344072 | tf_op jit(solution)/shard_map/ppermute | solution.py:538
  131.6 13.2 %collective-permute-start.14 = (f32[14,16,128]{2,1,0:T(8,128)S(1)}, f32[14,16,128]{2,1,0:T(8,128)S(1)}, u32[]{:S(2)}, u32[]{:S(2)}) collective-permute-start(f32[14,16,128]{2,1,0:T(8,128)S(1)} %copy-done.9), channel_id=1, source_target_pairs={{0,1},{1,2},{2,3},{3,4},{4,5},{5,6},{6,7},{7,8},{8,9},{9,10},{10,1... | collective-permute-start | bytes 344072 | tf_op jit(solution)/shard_map/ppermute | solution.py:538
  133.5 13.2 %collective-permute-start.15 = (f32[14,16,128]{2,1,0:T(8,128)S(1)}, f32[14,16,128]{2,1,0:T(8,128)S(1)}, u32[]{:S(2)}, u32[]{:S(2)}) collective-permute-start(f32[14,16,128]{2,1,0:T(8,128)S(1)} %get-tuple-element.67), channel_id=1, source_target_pairs={{0,31},{1,0},{2,1},{3,2},{4,3},{5,4},{6,5},{7,6},{8,7},{9,8},{10,9... | collective-permute-start | bytes 344072 | tf_op jit(solution)/shard_map/ppermute | solution.py:538
  139.6 16.4 %collective-permute-start.45 = (f32[8,512]{1,0:T(8,128)S(1)}, f32[8,512]{1,0:T(8,128)S(1)}, u32[]{:S(2)}, u32[]{:S(2)}) collective-permute-start(f32[8,512]{1,0:T(8,128)S(1)} %shard_map.161.here), channel_id=1, source_target_pairs={{0,30},{1,31},{2,0},{3,1},{4,2},{5,3},{6,4},{7,5},{8,6},{9,7},{10,... | collective-permute-start | bytes 49160 | tf_op jit(solution)/shard_map/ppermute | solution.py:538
  140.8 16.6 %collective-permute-start.44 = (f32[8,512]{1,0:T(8,128)S(1)}, f32[8,512]{1,0:T(8,128)S(1)}, u32[]{:S(2)}, u32[]{:S(2)}) collective-permute-start(f32[8,512]{1,0:T(8,128)S(1)} %shard_map.161.here), channel_id=1, source_target_pairs={{0,31},{1,0},{2,1},{3,2},{4,3},{5,4},{6,5},{7,6},{8,7},{9,8},{10,9... | collective-permute-start | bytes 49160 | tf_op jit(solution)/shard_map/ppermute | solution.py:538
  144.9 19.0 %collective-permute-start.42 = (f32[8,512]{1,0:T(8,128)S(1)}, f32[8,512]{1,0:T(8,128)S(1)}, u32[]{:S(2)}, u32[]{:S(2)}) collective-permute-start(f32[8,512]{1,0:T(8,128)S(1)} %shard_map.161.here), channel_id=1, source_target_pairs={{0,2},{1,3},{2,4},{3,5},{4,6},{5,7},{6,8},{7,9},{8,10},{9,11},{10,... | collective-permute-start | bytes 49160 | tf_op jit(solution)/shard_map/ppermute | solution.py:538
  154.1 23.1 %collective-permute-start.31 = (f32[16,16,128]{2,1,0:T(8,128)}, f32[16,16,128]{2,1,0:T(8,128)S(1)}, u32[]{:S(2)}, u32[]{:S(2)}) collective-permute-start(f32[16,16,128]{2,1,0:T(8,128)} %get-tuple-element.81), channel_id=1, source_target_pairs={{0,32},{32,64},{64,96},{96,0},{1,33},{33,65},{65,97},{97,1},{2,34}... | collective-permute-start | bytes 393224 | tf_op jit(solution)/shard_map/ppermute | solution.py:538
  156.0 21.2 %collective-permute-start.32 = (f32[16,16,128]{2,1,0:T(8,128)}, f32[16,16,128]{2,1,0:T(8,128)S(1)}, u32[]{:S(2)}, u32[]{:S(2)}) collective-permute-start(f32[16,16,128]{2,1,0:T(8,128)} %get-tuple-element.82), channel_id=1, source_target_pairs={{0,96},{32,0},{64,32},{96,64},{1,97},{33,1},{65,33},{97,65},{2,98}... | collective-permute-start | bytes 393224 | tf_op jit(solution)/shard_map/ppermute | solution.py:538
  157.3 19.9 %collective-permute-start.33 = (f32[16,16,128]{2,1,0:T(8,128)}, f32[16,16,128]{2,1,0:T(8,128)S(1)}, u32[]{:S(2)}, u32[]{:S(2)}) collective-permute-start(f32[16,16,128]{2,1,0:T(8,128)} %get-tuple-element.83), channel_id=1, source_target_pairs={{0,1},{1,2},{2,3},{3,4},{4,5},{5,6},{6,7},{7,8},{8,9},{9,10},{10,1... | collective-permute-start | bytes 393224 | tf_op jit(solution)/shard_map/ppermute | solution.py:538
  157.3 19.9 %collective-permute-start.34 = (f32[16,16,128]{2,1,0:T(8,128)S(1)}, f32[16,16,128]{2,1,0:T(8,128)S(1)}, u32[]{:S(2)}, u32[]{:S(2)}) collective-permute-start(f32[16,16,128]{2,1,0:T(8,128)S(1)} %get-tuple-element.84), channel_id=1, source_target_pairs={{0,31},{1,0},{2,1},{3,2},{4,3},{5,4},{6,5},{7,6},{8,7},{9,8},{10,9... | collective-permute-start | bytes 393224 | tf_op jit(solution)/shard_map/ppermute | solution.py:538
  (44 other events, 218.9 us)

commit v2 on v1

--- a/solution.py
+++ b/solution.py
@@ -44,9 +44,9 @@
 def half_slope(before, centre, after, half_limiter):
     forward = after - centre
     backward = centre - before
-    low = jnp.minimum(forward, backward)
-    high = jnp.maximum(forward, backward)
-    return half_limiter * (jnp.maximum(low, 0.0) + jnp.minimum(high, 0.0))
+    low = jnp.minimum(backward, 0.0)
+    high = jnp.maximum(backward, 0.0)
+    return half_limiter * jnp.minimum(jnp.maximum(forward, low), high)
 
 
 def side(w, d):
@@ -82,15 +82,19 @@
 def face_flux(left, right, d):
     flux_l, state_l, speed_l = side(left, d)
     flux_r, state_r, speed_r = side(right, d)
-    speed = 0.5 * jnp.maximum(speed_l, speed_r)
+    speed = jnp.maximum(speed_l, speed_r)
     out = []
     for k in range(8):
         jump = speed * (state_r[k] - state_l[k])
         if flux_l[k] is None:
             out.append(-jump)
         else:
-            out.append(0.5 * (flux_l[k] + flux_r[k]) - jump)
+            out.append(flux_l[k] + flux_r[k] - jump)
     return out
+
+
+def core():
+    return lax.rem(lax.axis_index("blk"), 2)
 
 
 def substep_kernel(mode, split, refs):
@@ -104,19 +108,17 @@
         uy_faces = refs[1:5]
         refs = refs[5:]
     if mode == "final":
-        push_ref = refs[0]
-        refs = refs[1:]
         out_ref = refs[0]
         outs = ()
         refs = refs[1:]
     else:
         out_ref = refs[0]
-        outs = refs[1:9]
-        refs = refs[9:]
-    ext, lim_ext, lx, hx, lb, ht = refs
-    iota = lax.broadcasted_iota(jnp.int32, (CY, CZ), 0)
-    first_row = iota == 0
-    last_row = iota == CY - 1
+        outs = refs[1:5]
+        refs = refs[5:]
+    ext, lim_ext, turned, lim_turned, across, lx, hx = refs
+    even = core() == 0
+    place_a = jnp.where(even, CX + 2, 0)
+    place_b = CX + 2 - place_a
 
     def halo(which, f, r):
         if split:
@@ -126,79 +128,69 @@
         return faces[which][2 * f + r]
 
     for f in range(8):
-        ext[f, 0] = halo(2, f, 0)
-        ext[f, 1] = halo(2, f, 1)
-        if split and f == 2:
-            ext[f, 2 : 2 + CX] = uy_ref[...]
-        else:
-            ext[f, 2 : 2 + CX] = w_ref[f]
-        ext[f, 2 + CX] = halo(3, f, 0)
-        ext[f, 3 + CX] = halo(3, f, 1)
-    lim_ext[0] = 0.5 * lims[2][...]
+        for r in range(2):
+            ext[f, place_a + r] = halo(2, f, r)
+            ext[f, place_b + r] = halo(3, f, r)
+            turned[f, r] = halo(0, f, r)
+            turned[f, CY + 2 + r] = halo(1, f, r)
+        centre = uy_ref if split and f == 2 else w_ref.at[f]
+        ext[f, 2 : 2 + CX] = centre[...]
+        for y in range(CY):
+            turned[f, 2 + y] = centre[:, y, :]
     lim_ext[1 : 1 + CX] = 0.5 * lim_ref[...]
-    lim_ext[1 + CX] = 0.5 * lims[3][...]
-
-    def row(f, r):
-        return ext[f, 2 : 2 + CX, r, :]
-
-    lim_low = 0.5 * lims[0][...]
-    lim_high = 0.5 * lims[1][...]
-    lim_last = lim_ext[1 : 1 + CX, CY - 1, :]
-    left = []
-    right = []
-    for f in range(8):
-        low0, low1 = halo(0, f, 0), halo(0, f, 1)
-        high0, high1 = halo(1, f, 0), halo(1, f, 1)
-        lb[f] = low1 + half_slope(low0, low1, row(f, 0), lim_low)
-        last = row(f, CY - 1)
-        left.append(last + half_slope(row(f, CY - 2), last, high0, lim_last))
-        right.append(high0 - half_slope(last, high0, high1, lim_high))
-    for f, value in enumerate(face_flux(left, right, 1)):
-        ht[f] = value
-
-    left = []
-    right = []
-    for f in range(8):
-        a, b, c, d = ext[f, 0], ext[f, 1], ext[f, 2], ext[f, 3]
-        left.append(b + half_slope(a, b, c, lim_ext[0]))
-        s = half_slope(b, c, d, lim_ext[1])
-        right.append(c - s)
-        lx[f] = c + s
-    for f, value in enumerate(face_flux(left, right, 0)):
-        hx[f] = value
-
-    def plane(i, carry):
-        lim = lim_ext[i + 1]
-        lim_next = lim_ext[i + 2]
-        w = [ext[f, i + 2] for f in range(8)]
+    place = jnp.where(even, CX + 1, 0)
+    lim_ext[place] = 0.5 * lims[2][16]
+    lim_ext[CX + 1 - place] = 0.5 * lims[3][16]
+    lim_turned[0] = 0.5 * lims[0][16]
+    lim_turned[CY + 1] = 0.5 * lims[1][16]
+    for y in range(CY):
+        lim_turned[1 + y] = 0.5 * lim_ref[:, y, :]
+
+    def lowest(w, lim, d):
+        left = []
+        right = []
+        for f in range(8):
+            p, q, r, s = w[f, 0], w[f, 1], w[f, 2], w[f, 3]
+            left.append(q + half_slope(p, q, r, lim[0]))
+            slope = half_slope(q, r, s, lim[1])
+            right.append(r - slope)
+            lx[f] = r + slope
+        for f, value in enumerate(face_flux(left, right, d)):
+            hx[f] = value
+
+    def next_face(w, lim, i, d):
         left = [lx[f] for f in range(8)]
         right = []
         for f in range(8):
-            after = ext[f, i + 3]
-            s = half_slope(w[f], after, ext[f, i + 4], lim_next)
-            right.append(after - s)
-            lx[f] = after + s
-        flux = face_flux(left, right, 0)
-        total = []
+            after = w[f, i + 3]
+            slope = half_slope(w[f, i + 2], after, w[f, i + 4], lim[i + 2])
+            right.append(after - slope)
+            lx[f] = after + slope
+        flux = face_flux(left, right, d)
+        difference = []
         for f in range(8):
-            total.append(flux[f] - hx[f])
+            difference.append(flux[f] - hx[f])
             hx[f] = flux[f]
-        left = []
-        right = []
-        for f in range(8):
-            before = jnp.where(first_row, halo_row(f, i, 1), pltpu.roll(w[f], 1, 0))
-            after = jnp.where(last_row, halo_row(f, i, 2), pltpu.roll(w[f], CY - 1, 0))
-            s = half_slope(before, w[f], after, lim)
-            right.append(w[f] - s)
-            left.append(
-                jnp.where(first_row, lb[f, pl.ds(i, 1), :], pltpu.roll(w[f] + s, 1, 0))
-            )
-        flux = face_flux(left, right, 1)
-        for f in range(8):
-            upper = jnp.where(
-                last_row, ht[f, pl.ds(i, 1), :], pltpu.roll(flux[f], CY - 1, 0)
-            )
-            total[f] = total[f] + (upper - flux[f])
+        return difference
+
+    lowest(turned, lim_turned, 1)
+
+    def row(i, carry):
+        for f, value in enumerate(next_face(turned, lim_turned, i, 1)):
+            turned[f, i] = value
+        return carry
+
+    lax.fori_loop(0, CY, row, 0, unroll=2)
+    for f in range(8):
+        for x in range(CX):
+            across[f, x] = turned[f, 0:CY, x, :]
+
+    lowest(ext, lim_ext, 0)
+
+    def plane(i, carry):
+        lim = lim_ext[i + 1]
+        w = [ext[f, i + 2] for f in range(8)]
+        total = next_face(ext, lim_ext, i, 0)
         left = []
         right = []
         for f in range(8):
@@ -207,19 +199,17 @@
             right.append(pltpu.roll(w[f] - s, CZ - 1, 1))
         flux = face_flux(left, right, 2)
         for f in range(8):
-            total[f] = total[f] + (flux[f] - pltpu.roll(flux[f], 1, 1))
+            total[f] = (total[f] + across[f, i]) + (flux[f] - pltpu.roll(flux[f], 1, 1))
         rho, ux, uy, uz, bx, by, bz, p = w
         m = [rho * ux, rho * uy, rho * uz]
         energy = 1.5 * p + 0.5 * (
             m[0] * ux + m[1] * uy + m[2] * uz + bx * bx + by * by + bz * bz
         )
         state = [rho, m[0], m[1], m[2], bx, by, bz, energy]
-        state = [state[f] - TIME_STEP * total[f] for f in range(8)]
+        state = [state[f] - (0.5 * TIME_STEP) * total[f] for f in range(8)]
         rho, mx, my, mz, bx, by, bz, energy = state
         if mode == "final":
-            added = rho * push_ref[0, i] - my * push_ref[1, i]
-            energy = energy + (my * added + 0.5 * added * added) / rho
-            result = [rho, mx, my + added, mz, bx, by, bz, energy]
+            result = state
         else:
             inverse = 1.0 / rho
             p = (HEAT_RATIO - 1.0) * (
@@ -232,66 +222,63 @@
             out_ref[f, i] = result[f]
         return carry
 
-    def halo_row(f, i, which):
-        if split and f == 2:
-            return uy_faces[0][1, pl.ds(i, 1), :] if which == 1 else uy_faces[1][0, pl.ds(i, 1), :]
-        g = (f if f < 2 else f - 1) if split else f
-        if which == 1:
-            return faces[0][2 * g + 1, pl.ds(i, 1), :]
-        return faces[1][2 * g, pl.ds(i, 1), :]
-
-    lax.fori_loop(0, CX, plane, 0)
+    lax.fori_loop(0, CX, plane, 0, unroll=2)
     if mode != "final":
         write_faces(out_ref, outs, mode == "late")
 
 
+def face_start():
+    return jnp.where(core() == 0, CX - 2, 0)
+
+
 def write_faces(w_ref, outs, late):
-    y_low, y_high, x_low, x_high, bx_low, bx_high, by_low, by_high = outs
+    y_low, y_high, x_a, x_b = outs
+    start = face_start()
     fields = [f for f in range(8) if not (late and f == 2)]
     for g, f in enumerate(fields):
         for r in range(2):
             y_low[2 * g + r] = w_ref[f, :, r, :]
             y_high[2 * g + r] = w_ref[f, :, CY - 2 + r, :]
-            x_low[2 * g + r] = w_ref[f, r]
-            x_high[2 * g + r] = w_ref[f, CX - 2 + r]
-    bx_low[...] = w_ref[4, :, 0, :]
-    bx_high[...] = w_ref[4, :, CY - 1, :]
-    by_low[...] = w_ref[5, 0]
-    by_high[...] = w_ref[5, CX - 1]
-
-
-def face_shapes(fields):
-    return [shape(2 * fields, CX, CZ)] * 4 + [shape(CX, CZ)] * 4
-
-
-def pack_kernel(rho, u, b, p, flags, w_ref, lim_ref, *outs):
-    w_ref[0] = rho[...]
-    w_ref[1:4] = u[...]
-    w_ref[4:7] = b[...]
-    w_ref[7] = p[...]
-    lim_ref[...] = flags[...].astype(F32)
-    faces, lims = outs[:8], outs[8:]
-    write_faces(w_ref, faces, False)
-    lims[0][...] = lim_ref[:, 0, :]
-    lims[1][...] = lim_ref[:, CY - 1, :]
-    lims[2][...] = lim_ref[0]
-    lims[3][...] = lim_ref[CX - 1]
+            x_a[2 * g + r] = w_ref[f, start + r]
+            x_b[2 * g + r] = w_ref[f, CX - 2 - start + r]
+
+
+def pack_kernel(rho, u, b, p, flags, w_ref, lim_ref, y_low, y_high, x_a, x_b, raw, sems):
+    copies = [
+        pltpu.make_async_copy(rho, w_ref.at[0], sems.at[0]),
+        pltpu.make_async_copy(u, w_ref.at[1:4], sems.at[1]),
+        pltpu.make_async_copy(b, w_ref.at[4:7], sems.at[2]),
+        pltpu.make_async_copy(p, w_ref.at[7], sems.at[3]),
+        pltpu.make_async_copy(flags, raw, sems.at[4]),
+    ]
+    for copy in copies:
+        copy.start()
+    for copy in copies:
+        copy.wait()
+    lim_ref[...] = raw[...].astype(F32)
+    write_faces(w_ref, (y_low, y_high, x_a, x_b), False)
+    start = jnp.where(core() == 0, CX - 1, 0)
+    y_low[16] = lim_ref[:, 0, :]
+    y_high[16] = lim_ref[:, CY - 1, :]
+    x_a[16] = lim_ref[start]
+    x_b[16] = lim_ref[CX - 1 - start]
 
 
 def substep(mode, split, args):
     scratch = [
         pltpu.VMEM((8, CX + 4, CY, CZ), F32),
         pltpu.VMEM((CX + 2, CY, CZ), F32),
+        pltpu.VMEM((8, CY + 4, CX, CZ), F32),
+        pltpu.VMEM((CY + 2, CX, CZ), F32),
+        pltpu.VMEM((8, CX, CY, CZ), F32),
         pltpu.VMEM((8, CY, CZ), F32),
         pltpu.VMEM((8, CY, CZ), F32),
-        pltpu.VMEM((8, CX, CZ), F32),
-        pltpu.VMEM((8, CX, CZ), F32),
     ]
     outs = [shape(8, CX, CY, CZ)]
     if mode == "all":
-        outs += face_shapes(8)
+        outs += [shape(16, CX, CZ)] * 4
     elif mode == "late":
-        outs += face_shapes(7)
+        outs += [shape(14, CX, CZ)] * 4
 
     def body(*refs):
         substep_kernel(mode, split, refs)
@@ -313,21 +300,21 @@
     return rows == positions.astype(jnp.int32)
 
 
-def spread(rows, out_ref):
+def spread(rows, out_ref, first):
     for t in range(SLOTS // CZ):
         tile = rows[:, t * CZ : (t + 1) * CZ]
         for j in range(CZ // CAP):
             moved = tile if j == 0 else pltpu.roll(tile, CZ - CAP * j, 1)
-            out_ref[t * (CZ // CAP) + j] = moved[0:4]
-
-
-def collect(block_ref, rows_ref):
+            out_ref[t * (CZ // CAP) + j, first : first + 4, :] = moved[0:4]
+
+
+def collect(block_ref, rows_ref, first):
     lane = lax.broadcasted_iota(jnp.int32, (8, CZ), 1) // CAP
     per = CZ // CAP
     for t in range(SLOTS // CZ):
         total = jnp.zeros((8, CZ), F32)
         for j in range(per):
-            block = block_ref[t * per + j]
+            block = block_ref[t * per + j, first : first + 4, :]
             block = jnp.concatenate([block, block], axis=0)
             moved = block if j == 0 else pltpu.roll(block, CAP * j, 1)
             total = jnp.where(lane == j, moved, total)
@@ -351,11 +338,16 @@
     out_ref[2:3, :] = found[2:3] * CZ + found[3:4]
 
 
-def payload_kernel(w_ref, bx_low, bx_high, by_low, by_high, slot_ref, out_ref, fields, rows):
+def payload_kernel(fx, fy, w_ref, y_low, y_high, x_a, x_b, slot_ref, out_ref, fields, rows):
     iota = lax.broadcasted_iota(jnp.int32, (CY, CZ), 0)
+    even = core() == 0
+    by_low = jnp.where(even, x_b[2 * fy + 1], x_a[2 * fy + 1])
+    by_high = jnp.where(even, x_a[2 * fy], x_b[2 * fy])
+    bx_low = y_low[2 * fx + 1]
+    bx_high = y_high[2 * fx]
     for x in range(CX):
-        east = by_high[...] if x == CX - 1 else w_ref[5, x + 1]
-        west = by_low[...] if x == 0 else w_ref[5, x - 1]
+        east = by_high if x == CX - 1 else w_ref[5, x + 1]
+        west = by_low if x == 0 else w_ref[5, x - 1]
         bx = w_ref[4, x]
         north = jnp.where(iota == CY - 1, bx_high[x : x + 1, :], pltpu.roll(bx, CY - 1, 0))
         south = jnp.where(iota == 0, bx_low[x : x + 1, :], pltpu.roll(bx, 1, 0))
@@ -372,10 +364,10 @@
     for v in range(2):
         kept = jnp.where(levels, found[v * CZ : (v + 1) * CZ], 0.0)
         rows[v : v + 1, :] = jnp.sum(kept, axis=0, keepdims=True)
-    spread(rows[...], out_ref)
-
-
-def deposit(rows, column, out_ref, stack):
+    spread(rows[...], out_ref, 0)
+
+
+def deposit(rows, column, stack):
     upper = column >= float(LATS)
     place = one_hot(jnp.where(upper, column - LATS, column), LATS).astype(F32).astype(BF16)
     for v in range(2):
@@ -388,22 +380,31 @@
     total = lax.dot_general(
         stack[...].astype(BF16), place, (((1,), (1,)), ((), ())), preferred_element_type=F32
     )
-    out_ref[...] = total[0:4] + total[4:8] + total[8:12]
-
-
-def deposit_first_kernel(block_ref, out_ref, column_ref, rows, stack):
-    collect(block_ref, rows)
+    return total[0:4] + total[4:8] + total[8:12]
+
+
+def folded(value, out_ref, layer):
+    for t in range(LATS // CZ):
+        out_ref[layer, 4 * t : 4 * t + 4, :] = value[:, t * CZ : (t + 1) * CZ]
+
+
+def unfolded(ref, layer):
+    return [ref[layer, 4 * t : 4 * t + 4, :] for t in range(LATS // CZ)]
+
+
+def deposit_first_kernel(block_ref, low_in, high_in, low_out, high_out, sums, column_ref, rows, stack):
+    collect(block_ref, rows, 0)
     column_ref[...] = rows[...]
-    deposit(rows[...], rows[2:3, :], out_ref, stack)
-
-
-def deposit_next_kernel(block_ref, column_ref, out_ref, rows, stack):
-    collect(block_ref, rows)
-    deposit(rows[...], column_ref[2:3, :], out_ref, stack)
-
-
-def scatter(block_ref, slot_ref, rows, parts):
-    collect(block_ref, rows)
+    value = deposit(rows[...], rows[2:3, :], stack)
+    count = low_in.shape[0]
+    low_out[0:count] = low_in[...]
+    high_out[0:count] = high_in[...]
+    for out_ref, layer in ((low_out, count), (high_out, count), (sums, 0)):
+        folded(value, out_ref, layer)
+
+
+def scatter(block_ref, first, slot_ref, rows, parts):
+    collect(block_ref, rows, first)
     weight = DRAG_RATE * rows[1:2, :]
     cells = one_hot(slot_ref[0:1, :], CX * CY).astype(F32).astype(BF16)
     levels = one_hot(slot_ref[1:2, :], CZ)
@@ -419,20 +420,31 @@
     return first.reshape(CX, CY, CZ), second.reshape(CX, CY, CZ)
 
 
-def drag_kernel(block_ref, slot_ref, w_ref, out_ref, y_low, y_high, x_low, x_high, rows, parts):
-    first, second = scatter(block_ref, slot_ref, rows, parts)
+def drag_kernel(
+    block_ref, slot_ref, column_ref, w_ref, out_ref, y_low, y_high, x_a, x_b, sums, rows, parts, stack
+):
+    collect(block_ref, rows, 0)
+    value = deposit(rows[...], column_ref[2:3, :], stack)
+    for out_ref_, layer in ((y_low, 2), (y_high, 2), (sums, 0)):
+        folded(value, out_ref_, layer)
+    first, second = scatter(block_ref, 4, slot_ref, rows, parts)
     out_ref[...] = w_ref[2] * (1.0 - second) + first
+    start = face_start()
     for r in range(2):
         y_low[r] = out_ref[:, r, :]
         y_high[r] = out_ref[:, CY - 2 + r, :]
-        x_low[r] = out_ref[r]
-        x_high[r] = out_ref[CX - 2 + r]
-
-
-def scatter_kernel(block_ref, slot_ref, out_ref, rows, parts):
-    first, second = scatter(block_ref, slot_ref, rows, parts)
-    out_ref[0] = first
-    out_ref[1] = second
+        x_a[r] = out_ref[start + r]
+        x_b[r] = out_ref[CX - 2 - start + r]
+
+
+def last_drag_kernel(block_ref, slot_ref, u_ref, out_ref, rows, parts):
+    first, second = scatter(block_ref, 0, slot_ref, rows, parts)
+    out_ref[...] = u_ref[...]
+    rho = u_ref[0]
+    my = u_ref[2]
+    added = rho * first - my * second
+    out_ref[2] = my + added
+    out_ref[7] = u_ref[7] + (my * added + 0.5 * added * added) / rho
 
 
 def base_kernel(inverse_ref, pedersen_ref, warming_ref, thermal_ref, out_ref, factors):
@@ -463,16 +475,52 @@
     out_ref[6:8, :] = jnp.zeros((2, LATS), F32)
 
 
-def gather_kernel(at, a, b, c, d, potential, base, out_ref):
-    out_ref[0:4, :] = (a[...] + b[...]) + (c[...] + d[...])
-    out_ref[4:6, :] = potential[...]
-    out_ref[6:8, :] = base[at : at + 2, :]
-
-
-def sweep_kernel(m2, m1, here, p1, p2, base, column_ref, out_v, out_block, out_base, ext, table):
+def gather_kernel(
+    at, own, low, high, far, potential, base, a_in, b_in, a_out, b_out, here_ref
+):
+    count = a_in.shape[0]
+    a_out[0:count] = a_in[...]
+    b_out[0:count] = b_in[...]
+    parts = [
+        unfolded(own, 0),
+        unfolded(low, low.shape[0] - 1),
+        unfolded(high, high.shape[0] - 1),
+        unfolded(far, 0),
+    ]
+    for t in range(LATS // CZ):
+        lanes = slice(t * CZ, (t + 1) * CZ)
+        total = (parts[0][t] + parts[1][t]) + (parts[2][t] + parts[3][t])
+        row = (t % 2) * 8
+        for out_ref, layer in ((a_out, count), (b_out, count), (here_ref, 0)):
+            out_ref[layer + t // 2, row : row + 4, :] = total
+            out_ref[layer + t // 2, row + 4 : row + 6, :] = potential[:, lanes]
+            out_ref[layer + t // 2, row + 6 : row + 8, :] = base[at : at + 2, lanes]
+
+
+def flat(ref, first):
+    pieces = [ref[first + t // 2, (t % 2) * 8 : (t % 2) * 8 + 8, :] for t in range(LATS // CZ)]
+    return jnp.concatenate(pieces, axis=1)
+
+
+def sweep_kernel(m2, x_a, here_ref, x_b, p2, base, column_ref, *refs):
+    payload = refs[0] if len(refs) == 7 else None
+    out_v, out_block, out_base, out_here, ext, table = refs[-6:]
+    even = core() == 0
+    mate = flat(x_a, x_a.shape[0] - 2)
+    other = flat(x_b, x_b.shape[0] - 2)
+    own = flat(here_ref, 0)
+    out_here[...] = own
+    around = (
+        flat(m2, 0),
+        jnp.where(even, other, mate),
+        own,
+        jnp.where(even, mate, other),
+        flat(p2, 0),
+    )
+    for at, value in enumerate(around):
+        for k in range(4):
+            ext[k, 2 * at : 2 * at + 2, :] = value[2 * k : 2 * k + 2, :]
     for k in range(4):
-        for at, ref in enumerate((m2, m1, here, p1, p2)):
-            ext[k, 2 * at : 2 * at + 2, :] = ref[2 * k : 2 * k + 2, :]
         ext[k, 10:16, :] = jnp.ones((6, LATS), F32)
     source = ext[0]
     heat = ext[1]
@@ -505,7 +553,7 @@
     ext[3] = conductance
     out_v[...] = ext[2, 4:6, :]
     out_base[...] = base[...]
-    out_base[2:4, :] = base[2:4, :] + base[5:6, :] * here[2:4, :]
+    out_base[2:4, :] = base[2:4, :] + base[5:6, :] * own[2:4, :]
     for v in range(2):
         for k, part in enumerate(rounded_parts(ext[2 + v, 4:6, :], 3)):
             table[4 * k + 2 * v : 4 * k + 2 * v + 2, :] = part
@@ -518,7 +566,10 @@
     voltage = jnp.where(upper, found[1:2], found[0:1])
     weight = jnp.where(upper, found[3:4], found[2:3])
     sub = lax.broadcasted_iota(jnp.int32, (8, SLOTS), 0)
-    spread(jnp.where(sub == 0, voltage, weight), out_block)
+    spread(jnp.where(sub % 4 == 0, voltage, weight), out_block, 4 if payload is not None else 0)
+    if payload is not None:
+        for owner in range(BLOCKS):
+            out_block[owner, 0:4, :] = payload[owner]
 
 
 def thermal_kernel(thermal_ref, inverse_ref, warming_ref, one_ref, two_ref, out_ref):
@@ -538,13 +589,19 @@
     return lax.ppermute(value, axis, [(i, (i + by) % count) for i in range(count)])
 
 
+def swapped(value, first):
+    count = lax.axis_size("blk")
+    pairs = [(i, (i + 1) % count) for i in range(first, count, 2)]
+    return lax.ppermute(value, "blk", pairs + [(j, i) for i, j in pairs])
+
+
 def halos(faces):
-    y_low, y_high, x_low, x_high = faces
+    y_low, y_high, x_a, x_b = faces
     return (
         shifted(y_high, "grp", 1),
         shifted(y_low, "grp", -1),
-        shifted(x_high, "blk", 1),
-        shifted(x_low, "blk", -1),
+        swapped(x_a, 0),
+        swapped(x_b, 1),
     )
 
 
@@ -583,16 +640,14 @@
     ).astype(F32)
     quarter = LATS // 4
 
-    packed = kernel_call(
+    fluid, limiter, *faces = pl.pallas_call(
         pack_kernel,
-        [shape(8, CX, CY, CZ), shape(CX, CY, CZ)] + face_shapes(8) + [shape(CX, CZ)] * 4,
-        1.0,
+        out_shape=[shape(8, CX, CY, CZ), shape(CX, CY, CZ)] + [shape(17, CX, CZ)] * 4,
+        in_specs=[pl.BlockSpec(memory_space=pltpu.HBM)] * 5,
+        scratch_shapes=[pltpu.VMEM((CX, CY, CZ), jnp.int32), pltpu.SemaphoreType.DMA((5,))],
+        compiler_params=pltpu.CompilerParams(vmem_limit_bytes=60 * 1024 * 1024),
     )(mass_per_volume, flow_vector, magnetic_vector, thermal_push, gradient_clipping_flags)
-    fluid, limiter = packed[:2]
-    faces, field_faces, limit_faces = packed[2:6], packed[6:10], packed[10:14]
-    field_halos = halos(field_faces)
-    all_halos = halos(faces)
-    limit_halos = halos(limit_faces)
+    first_halos = halos(faces)
 
     slots = kernel_call(slot_kernel, shape(8, SLOTS), 1.0)(tracer_holder_tile, line_rows)
     base = kernel_call(
@@ -608,9 +663,9 @@
     stack_scratch = pltpu.VMEM((16, SLOTS), F32)
     parts_scratch = pltpu.VMEM((4 * CZ, SLOTS), BF16)
 
-    def payload(w, near):
+    def payload(w, near, fx, fy):
         return kernel_call(
-            payload_kernel,
+            functools.partial(payload_kernel, fx, fy),
             shape(BLOCKS, 4, CZ),
             2.0,
             [pltpu.VMEM((CX * CY, 2 * CZ), F32), rows_scratch],
@@ -619,57 +674,69 @@
     def exchange(blocks):
         return lax.all_to_all(blocks, "blk", split_axis=0, concat_axis=0, tiled=True)
 
-    def ionosphere(at, sums, potential, base_now, column):
-        terms = [sums] + [shifted(sums, "grp", k) for k in range(1, 4)]
-        here = kernel_call(
-            functools.partial(gather_kernel, at), shape(8, LATS), 0.3
-        )(*terms, potential, base_now)
-        around = [shifted(here, "blk", k) for k in (2, 1)]
-        around += [here]
-        around += [shifted(here, "blk", k) for k in (-1, -2)]
-        voltage, reply, base_next = kernel_call(
+    def gathered(at, sums, near, far, potential, base_now, x_a, x_b):
+        count = x_a.shape[0] + 2
+        return kernel_call(
+            functools.partial(gather_kernel, at),
+            [shape(count, CX, CZ)] * 2 + [shape(2, CX, CZ)],
+            0.5,
+        )(sums, near[0], near[1], far, potential, base_now, x_a, x_b)
+
+    def swept(m2, x_a, here, x_b, p2, base_now, column, *payload):
+        rows = 8 if payload else 4
+        return kernel_call(
             sweep_kernel,
-            [shape(2, LATS), shape(BLOCKS, 4, CZ), shape(8, LATS)],
+            [shape(2, LATS), shape(BLOCKS, rows, CZ), shape(8, LATS), shape(8, LATS)],
             2.0,
             [pltpu.VMEM((4, 16, LATS), F32), pltpu.VMEM((16, LATS), F32)],
-        )(*around, base_now, column)
-        return here, voltage, exchange(reply), base_next
-
-    arrived = exchange(payload(fluid, field_halos))
-    middle = substep("all", False, (fluid, limiter, *all_halos, *limit_halos))
-    sums, column = kernel_call(
+        )(m2, x_a, here, x_b, p2, base_now, column, *payload)
+
+    arrived = exchange(payload(fluid, first_halos, 4, 5))
+    fluid, y_low, y_high, x_a, x_b = substep(
+        "all", False, (fluid, limiter, *first_halos, *first_halos)
+    )
+    y_low, y_high, sums, column = kernel_call(
         deposit_first_kernel,
-        [shape(4, LATS), shape(8, SLOTS)],
+        [shape(17, CX, CZ)] * 2 + [shape(1, CX, CZ), shape(8, SLOTS)],
         1.5,
         [rows_scratch, stack_scratch],
-    )(arrived)
-    here_one, voltage, returned, base_next = ionosphere(
-        0, sums, electric_voltage, base, column
-    )
-    ended = substep("late", False, (middle[0], limiter, *halos(middle[1:5]), *limit_halos))
-    fluid = ended[0]
-    late_halos = halos(ended[1:5])
-    arrived = exchange(payload(fluid, halos(ended[5:9])))
-    dragged = kernel_call(
+    )(arrived, y_low, y_high)
+    near = halos((y_low, y_high, x_a, x_b))
+    far = shifted(sums, "grp", 2)
+    fluid, y_low, y_high, x_a, x_b = substep(
+        "late", False, (fluid, limiter, *near, *first_halos)
+    )
+    x_a, x_b, here = gathered(0, sums, near, far, electric_voltage, base, x_a, x_b)
+    late_halos = halos((y_low, y_high, x_a, x_b))
+    m2, p2 = shifted(here, "blk", 2), shifted(here, "blk", -2)
+    lines = payload(fluid, late_halos, 3, 4)
+    voltage, blocks, base_next, here_one = swept(
+        m2, late_halos[2], here, late_halos[3], p2, base, column, lines
+    )
+    arrived = exchange(blocks)
+    speed, *faces, sums = kernel_call(
         drag_kernel,
-        [shape(CX, CY, CZ)] + [shape(2, CX, CZ)] * 4,
+        [shape(CX, CY, CZ)]
+        + [shape(3, CX, CZ)] * 2
+        + [shape(2, CX, CZ)] * 2
+        + [shape(1, CX, CZ)],
         2.0,
-        [rows_scratch, parts_scratch],
-    )(returned, slots, fluid)
-    speed, speed_halos = dragged[0], halos(dragged[1:5])
-    sums = kernel_call(
-        deposit_next_kernel, shape(4, LATS), 1.5, [rows_scratch, stack_scratch]
-    )(arrived, column)
-    here_two, voltage, returned, base_next = ionosphere(2, sums, voltage, base_next, column)
-    middle = substep(
-        "all", True, (fluid, limiter, *late_halos, *limit_halos, speed, *speed_halos)
-    )
-    push = kernel_call(
-        scatter_kernel, shape(2, CX, CY, CZ), 2.0, [rows_scratch, parts_scratch]
-    )(returned, slots)
-    (conserved_quantities,) = substep(
-        "final", False, (middle[0], limiter, *halos(middle[1:5]), *limit_halos, push)
-    )
+        [rows_scratch, parts_scratch, stack_scratch],
+    )(arrived, slots, column, fluid)
+    speed_halos = halos(faces)
+    far = shifted(sums, "grp", 2)
+    fluid, y_low, y_high, x_a, x_b = substep(
+        "all", True, (fluid, limiter, *late_halos, *first_halos, speed, *speed_halos)
+    )
+    x_a, x_b, here = gathered(2, sums, speed_halos, far, voltage, base_next, x_a, x_b)
+    near = halos((y_low, y_high, x_a, x_b))
+    m2, p2 = shifted(here, "blk", 2), shifted(here, "blk", -2)
+    voltage, blocks, _, here_two = swept(m2, near[2], here, near[3], p2, base_next, column)
+    returned = exchange(blocks)
+    (state,) = substep("final", False, (fluid, limiter, *near, *first_halos))
+    conserved_quantities = kernel_call(
+        last_drag_kernel, shape(8, CX, CY, CZ), 1.5, [rows_scratch, parts_scratch]
+    )(returned, slots, state)
 
     start = group * quarter
     ending_thermal_state = kernel_call(

time: 186 us -> 131 us (0.70)
  starting transfers between devices: 82.8 us -> 54 us
  waiting for transfers between devices: 51.4 us -> 22.9 us
  local copies, waits for them, and re-layouts: 9.97 us -> 13 us
    ppermute x46 -> x16, starting transfers between devices: 64.5 us -> 19.4 us  [shifted(): lax.ppermute(value, axis, [(i, (i + by) % count) for i in range(count)])]
    ppermute x46 -> x16, waiting for transfers between devices: 44.1 us -> 11.6 us  [shifted(): lax.ppermute(value, axis, [(i, (i + by) % count) for i in range(count)])]
    ppermute x0 -> x10, starting transfers between devices: none -> 19.9 us  [swapped(): return lax.ppermute(value, 'blk', pairs + [(j, i) for i, j in pairs])]
    all_to_all x4 -> x3, starting transfers between devices: 18.3 us -> 14.8 us  [exchange(): lax.all_to_all(blocks, 'blk', split_axis=0, concat_axis=0, tiled=True)]
    pallas_call x4, Pallas kernels: 28.6 us -> 25.4 us  [substep(): return kernel_call(body, outs, 5.0, scratch)(*args)]
    ppermute x0 -> x10, waiting for transfers between devices: none -> 2.89 us  [swapped(): return lax.ppermute(value, 'blk', pairs + [(j, i) for i, j in pairs])]
    pallas_call x11 -> x10, Pallas kernels: 8.09 us -> 10.6 us  [the longest x2 2.73 us: swept(): kernel_call(sweep_kernel, [shape(2, LATS), shape(BLOCKS, rows, CZ), shape...]
    unnamed x38 -> x50, local copies, waits for them, and re-layouts: 9.12 us -> 11.4 us
  transfers between devices with their start and end apart: 50 -> 29, of which waited for: 16 -> 10; matrix products, arithmetic and copies ran while one was open for 1% -> 1% of each run, Pallas kernels for 17% -> 23%
where the time goes in v2:
time: 131 us; the launch traced here: 130 us
  starting transfers between devices  54 us (41%)
  Pallas kernels  38.7 us (30%)
  waiting for transfers between devices  22.9 us (17%)
  local copies, waits for them, and re-layouts  13 us (10%)
    pallas_call x4, Pallas kernels, substep(): return kernel_call(body, outs, 5.0, scratch)(*args)  25.4 us
    ppermute x10, starting transfers between devices, swapped(): return lax.ppermute(value, 'blk', pairs + [(j, i) for i, j in pairs])  19.9 us
    ppermute x16, starting transfers between devices, shifted(): lax.ppermute(value, axis, [(i, (i + by) % count) for i in range(count)])  19.4 us
    all_to_all x3, starting transfers between devices, exchange(): lax.all_to_all(blocks, 'blk', split_axis=0, concat_axis=0, tiled=True)  14.8 us
    ppermute x16, waiting for transfers between devices, shifted(): lax.ppermute(value, axis, [(i, (i + by) % count) for i in range(count)])  11.6 us
    unnamed x50, local copies, waits for them, and re-layouts  11.4 us
    all_to_all x3, waiting for transfers between devices, exchange(): lax.all_to_all(blocks, 'blk', split_axis=0, concat_axis=0, tiled=True)  8.4 us
    ppermute x10, waiting for transfers between devices, swapped(): return lax.ppermute(value, 'blk', pairs + [(j, i) for i, j in pairs])  2.89 us
  transfers between devices with their start and end apart: 29, of which 10 were waited for; matrix products, arithmetic and copies ran while one was open for 1% of the time, Pallas kernels for 23%

profile of v2, /device:TPU:0, one launch (start us, length us, event | category | flops | bytes accessed | tf_op | source)
XLA Modules:
  0.0 129.7 jit_solution(14740107304504525044)
XLA Ops:
  0.6 2.5 %shard_map.148 = (f32[8,16,16,128]{3,2,1,0:T(8,128)}, f32[16,16,128]{2,1,0:T(8,128)}, f32[17,16,128]{2,1,0:T(8,128)}, f32[17,16,128]{2,1,0:T(8,128)}, f32[17,16,128]{2,1,0:T(8,128)}, /*index=5*/f32[17,16,128]{2,1,0:T(8,128)}) custom-call(f32[16,16,128]{2,1,0:T(8,128)} %rho.1, f32[3,16,16,128]{3,2,1,0:T(8,128)} %u.1, f32[3,16,16,128]{3,2,1,0:T(8,128)} %b.1, ...), custom_call_target="tpu_custom_call" | custom-call | tf_op jit(solution)/shard_map/pallas_call | solution.py:643
  3.1 1.7 %collective-permute-start = (f32[17,16,128]{2,1,0:T(8,128)}, f32[17,16,128]{2,1,0:T(8,128)S(1)}, u32[]{:S(2)}, u32[]{:S(2)}) collective-permute-start(f32[17,16,128]{2,1,0:T(8,128)} %get-tuple-element.48), channel_id=1, source_target_pairs={{0,32},{32,64},{64,96},{96,0},{1,33},{33,65},{65,97},{97,1},{2,34}... | collective-permute-start | bytes 417800 | tf_op jit(solution)/shard_map/ppermute | solution.py:589
  6.4 6.4 %collective-permute-start.3 = (f32[17,16,128]{2,1,0:T(8,128)}, f32[17,16,128]{2,1,0:T(8,128)S(1)}, u32[]{:S(2)}, u32[]{:S(2)}) collective-permute-start(f32[17,16,128]{2,1,0:T(8,128)} %get-tuple-element.51), channel_id=1, source_target_pairs={{1,2},{3,4},{5,6},{7,8},{9,10},{11,12},{13,14},{15,16},{17,18},{19... | collective-permute-start | bytes 417800 | tf_op jit(solution)/shard_map/ppermute | solution.py:595
  18.5 6.9 %all-to-all-start = ((f32[32,4,128]{2,1,0:T(4,128)}), f32[32,4,128]{2,1,0:T(4,128)S(1)}, u32[]{:S(2)}, u32[]{:S(2)}) async-start(f32[32,4,128]{2,1,0:T(4,128)} %shard_map.150), calls=%async_computation | async-start | bytes 131072 | tf_op jit(solution)/shard_map/all_to_all | solution.py:675
  25.4 7.0 %shard_map.151 = (f32[8,16,16,128]{3,2,1,0:T(8,128)S(1)}, f32[16,16,128]{2,1,0:T(8,128)S(1)}, f32[16,16,128]{2,1,0:T(8,128)S(1)}, f32[16,16,128]{2,1,0:T(8,128)}, f32[16,16,128]{2,1,0:T(8,128)}) custom-call(f32[8,16,16,128]{3,2,1,0:T(8,128)S(1)} %copy-done.1, f32[16,16,128]{2,1,0:T(8,128)S(1)} %copy-done.2, ...), custom_call_target="tpu_custom_call" | custom-call | bytes 16500000 | tf_op jit(solution)/shard_map/pallas_call | solution.py:286
  33.8 2.9 %collective-permute-start.5 = (f32[17,16,128]{2,1,0:T(8,128)S(1)}, f32[17,16,128]{2,1,0:T(8,128)S(1)}, u32[]{:S(2)}, u32[]{:S(2)}) collective-permute-start(f32[17,16,128]{2,1,0:T(8,128)S(1)} %get-tuple-element.57), channel_id=1, source_target_pairs={{0,96},{32,0},{64,32},{96,64},{1,97},{33,1},{65,33},{97,65},{2,98}... | collective-permute-start | bytes 417800 | tf_op jit(solution)/shard_map/ppermute | solution.py:589
  36.7 4.8 %collective-permute-start.8 = (f32[16,16,128]{2,1,0:T(8,128)}, f32[16,16,128]{2,1,0:T(8,128)S(1)}, u32[]{:S(2)}, u32[]{:S(2)}) collective-permute-start(f32[16,16,128]{2,1,0:T(8,128)} %get-tuple-element.60), channel_id=1, source_target_pairs={{1,2},{3,4},{5,6},{7,8},{9,10},{11,12},{13,14},{15,16},{17,18},{19... | collective-permute-start | bytes 393224 | tf_op jit(solution)/shard_map/ppermute | solution.py:595
  47.1 6.2 %shard_map.154 = (f32[8,16,16,128]{3,2,1,0:T(8,128)S(1)}, f32[14,16,128]{2,1,0:T(8,128)S(1)}, f32[14,16,128]{2,1,0:T(8,128)S(1)}, f32[14,16,128]{2,1,0:T(8,128)S(1)}, f32[14,16,128]{2,1,0:T(8,128)S(1)}) custom-call(f32[8,16,16,128]{3,2,1,0:T(8,128)S(1)} %get-tuple-element.58.refs_0_, f32[16,16,128]{2,1,0:T(8,128)S(1)} %copy-done.2, ...), custom_call_target="tpu_custom_call" | custom-call | bytes 16500000 | tf_op jit(solution)/shard_map/pallas_call | solution.py:286
  53.5 4.8 %collective-permute-start.11 = (f32[16,16,128]{2,1,0:T(8,128)S(1)}, f32[16,16,128]{2,1,0:T(8,128)S(1)}, u32[]{:S(2)}, u32[]{:S(2)}) collective-permute-start(f32[16,16,128]{2,1,0:T(8,128)S(1)} %get-tuple-element.65), channel_id=1, source_target_pairs={{1,2},{3,4},{5,6},{7,8},{9,10},{11,12},{13,14},{15,16},{17,18},{19... | collective-permute-start | bytes 393224 | tf_op jit(solution)/shard_map/ppermute | solution.py:595
  58.3 3.2 %collective-permute-start.14 = (f32[14,16,128]{2,1,0:T(8,128)S(1)}, f32[14,16,128]{2,1,0:T(8,128)S(1)}, u32[]{:S(2)}, u32[]{:S(2)}) collective-permute-start(f32[14,16,128]{2,1,0:T(8,128)S(1)} %get-tuple-element.69), channel_id=1, source_target_pairs={{0,96},{32,0},{64,32},{96,64},{1,97},{33,1},{65,33},{97,65},{2,98}... | collective-permute-start | bytes 344072 | tf_op jit(solution)/shard_map/ppermute | solution.py:589
  61.9 2.4 %collective-permute-done.13.y_low.refs_2_ = f32[14,16,128]{2,1,0:T(8,128)S(1)} collective-permute-done((f32[14,16,128]{2,1,0:T(8,128)S(1)}, f32[14,16,128]{2,1,0:T(8,128)S(1)}, u32[]{:S(2)}, u32[]{:S(2)}) %collective-permute-start.13) | collective-permute-done | bytes 114720 | tf_op jit(solution)/shard_map/ppermute | solution.py:589
  65.3 6.1 %collective-permute-done.9.m2 = f32[2,16,128]{2,1,0:T(8,128)S(1)} collective-permute-done((f32[2,16,128]{2,1,0:T(8,128)S(1)}, f32[2,16,128]{2,1,0:T(8,128)S(1)}, u32[]{:S(2)}, u32[]{:S(2)}) %collective-permute-start.9) | collective-permute-done | bytes 16416 | tf_op jit(solution)/shard_map/ppermute | solution.py:589
  72.8 3.9 %all-to-all-start.1 = ((f32[32,8,128]{2,1,0:T(8,128)}), f32[32,8,128]{2,1,0:T(8,128)S(1)}, u32[]{:S(2)}, u32[]{:S(2)}) async-start(f32[32,8,128]{2,1,0:T(8,128)} %get-tuple-element.70), calls=%async_computation.1 | async-start | bytes 262144 | tf_op jit(solution)/shard_map/all_to_all | solution.py:675
  76.6 7.9 %all-to-all-done.1.block_ref = f32[32,8,128]{2,1,0:T(8,128)S(1)} async-done(((f32[32,8,128]{2,1,0:T(8,128)}), f32[32,8,128]{2,1,0:T(8,128)S(1)}, u32[]{:S(2)}, u32[]{:S(2)}) %all-to-all-start.1) | async-done | bytes 131104 | tf_op jit(solution)/shard_map/all_to_all | solution.py:675
  86.1 1.8 %collective-permute-start.19 = (f32[2,16,128]{2,1,0:T(8,128)S(1)}, f32[2,16,128]{2,1,0:T(8,128)S(1)}, u32[]{:S(2)}, u32[]{:S(2)}) collective-permute-start(f32[2,16,128]{2,1,0:T(8,128)S(1)} %get-tuple-element.78), channel_id=1, source_target_pairs={{1,2},{3,4},{5,6},{7,8},{9,10},{11,12},{13,14},{15,16},{17,18},{19... | collective-permute-start | bytes 49160 | tf_op jit(solution)/shard_map/ppermute | solution.py:595
  88.4 2.8 %collective-permute-start.16 = (f32[3,16,128]{2,1,0:T(8,128)S(1)}, f32[3,16,128]{2,1,0:T(8,128)S(1)}, u32[]{:S(2)}, u32[]{:S(2)}) collective-permute-start(f32[3,16,128]{2,1,0:T(8,128)S(1)} %get-tuple-element.73), channel_id=1, source_target_pairs={{0,96},{32,0},{64,32},{96,64},{1,97},{33,1},{65,33},{97,65},{2,98}... | collective-permute-start | bytes 73736 | tf_op jit(solution)/shard_map/ppermute | solution.py:589
  94.1 6.2 %shard_map.159 = (f32[8,16,16,128]{3,2,1,0:T(8,128)S(1)}, f32[16,16,128]{2,1,0:T(8,128)S(1)}, f32[16,16,128]{2,1,0:T(8,128)S(1)}, f32[16,16,128]{2,1,0:T(8,128)S(1)}, f32[16,16,128]{2,1,0:T(8,128)S(1)}) custom-call(f32[8,16,16,128]{3,2,1,0:T(8,128)S(1)} %get-tuple-element.67.w_ref.refs_0_, f32[16,16,128]{2,1,0:T(8,128)S(1)} %copy-done.2, ...), custom_call_target="tpu_custom_call" | custom-call | bytes 16500000 | tf_op jit(solution)/shard_map/pallas_call | solution.py:286
  101.4 1.9 %collective-permute-start.21 = (f32[18,16,128]{2,1,0:T(8,128)S(1)}, f32[18,16,128]{2,1,0:T(8,128)S(1)}, u32[]{:S(2)}, u32[]{:S(2)}) collective-permute-start(f32[18,16,128]{2,1,0:T(8,128)S(1)} %get-tuple-element.82), channel_id=1, source_target_pairs={{0,1},{2,3},{4,5},{6,7},{8,9},{10,11},{12,13},{14,15},{16,17},{18,... | collective-permute-start | bytes 442376 | tf_op jit(solution)/shard_map/ppermute | solution.py:595
  104.1 1.7 %collective-permute-start.20 = (f32[2,16,128]{2,1,0:T(8,128)S(1)}, f32[2,16,128]{2,1,0:T(8,128)S(1)}, u32[]{:S(2)}, u32[]{:S(2)}) collective-permute-start(f32[2,16,128]{2,1,0:T(8,128)S(1)} %get-tuple-element.81.here_ref), channel_id=1, source_target_pairs={{0,2},{1,3},{2,4},{3,5},{4,6},{5,7},{6,8},{7,9},{8,10},{9,11},{10,... | collective-permute-start | bytes 49160 | tf_op jit(solution)/shard_map/ppermute | solution.py:589
  105.8 1.7 %collective-permute-start.24 = (f32[16,16,128]{2,1,0:T(8,128)}, f32[16,16,128]{2,1,0:T(8,128)S(1)}, u32[]{:S(2)}, u32[]{:S(2)}) collective-permute-start(f32[16,16,128]{2,1,0:T(8,128)} %copy-done.18), channel_id=1, source_target_pairs={{0,32},{32,64},{64,96},{96,0},{1,33},{33,65},{65,97},{97,1},{2,34}... | collective-permute-start | bytes 393224 | tf_op jit(solution)/shard_map/ppermute | solution.py:589
  109.1 2.4 %collective-permute-done.20.m2 = f32[2,16,128]{2,1,0:T(8,128)S(1)} collective-permute-done((f32[2,16,128]{2,1,0:T(8,128)S(1)}, f32[2,16,128]{2,1,0:T(8,128)S(1)}, u32[]{:S(2)}, u32[]{:S(2)}) %collective-permute-start.20) | collective-permute-done | bytes 16416 | tf_op jit(solution)/shard_map/ppermute | solution.py:589
  112.8 4.1 %all-to-all-start.2 = ((f32[32,4,128]{2,1,0:T(4,128)}), f32[32,4,128]{2,1,0:T(4,128)S(1)}, u32[]{:S(2)}, u32[]{:S(2)}) async-start(f32[32,4,128]{2,1,0:T(4,128)} %get-tuple-element.84), calls=%async_computation.2 | async-start | bytes 131072 | tf_op jit(solution)/shard_map/all_to_all | solution.py:675
  121.5 6.0 %shard_map.162.u_ref = f32[8,16,16,128]{3,2,1,0:T(8,128)S(1)} custom-call(f32[8,16,16,128]{3,2,1,0:T(8,128)S(1)} %get-tuple-element.85.refs_0_, f32[16,16,128]{2,1,0:T(8,128)S(1)} %copy-done.2, f32[16,16,128]{2,1,0:T(8,128)S(1)} %copy-done.7, f32[16,16,128]{2,1,0:T(8,128)S(1)} %copy-done.9, f32[18,16,128]{2,1,0:T(8,128)S(1)} %collective-permute-done.21.x_a.refs_4_, ...), custom_call_target="tpu_custom_call" | custom-call | bytes 16500000 | tf_op jit(solution)/shard_map/pallas_call | solution.py:286
  128.1 1.6 %shard_map.163 = f32[8,16,16,128]{3,2,1,0:T(8,128)} custom-call(f32[32,4,128]{2,1,0:T(4,128)S(1)} %all-to-all-done.2.block_ref, f32[8,1024]{1,0:T(8,128)S(1)} %shard_map.149.slot_ref, f32[8,16,16,128]{3,2,1,0:T(8,128)S(1)} %shard_map.162.u_ref), custom_call_target="tpu_custom_call" | custom-call | bytes 4950000 | tf_op jit(solution)/shard_map/pallas_call | solution.py:737
  (115 shorter events, 32.0 us)
Async XLA Ops:
  3.1 11.3 %collective-permute-start = (f32[17,16,128]{2,1,0:T(8,128)}, f32[17,16,128]{2,1,0:T(8,128)S(1)}, u32[]{:S(2)}, u32[]{:S(2)}) collective-permute-start(f32[17,16,128]{2,1,0:T(8,128)} %get-tuple-element.48), channel_id=1, source_target_pairs={{0,32},{32,64},{64,96},{96,0},{1,33},{33,65},{65,97},{97,1},{2,34}... | collective-permute-start | bytes 417800 | tf_op jit(solution)/shard_map/ppermute | solution.py:589
  4.9 9.6 %collective-permute-start.1 = (f32[17,16,128]{2,1,0:T(8,128)}, f32[17,16,128]{2,1,0:T(8,128)S(1)}, u32[]{:S(2)}, u32[]{:S(2)}) collective-permute-start(f32[17,16,128]{2,1,0:T(8,128)} %get-tuple-element.49), channel_id=1, source_target_pairs={{0,96},{32,0},{64,32},{96,64},{1,97},{33,1},{65,33},{97,65},{2,98}... | collective-permute-start | bytes 417800 | tf_op jit(solution)/shard_map/ppermute | solution.py:589
  6.4 8.0 %collective-permute-start.2 = (f32[17,16,128]{2,1,0:T(8,128)}, f32[17,16,128]{2,1,0:T(8,128)S(1)}, u32[]{:S(2)}, u32[]{:S(2)}) collective-permute-start(f32[17,16,128]{2,1,0:T(8,128)} %get-tuple-element.50), channel_id=1, source_target_pairs={{0,1},{2,3},{4,5},{6,7},{8,9},{10,11},{12,13},{14,15},{16,17},{18,... | collective-permute-start | bytes 417800 | tf_op jit(solution)/shard_map/ppermute | solution.py:595
  6.4 9.4 %collective-permute-start.3 = (f32[17,16,128]{2,1,0:T(8,128)}, f32[17,16,128]{2,1,0:T(8,128)S(1)}, u32[]{:S(2)}, u32[]{:S(2)}) collective-permute-start(f32[17,16,128]{2,1,0:T(8,128)} %get-tuple-element.51), channel_id=1, source_target_pairs={{1,2},{3,4},{5,6},{7,8},{9,10},{11,12},{13,14},{15,16},{17,18},{19... | collective-permute-start | bytes 417800 | tf_op jit(solution)/shard_map/ppermute | solution.py:595
  18.5 14.4 %all-to-all-start = ((f32[32,4,128]{2,1,0:T(4,128)}), f32[32,4,128]{2,1,0:T(4,128)S(1)}, u32[]{:S(2)}, u32[]{:S(2)}) async-start(f32[32,4,128]{2,1,0:T(4,128)} %shard_map.150), calls=%async_computation | async-start | bytes 131072 | tf_op jit(solution)/shard_map/all_to_all | solution.py:675
  33.4 11.8 %collective-permute-start.4 = (f32[17,16,128]{2,1,0:T(8,128)S(1)}, f32[17,16,128]{2,1,0:T(8,128)S(1)}, u32[]{:S(2)}, u32[]{:S(2)}) collective-permute-start(f32[17,16,128]{2,1,0:T(8,128)S(1)} %get-tuple-element.56), channel_id=1, source_target_pairs={{0,32},{32,64},{64,96},{96,0},{1,33},{33,65},{65,97},{97,1},{2,34}... | collective-permute-start | bytes 417800 | tf_op jit(solution)/shard_map/ppermute | solution.py:589
  33.8 11.5 %collective-permute-start.5 = (f32[17,16,128]{2,1,0:T(8,128)S(1)}, f32[17,16,128]{2,1,0:T(8,128)S(1)}, u32[]{:S(2)}, u32[]{:S(2)}) collective-permute-start(f32[17,16,128]{2,1,0:T(8,128)S(1)} %get-tuple-element.57), channel_id=1, source_target_pairs={{0,96},{32,0},{64,32},{96,64},{1,97},{33,1},{65,33},{97,65},{2,98}... | collective-permute-start | bytes 417800 | tf_op jit(solution)/shard_map/ppermute | solution.py:589
  36.7 7.3 %collective-permute-start.7 = (f32[16,16,128]{2,1,0:T(8,128)}, f32[16,16,128]{2,1,0:T(8,128)S(1)}, u32[]{:S(2)}, u32[]{:S(2)}) collective-permute-start(f32[16,16,128]{2,1,0:T(8,128)} %get-tuple-element.59), channel_id=1, source_target_pairs={{0,1},{2,3},{4,5},{6,7},{8,9},{10,11},{12,13},{14,15},{16,17},{18,... | collective-permute-start | bytes 393224 | tf_op jit(solution)/shard_map/ppermute | solution.py:595
  36.7 7.9 %collective-permute-start.8 = (f32[16,16,128]{2,1,0:T(8,128)}, f32[16,16,128]{2,1,0:T(8,128)S(1)}, u32[]{:S(2)}, u32[]{:S(2)}) collective-permute-start(f32[16,16,128]{2,1,0:T(8,128)} %get-tuple-element.60), channel_id=1, source_target_pairs={{1,2},{3,4},{5,6},{7,8},{9,10},{11,12},{13,14},{15,16},{17,18},{19... | collective-permute-start | bytes 393224 | tf_op jit(solution)/shard_map/ppermute | solution.py:595
  41.5 11.9 %collective-permute-start.6 = (f32[1,16,128]{2,1,0:T(8,128)S(1)}, f32[1,16,128]{2,1,0:T(8,128)S(1)}, u32[]{:S(2)}, u32[]{:S(2)}) collective-permute-start(f32[1,16,128]{2,1,0:T(8,128)S(1)} %get-tuple-element.55.own), channel_id=1, source_target_pairs={{0,64},{32,96},{64,0},{96,32},{1,65},{33,97},{65,1},{97,33},{2,66}... | collective-permute-start | bytes 24584 | tf_op jit(solution)/shard_map/ppermute | solution.py:589
  53.4 10.9 %collective-permute-start.10 = (f32[16,16,128]{2,1,0:T(8,128)S(1)}, f32[16,16,128]{2,1,0:T(8,128)S(1)}, u32[]{:S(2)}, u32[]{:S(2)}) collective-permute-start(f32[16,16,128]{2,1,0:T(8,128)S(1)} %get-tuple-element.64), channel_id=1, source_target_pairs={{0,1},{2,3},{4,5},{6,7},{8,9},{10,11},{12,13},{14,15},{16,17},{18,... | collective-permute-start | bytes 393224 | tf_op jit(solution)/shard_map/ppermute | solution.py:595
  53.5 10.9 %collective-permute-start.11 = (f32[16,16,128]{2,1,0:T(8,128)S(1)}, f32[16,16,128]{2,1,0:T(8,128)S(1)}, u32[]{:S(2)}, u32[]{:S(2)}) collective-permute-start(f32[16,16,128]{2,1,0:T(8,128)S(1)} %get-tuple-element.65), channel_id=1, source_target_pairs={{1,2},{3,4},{5,6},{7,8},{9,10},{11,12},{13,14},{15,16},{17,18},{19... | collective-permute-start | bytes 393224 | tf_op jit(solution)/shard_map/ppermute | solution.py:595
  58.3 6.0 %collective-permute-start.14 = (f32[14,16,128]{2,1,0:T(8,128)S(1)}, f32[14,16,128]{2,1,0:T(8,128)S(1)}, u32[]{:S(2)}, u32[]{:S(2)}) collective-permute-start(f32[14,16,128]{2,1,0:T(8,128)S(1)} %get-tuple-element.69), channel_id=1, source_target_pairs={{0,96},{32,0},{64,32},{96,64},{1,97},{33,1},{65,33},{97,65},{2,98}... | collective-permute-start | bytes 344072 | tf_op jit(solution)/shard_map/ppermute | solution.py:589
  64.3 7.1 %collective-permute-start.9 = (f32[2,16,128]{2,1,0:T(8,128)S(1)}, f32[2,16,128]{2,1,0:T(8,128)S(1)}, u32[]{:S(2)}, u32[]{:S(2)}) collective-permute-start(f32[2,16,128]{2,1,0:T(8,128)S(1)} %get-tuple-element.63.here_ref), channel_id=1, source_target_pairs={{0,2},{1,3},{2,4},{3,5},{4,6},{5,7},{6,8},{7,9},{8,10},{9,11},{10,... | collective-permute-start | bytes 49160 | tf_op jit(solution)/shard_map/ppermute | solution.py:589
  72.8 11.7 %all-to-all-start.1 = ((f32[32,8,128]{2,1,0:T(8,128)}), f32[32,8,128]{2,1,0:T(8,128)S(1)}, u32[]{:S(2)}, u32[]{:S(2)}) async-start(f32[32,8,128]{2,1,0:T(8,128)} %get-tuple-element.70), calls=%async_computation.1 | async-start | bytes 262144 | tf_op jit(solution)/shard_map/all_to_all | solution.py:675
  86.0 14.3 %collective-permute-start.17 = (f32[1,16,128]{2,1,0:T(8,128)S(1)}, f32[1,16,128]{2,1,0:T(8,128)S(1)}, u32[]{:S(2)}, u32[]{:S(2)}) collective-permute-start(f32[1,16,128]{2,1,0:T(8,128)S(1)} %get-tuple-element.71.own), channel_id=1, source_target_pairs={{0,64},{32,96},{64,0},{96,32},{1,65},{33,97},{65,1},{97,33},{2,66}... | collective-permute-start | bytes 24584 | tf_op jit(solution)/shard_map/ppermute | solution.py:589
  86.1 6.5 %collective-permute-start.19 = (f32[2,16,128]{2,1,0:T(8,128)S(1)}, f32[2,16,128]{2,1,0:T(8,128)S(1)}, u32[]{:S(2)}, u32[]{:S(2)}) collective-permute-start(f32[2,16,128]{2,1,0:T(8,128)S(1)} %get-tuple-element.78), channel_id=1, source_target_pairs={{1,2},{3,4},{5,6},{7,8},{9,10},{11,12},{13,14},{15,16},{17,18},{19... | collective-permute-start | bytes 49160 | tf_op jit(solution)/shard_map/ppermute | solution.py:595
  101.1 6.5 %collective-permute-start.23 = (f32[2,16,128]{2,1,0:T(8,128)S(1)}, f32[2,16,128]{2,1,0:T(8,128)S(1)}, u32[]{:S(2)}, u32[]{:S(2)}) collective-permute-start(f32[2,16,128]{2,1,0:T(8,128)S(1)} %get-tuple-element.81.here_ref), channel_id=1, source_target_pairs={{0,30},{1,31},{2,0},{3,1},{4,2},{5,3},{6,4},{7,5},{8,6},{9,7},{10,... | collective-permute-start | bytes 49160 | tf_op jit(solution)/shard_map/ppermute | solution.py:589
  101.4 10.1 %collective-permute-start.21 = (f32[18,16,128]{2,1,0:T(8,128)S(1)}, f32[18,16,128]{2,1,0:T(8,128)S(1)}, u32[]{:S(2)}, u32[]{:S(2)}) collective-permute-start(f32[18,16,128]{2,1,0:T(8,128)S(1)} %get-tuple-element.82), channel_id=1, source_target_pairs={{0,1},{2,3},{4,5},{6,7},{8,9},{10,11},{12,13},{14,15},{16,17},{18,... | collective-permute-start | bytes 442376 | tf_op jit(solution)/shard_map/ppermute | solution.py:595
  103.2 8.2 %collective-permute-start.22 = (f32[18,16,128]{2,1,0:T(8,128)S(1)}, f32[18,16,128]{2,1,0:T(8,128)S(1)}, u32[]{:S(2)}, u32[]{:S(2)}) collective-permute-start(f32[18,16,128]{2,1,0:T(8,128)S(1)} %get-tuple-element.83), channel_id=1, source_target_pairs={{1,2},{3,4},{5,6},{7,8},{9,10},{11,12},{13,14},{15,16},{17,18},{19... | collective-permute-start | bytes 442376 | tf_op jit(solution)/shard_map/ppermute | solution.py:595
  104.1 7.3 %collective-permute-start.20 = (f32[2,16,128]{2,1,0:T(8,128)S(1)}, f32[2,16,128]{2,1,0:T(8,128)S(1)}, u32[]{:S(2)}, u32[]{:S(2)}) collective-permute-start(f32[2,16,128]{2,1,0:T(8,128)S(1)} %get-tuple-element.81.here_ref), channel_id=1, source_target_pairs={{0,2},{1,3},{2,4},{3,5},{4,6},{5,7},{6,8},{7,9},{8,10},{9,11},{10,... | collective-permute-start | bytes 49160 | tf_op jit(solution)/shard_map/ppermute | solution.py:589
  105.8 12.6 %collective-permute-start.24 = (f32[16,16,128]{2,1,0:T(8,128)}, f32[16,16,128]{2,1,0:T(8,128)S(1)}, u32[]{:S(2)}, u32[]{:S(2)}) collective-permute-start(f32[16,16,128]{2,1,0:T(8,128)} %copy-done.18), channel_id=1, source_target_pairs={{0,32},{32,64},{64,96},{96,0},{1,33},{33,65},{65,97},{97,1},{2,34}... | collective-permute-start | bytes 393224 | tf_op jit(solution)/shard_map/ppermute | solution.py:589
  107.6 11.5 %collective-permute-start.25 = (f32[16,16,128]{2,1,0:T(8,128)S(1)}, f32[16,16,128]{2,1,0:T(8,128)S(1)}, u32[]{:S(2)}, u32[]{:S(2)}) collective-permute-start(f32[16,16,128]{2,1,0:T(8,128)S(1)} %copy-done.17), channel_id=1, source_target_pairs={{0,96},{32,0},{64,32},{96,64},{1,97},{33,1},{65,33},{97,65},{2,98}... | collective-permute-start | bytes 393224 | tf_op jit(solution)/shard_map/ppermute | solution.py:589
  112.8 15.3 %all-to-all-start.2 = ((f32[32,4,128]{2,1,0:T(4,128)}), f32[32,4,128]{2,1,0:T(4,128)S(1)}, u32[]{:S(2)}, u32[]{:S(2)}) async-start(f32[32,4,128]{2,1,0:T(4,128)} %get-tuple-element.84), calls=%async_computation.2 | async-start | bytes 131072 | tf_op jit(solution)/shard_map/all_to_all | solution.py:675
  (29 other events, 92.4 us)

commit v3 on v2

--- a/solution.py
+++ b/solution.py
@@ -22,7 +22,7 @@
 F32 = jnp.float32
 BF16 = jnp.bfloat16
 HIGHEST = lax.Precision.HIGHEST
-VMEM_LIMIT = 40 * 1024 * 1024
+VMEM_LIMIT = 16 * 1024 * 1024
 
 
 def shape(*dims):
@@ -47,6 +47,10 @@
     low = jnp.minimum(backward, 0.0)
     high = jnp.maximum(backward, 0.0)
     return half_limiter * jnp.minimum(jnp.maximum(forward, low), high)
+
+
+def root(v):
+    return v * lax.rsqrt(jnp.maximum(v, 1e-30))
 
 
 def side(w, d):
@@ -74,8 +78,8 @@
     alfven = square * inverse
     transverse = across * inverse
     gap = sound - alfven
-    fast = 0.5 * (sound + alfven + jnp.sqrt(gap * gap + 4.0 * sound * transverse))
-    speed = jnp.abs(u[d]) + jnp.sqrt(fast)
+    fast = 0.5 * (sound + alfven + root(gap * gap + 4.0 * sound * transverse))
+    speed = jnp.abs(u[d]) + root(fast)
     return flux, [rho, m[0], m[1], m[2], bx, by, bz, energy], speed
 
 
@@ -101,8 +105,12 @@
     refs = list(refs)
     w_ref, lim_ref = refs[:2]
     faces = refs[2:6]
-    lims = refs[6:10]
-    refs = refs[10:]
+    refs = refs[6:]
+    if mode == "first":
+        lims = [face[16] for face in faces]
+    else:
+        lims = [refs[0][k] for k in range(4)]
+        refs = refs[1:]
     if split:
         uy_ref = refs[0]
         uy_faces = refs[1:5]
@@ -115,6 +123,10 @@
         out_ref = refs[0]
         outs = refs[1:5]
         refs = refs[5:]
+    if mode == "first":
+        for k in range(4):
+            refs[0][k] = lims[k]
+        refs = refs[1:]
     ext, lim_ext, turned, lim_turned, across, lx, hx = refs
     even = core() == 0
     place_a = jnp.where(even, CX + 2, 0)
@@ -139,10 +151,10 @@
             turned[f, 2 + y] = centre[:, y, :]
     lim_ext[1 : 1 + CX] = 0.5 * lim_ref[...]
     place = jnp.where(even, CX + 1, 0)
-    lim_ext[place] = 0.5 * lims[2][16]
-    lim_ext[CX + 1 - place] = 0.5 * lims[3][16]
-    lim_turned[0] = 0.5 * lims[0][16]
-    lim_turned[CY + 1] = 0.5 * lims[1][16]
+    lim_ext[place] = 0.5 * lims[2]
+    lim_ext[CX + 1 - place] = 0.5 * lims[3]
+    lim_turned[0] = 0.5 * lims[0]
+    lim_turned[CY + 1] = 0.5 * lims[1]
     for y in range(CY):
         lim_turned[1 + y] = 0.5 * lim_ref[:, y, :]
 
@@ -154,43 +166,34 @@
             left.append(q + half_slope(p, q, r, lim[0]))
             slope = half_slope(q, r, s, lim[1])
             right.append(r - slope)
-            lx[f] = r + slope
+            lx[d, f] = r + slope
         for f, value in enumerate(face_flux(left, right, d)):
-            hx[f] = value
+            hx[d, f] = value
 
     def next_face(w, lim, i, d):
-        left = [lx[f] for f in range(8)]
+        left = [lx[d, f] for f in range(8)]
         right = []
         for f in range(8):
             after = w[f, i + 3]
             slope = half_slope(w[f, i + 2], after, w[f, i + 4], lim[i + 2])
             right.append(after - slope)
-            lx[f] = after + slope
+            lx[d, f] = after + slope
         flux = face_flux(left, right, d)
         difference = []
         for f in range(8):
-            difference.append(flux[f] - hx[f])
-            hx[f] = flux[f]
+            difference.append(flux[f] - hx[d, f])
+            hx[d, f] = flux[f]
         return difference
 
     lowest(turned, lim_turned, 1)
-
-    def row(i, carry):
-        for f, value in enumerate(next_face(turned, lim_turned, i, 1)):
-            turned[f, i] = value
-        return carry
-
-    lax.fori_loop(0, CY, row, 0, unroll=2)
-    for f in range(8):
-        for x in range(CX):
-            across[f, x] = turned[f, 0:CY, x, :]
-
     lowest(ext, lim_ext, 0)
 
     def plane(i, carry):
         lim = lim_ext[i + 1]
         w = [ext[f, i + 2] for f in range(8)]
         total = next_face(ext, lim_ext, i, 0)
+        for f, value in enumerate(next_face(turned, lim_turned, i, 1)):
+            turned[f, i] = value
         left = []
         right = []
         for f in range(8):
@@ -199,7 +202,12 @@
             right.append(pltpu.roll(w[f] - s, CZ - 1, 1))
         flux = face_flux(left, right, 2)
         for f in range(8):
-            total[f] = (total[f] + across[f, i]) + (flux[f] - pltpu.roll(flux[f], 1, 1))
+            across[f, i] = total[f] + (flux[f] - pltpu.roll(flux[f], 1, 1))
+        return carry
+
+    def close(i, carry):
+        w = [ext[f, i + 2] for f in range(8)]
+        total = [across[f, i] for f in range(8)]
         rho, ux, uy, uz, bx, by, bz, p = w
         m = [rho * ux, rho * uy, rho * uz]
         energy = 1.5 * p + 0.5 * (
@@ -223,6 +231,10 @@
         return carry
 
     lax.fori_loop(0, CX, plane, 0, unroll=2)
+    for f in range(8):
+        for x in range(CX):
+            across[f, x] = across[f, x] + turned[f, 0:CY, x, :]
+    lax.fori_loop(0, CX, close, 0, unroll=4)
     if mode != "final":
         write_faces(out_ref, outs, mode == "late")
 
@@ -271,14 +283,16 @@
         pltpu.VMEM((8, CY + 4, CX, CZ), F32),
         pltpu.VMEM((CY + 2, CX, CZ), F32),
         pltpu.VMEM((8, CX, CY, CZ), F32),
-        pltpu.VMEM((8, CY, CZ), F32),
-        pltpu.VMEM((8, CY, CZ), F32),
+        pltpu.VMEM((2, 8, CY, CZ), F32),
+        pltpu.VMEM((2, 8, CY, CZ), F32),
     ]
     outs = [shape(8, CX, CY, CZ)]
-    if mode == "all":
+    if mode in ("first", "all"):
         outs += [shape(16, CX, CZ)] * 4
     elif mode == "late":
         outs += [shape(14, CX, CZ)] * 4
+    if mode == "first":
+        outs += [shape(4, CX, CZ)]
 
     def body(*refs):
         substep_kernel(mode, split, refs)
@@ -300,21 +314,21 @@
     return rows == positions.astype(jnp.int32)
 
 
-def spread(rows, out_ref, first):
+def spread(rows, out_ref, first, last):
     for t in range(SLOTS // CZ):
         tile = rows[:, t * CZ : (t + 1) * CZ]
         for j in range(CZ // CAP):
             moved = tile if j == 0 else pltpu.roll(tile, CZ - CAP * j, 1)
-            out_ref[t * (CZ // CAP) + j, first : first + 4, :] = moved[0:4]
-
-
-def collect(block_ref, rows_ref, first):
+            out_ref[t * (CZ // CAP) + j, first:last, :] = moved[first:last]
+
+
+def collect(block_ref, rows_ref):
     lane = lax.broadcasted_iota(jnp.int32, (8, CZ), 1) // CAP
     per = CZ // CAP
     for t in range(SLOTS // CZ):
         total = jnp.zeros((8, CZ), F32)
         for j in range(per):
-            block = block_ref[t * per + j, first : first + 4, :]
+            block = block_ref[t * per + j]
             block = jnp.concatenate([block, block], axis=0)
             moved = block if j == 0 else pltpu.roll(block, CAP * j, 1)
             total = jnp.where(lane == j, moved, total)
@@ -364,7 +378,7 @@
     for v in range(2):
         kept = jnp.where(levels, found[v * CZ : (v + 1) * CZ], 0.0)
         rows[v : v + 1, :] = jnp.sum(kept, axis=0, keepdims=True)
-    spread(rows[...], out_ref, 0)
+    spread(rows[...], out_ref, 0, 4)
 
 
 def deposit(rows, column, stack):
@@ -393,7 +407,7 @@
 
 
 def deposit_first_kernel(block_ref, low_in, high_in, low_out, high_out, sums, column_ref, rows, stack):
-    collect(block_ref, rows, 0)
+    collect(block_ref, rows)
     column_ref[...] = rows[...]
     value = deposit(rows[...], rows[2:3, :], stack)
     count = low_in.shape[0]
@@ -403,12 +417,11 @@
         folded(value, out_ref, layer)
 
 
-def scatter(block_ref, first, slot_ref, rows, parts):
-    collect(block_ref, rows, first)
-    weight = DRAG_RATE * rows[1:2, :]
+def scatter(rows, at, slot_ref, parts):
+    weight = DRAG_RATE * rows[at + 1 : at + 2, :]
     cells = one_hot(slot_ref[0:1, :], CX * CY).astype(F32).astype(BF16)
     levels = one_hot(slot_ref[1:2, :], CZ)
-    for v, value in enumerate((weight * rows[0:1, :], weight)):
+    for v, value in enumerate((weight * rows[at : at + 1, :], weight)):
         for k, part in enumerate(rounded_parts(value, 2)):
             at = (2 * v + k) * CZ
             parts[at : at + CZ, :] = jnp.where(levels, part, 0.0).astype(BF16)
@@ -423,11 +436,11 @@
 def drag_kernel(
     block_ref, slot_ref, column_ref, w_ref, out_ref, y_low, y_high, x_a, x_b, sums, rows, parts, stack
 ):
-    collect(block_ref, rows, 0)
+    collect(block_ref, rows)
     value = deposit(rows[...], column_ref[2:3, :], stack)
     for out_ref_, layer in ((y_low, 2), (y_high, 2), (sums, 0)):
         folded(value, out_ref_, layer)
-    first, second = scatter(block_ref, 4, slot_ref, rows, parts)
+    first, second = scatter(rows, 2, slot_ref, parts)
     out_ref[...] = w_ref[2] * (1.0 - second) + first
     start = face_start()
     for r in range(2):
@@ -437,14 +450,28 @@
         x_b[r] = out_ref[CX - 2 - start + r]
 
 
-def last_drag_kernel(block_ref, slot_ref, u_ref, out_ref, rows, parts):
-    first, second = scatter(block_ref, 0, slot_ref, rows, parts)
-    out_ref[...] = u_ref[...]
+def last_drag_kernel(block_ref, slot_ref, u_ref, out_ref, rows, parts, changed, sems):
+    kept = [
+        pltpu.make_async_copy(u_ref.at[0:2], out_ref.at[0:2], sems.at[0]),
+        pltpu.make_async_copy(u_ref.at[3:7], out_ref.at[3:7], sems.at[1]),
+    ]
+    for copy in kept:
+        copy.start()
+    collect(block_ref, rows)
+    first, second = scatter(rows, 0, slot_ref, parts)
     rho = u_ref[0]
     my = u_ref[2]
     added = rho * first - my * second
-    out_ref[2] = my + added
-    out_ref[7] = u_ref[7] + (my * added + 0.5 * added * added) / rho
+    changed[0] = my + added
+    changed[1] = u_ref[7] + (my * added + 0.5 * added * added) / rho
+    new = [
+        pltpu.make_async_copy(changed.at[0], out_ref.at[2], sems.at[2]),
+        pltpu.make_async_copy(changed.at[1], out_ref.at[7], sems.at[3]),
+    ]
+    for copy in new:
+        copy.start()
+    for copy in kept + new:
+        copy.wait()
 
 
 def base_kernel(inverse_ref, pedersen_ref, warming_ref, thermal_ref, out_ref, factors):
@@ -566,20 +593,38 @@
     voltage = jnp.where(upper, found[1:2], found[0:1])
     weight = jnp.where(upper, found[3:4], found[2:3])
     sub = lax.broadcasted_iota(jnp.int32, (8, SLOTS), 0)
-    spread(jnp.where(sub % 4 == 0, voltage, weight), out_block, 4 if payload is not None else 0)
-    if payload is not None:
+    rows = jnp.where(sub % 2 == 0, voltage, weight)
+    if payload is None:
+        spread(rows, out_block, 0, 4)
+    else:
+        spread(rows, out_block, 2, 4)
         for owner in range(BLOCKS):
-            out_block[owner, 0:4, :] = payload[owner]
-
-
-def thermal_kernel(thermal_ref, inverse_ref, warming_ref, one_ref, two_ref, out_ref):
-    low_band = lax.broadcasted_iota(jnp.int32, (thermal_ref.shape[0], CZ), 1) < CZ // 2
+            out_block[owner, 0:2, :] = payload[owner, 0:2, :]
+
+
+def thermal_kernel(
+    thermal_ref, inverse_ref, warming_ref, one_ref, two_ref, voltage_ref, out_ref, out_v, own, sem
+):
+    group = lax.axis_index("grp")
+    lanes = pl.ds(pl.multiple_of(group * CZ, CZ), CZ)
+    copy = pltpu.make_async_copy(thermal_ref.at[:, :, lanes], own, sem)
+    copy.start()
+    out_v[...] = voltage_ref[:, lanes]
+    copy.wait()
+    low_band = lax.broadcasted_iota(jnp.int32, (own.shape[0], CZ), 1) < CZ // 2
     for lon in range(2):
-        field = thermal_ref[:, lon, :]
+        field = own[:, lon, :]
         for sums in (one_ref, two_ref):
-            forced = field + warming_ref[...] * sums[2 + lon : 3 + lon, :]
-            low = jnp.dot(inverse_ref[0], forced, precision=HIGHEST, preferred_element_type=F32)
-            high = jnp.dot(inverse_ref[1], forced, precision=HIGHEST, preferred_element_type=F32)
+            forced = field + warming_ref[...] * sums[2 + lon : 3 + lon, lanes]
+            low, high = (
+                jnp.dot(
+                    inverse_ref[2 * group + k],
+                    forced,
+                    precision=HIGHEST,
+                    preferred_element_type=F32,
+                )
+                for k in range(2)
+            )
             field = jnp.where(low_band, low, high)
         out_ref[:, lon, :] = field
 
@@ -603,6 +648,13 @@
         swapped(x_a, 0),
         swapped(x_b, 1),
     )
+
+
+def halos_and_far(faces, here):
+    y_low, y_high, x_a, x_b = faces
+    m2, p2 = shifted(here, "blk", 2), shifted(here, "blk", -2)
+    m2, p2, x_a = lax.optimization_barrier((m2, p2, x_a))
+    return halos((y_low, y_high, x_a, x_b)), m2, p2
 
 
 def body(
@@ -620,8 +672,6 @@
     warming_by_height,
     pedersen_by_height,
 ):
-    group = lax.axis_index("grp")
-    lines = tracer_launch_volume.shape[0]
     sources = tracer_launch_volume[:, 0]
     columns = holder_local_offset[:, 0]
     zero = jnp.zeros_like(sources)
@@ -638,14 +688,14 @@
         ],
         axis=0,
     ).astype(F32)
-    quarter = LATS // 4
 
     fluid, limiter, *faces = pl.pallas_call(
         pack_kernel,
-        out_shape=[shape(8, CX, CY, CZ), shape(CX, CY, CZ)] + [shape(17, CX, CZ)] * 4,
+        out_shape=[pltpu.VMEM((8, CX, CY, CZ), F32), pltpu.VMEM((CX, CY, CZ), F32)]
+        + [pltpu.VMEM((17, CX, CZ), F32)] * 4,
         in_specs=[pl.BlockSpec(memory_space=pltpu.HBM)] * 5,
         scratch_shapes=[pltpu.VMEM((CX, CY, CZ), jnp.int32), pltpu.SemaphoreType.DMA((5,))],
-        compiler_params=pltpu.CompilerParams(vmem_limit_bytes=60 * 1024 * 1024),
+        compiler_params=pltpu.CompilerParams(vmem_limit_bytes=56 * 1024 * 1024),
     )(mass_per_volume, flow_vector, magnetic_vector, thermal_push, gradient_clipping_flags)
     first_halos = halos(faces)
 
@@ -683,17 +733,16 @@
         )(sums, near[0], near[1], far, potential, base_now, x_a, x_b)
 
     def swept(m2, x_a, here, x_b, p2, base_now, column, *payload):
-        rows = 8 if payload else 4
         return kernel_call(
             sweep_kernel,
-            [shape(2, LATS), shape(BLOCKS, rows, CZ), shape(8, LATS), shape(8, LATS)],
+            [shape(2, LATS), shape(BLOCKS, 4, CZ), shape(8, LATS), shape(8, LATS)],
             2.0,
             [pltpu.VMEM((4, 16, LATS), F32), pltpu.VMEM((16, LATS), F32)],
         )(m2, x_a, here, x_b, p2, base_now, column, *payload)
 
     arrived = exchange(payload(fluid, first_halos, 4, 5))
-    fluid, y_low, y_high, x_a, x_b = substep(
-        "all", False, (fluid, limiter, *first_halos, *first_halos)
+    fluid, y_low, y_high, x_a, x_b, limits = substep(
+        "first", False, (fluid, limiter, *first_halos)
     )
     y_low, y_high, sums, column = kernel_call(
         deposit_first_kernel,
@@ -704,11 +753,10 @@
     near = halos((y_low, y_high, x_a, x_b))
     far = shifted(sums, "grp", 2)
     fluid, y_low, y_high, x_a, x_b = substep(
-        "late", False, (fluid, limiter, *near, *first_halos)
+        "late", False, (fluid, limiter, *near, limits)
     )
     x_a, x_b, here = gathered(0, sums, near, far, electric_voltage, base, x_a, x_b)
-    late_halos = halos((y_low, y_high, x_a, x_b))
-    m2, p2 = shifted(here, "blk", 2), shifted(here, "blk", -2)
+    late_halos, m2, p2 = halos_and_far((y_low, y_high, x_a, x_b), here)
     lines = payload(fluid, late_halos, 3, 4)
     voltage, blocks, base_next, here_one = swept(
         m2, late_halos[2], here, late_halos[3], p2, base, column, lines
@@ -726,29 +774,44 @@
     speed_halos = halos(faces)
     far = shifted(sums, "grp", 2)
     fluid, y_low, y_high, x_a, x_b = substep(
-        "all", True, (fluid, limiter, *late_halos, *first_halos, speed, *speed_halos)
+        "all", True, (fluid, limiter, *late_halos, limits, speed, *speed_halos)
     )
     x_a, x_b, here = gathered(2, sums, speed_halos, far, voltage, base_next, x_a, x_b)
-    near = halos((y_low, y_high, x_a, x_b))
-    m2, p2 = shifted(here, "blk", 2), shifted(here, "blk", -2)
+    near, m2, p2 = halos_and_far((y_low, y_high, x_a, x_b), here)
     voltage, blocks, _, here_two = swept(m2, near[2], here, near[3], p2, base_next, column)
     returned = exchange(blocks)
-    (state,) = substep("final", False, (fluid, limiter, *near, *first_halos))
-    conserved_quantities = kernel_call(
-        last_drag_kernel, shape(8, CX, CY, CZ), 1.5, [rows_scratch, parts_scratch]
+    (state,) = substep("final", False, (fluid, limiter, *near, limits))
+    vmem = pl.BlockSpec(memory_space=pltpu.VMEM)
+    conserved_quantities = pl.pallas_call(
+        last_drag_kernel,
+        out_shape=shape(8, CX, CY, CZ),
+        in_specs=[vmem] * 3,
+        out_specs=pl.BlockSpec(memory_space=pl.ANY),
+        scratch_shapes=[
+            rows_scratch,
+            parts_scratch,
+            pltpu.VMEM((2, CX, CY, CZ), F32),
+            pltpu.SemaphoreType.DMA((4,)),
+        ],
+        compiler_params=pltpu.CompilerParams(vmem_limit_bytes=VMEM_LIMIT),
+        cost_estimate=pl.CostEstimate(flops=0, bytes_accessed=5000000, transcendentals=0),
     )(returned, slots, state)
 
-    start = group * quarter
-    ending_thermal_state = kernel_call(
-        thermal_kernel, shape(50, 2, quarter), 2.0
+    ending_thermal_state, ending_electric_voltage = pl.pallas_call(
+        thermal_kernel,
+        out_shape=[shape(50, 2, CZ), shape(2, CZ)],
+        in_specs=[pl.BlockSpec(memory_space=pl.ANY)] + [vmem] * 5,
+        scratch_shapes=[pltpu.VMEM((50, 2, CZ), F32), pltpu.SemaphoreType.DMA],
+        compiler_params=pltpu.CompilerParams(vmem_limit_bytes=VMEM_LIMIT),
+        cost_estimate=pl.CostEstimate(flops=0, bytes_accessed=6600000, transcendentals=0),
     )(
-        lax.dynamic_slice_in_dim(neutral_thermal_field, start, quarter, 2),
-        lax.dynamic_slice_in_dim(reciprocal_operators, group * 2, 2, 0),
+        neutral_thermal_field,
+        reciprocal_operators,
         warming_by_height[:, None],
-        lax.dynamic_slice_in_dim(here_one, start, quarter, 1),
-        lax.dynamic_slice_in_dim(here_two, start, quarter, 1),
-    )
-    ending_electric_voltage = lax.dynamic_slice_in_dim(voltage, start, quarter, 1)
+        here_one,
+        here_two,
+        voltage,
+    )
     return (conserved_quantities, ending_thermal_state, ending_electric_voltage)
 
 

time: 131 us -> 120 us (0.916)
  local copies, waits for them, and re-layouts: 13 us -> 2.41 us
  blocking collectives: 0 us -> 10.5 us
  Pallas kernels: 38.7 us -> 32.3 us
  waiting for transfers between devices: 22.9 us -> 16.9 us
    all_to_all x0 -> x1, blocking collectives: none -> 10.5 us  [exchange(): lax.all_to_all(blocks, 'blk', split_axis=0, concat_axis=0, tiled=True)]
    unnamed x50 -> x18, local copies, waits for them, and re-layouts: 11.4 us -> 2.16 us
    ppermute x16, waiting for transfers between devices: 11.6 us -> 4.77 us  [shifted(): lax.ppermute(value, axis, [(i, (i + by) % count) for i in range(count)])]
    ppermute x16, starting transfers between devices: 19.4 us -> 25.8 us  [shifted(): lax.ppermute(value, axis, [(i, (i + by) % count) for i in range(count)])]
    ppermute x10, waiting for transfers between devices: 2.89 us -> 9.26 us  [swapped(): return lax.ppermute(value, 'blk', pairs + [(j, i) for i, j in pairs])]
    all_to_all x3 -> x2, waiting for transfers between devices: 8.4 us -> 2.85 us  [exchange(): lax.all_to_all(blocks, 'blk', split_axis=0, concat_axis=0, tiled=True)]
    pallas_call x4, Pallas kernels: 25.4 us -> 20.9 us  [substep(): return kernel_call(body, outs, 5.0, scratch)(*args)]
    all_to_all x3 -> x2, starting transfers between devices: 14.8 us -> 11 us  [exchange(): lax.all_to_all(blocks, 'blk', split_axis=0, concat_axis=0, tiled=True)]
  transfers between devices with their start and end apart: 29 -> 28, of which waited for: 10 -> 8; matrix products, arithmetic and copies ran while one was open for 1% -> 0% of each run, Pallas kernels for 23% -> 21%
where the time goes in v3:
time: 120 us; the launch traced here: 119 us
  starting transfers between devices  55.3 us (46%)
  Pallas kernels  32.3 us (27%)
  waiting for transfers between devices  16.9 us (14%)
  blocking collectives  10.5 us (9%)
  local copies, waits for them, and re-layouts  2.41 us (2%)
    ppermute x16, starting transfers between devices, shifted(): lax.ppermute(value, axis, [(i, (i + by) % count) for i in range(count)])  25.8 us
    pallas_call x4, Pallas kernels, substep(): return kernel_call(body, outs, 5.0, scratch)(*args)  20.9 us
    ppermute x10, starting transfers between devices, swapped(): return lax.ppermute(value, 'blk', pairs + [(j, i) for i, j in pairs])  18.5 us
    all_to_all x2, starting transfers between devices, exchange(): lax.all_to_all(blocks, 'blk', split_axis=0, concat_axis=0, tiled=True)  11 us
    all_to_all x1, blocking collectives, exchange(): lax.all_to_all(blocks, 'blk', split_axis=0, concat_axis=0, tiled=True)  10.5 us
    ppermute x10, waiting for transfers between devices, swapped(): return lax.ppermute(value, 'blk', pairs + [(j, i) for i, j in pairs])  9.26 us
    ppermute x16, waiting for transfers between devices, shifted(): lax.ppermute(value, axis, [(i, (i + by) % count) for i in range(count)])  4.77 us
    all_to_all x2, waiting for transfers between devices, exchange(): lax.all_to_all(blocks, 'blk', split_axis=0, concat_axis=0, tiled=True)  2.85 us
  transfers between devices with their start and end apart: 28, of which 8 were waited for; matrix products, arithmetic and copies ran while one was open for 0% of the time, Pallas kernels for 21%

profile of v3, /device:TPU:0, one launch (start us, length us, event | category | flops | bytes accessed | tf_op | source)
XLA Modules:
  0.0 118.5 jit_solution(7349584454825621553)
XLA Ops:
  2.1 1.7 %collective-permute-start = (f32[17,16,128]{2,1,0:T(8,128)S(1)}, f32[17,16,128]{2,1,0:T(8,128)S(1)}, u32[]{:S(2)}, u32[]{:S(2)}) collective-permute-start(f32[17,16,128]{2,1,0:T(8,128)S(1)} %get-tuple-element.57), channel_id=1, source_target_pairs={{0,32},{32,64},{64,96},{96,0},{1,33},{33,65},{65,97},{97,1},{2,34}... | collective-permute-start | bytes 417800 | tf_op jit(solution)/shard_map/ppermute | solution.py:634
  5.4 6.4 %collective-permute-start.3 = (f32[17,16,128]{2,1,0:T(8,128)S(1)}, f32[17,16,128]{2,1,0:T(8,128)S(1)}, u32[]{:S(2)}, u32[]{:S(2)}) collective-permute-start(f32[17,16,128]{2,1,0:T(8,128)S(1)} %get-tuple-element.60), channel_id=1, source_target_pairs={{1,2},{3,4},{5,6},{7,8},{9,10},{11,12},{13,14},{15,16},{17,18},{19... | collective-permute-start | bytes 417800 | tf_op jit(solution)/shard_map/ppermute | solution.py:640
  16.1 6.7 %all-to-all-start = ((f32[32,4,128]{2,1,0:T(4,128)}), f32[32,4,128]{2,1,0:T(4,128)S(1)}, u32[]{:S(2)}, u32[]{:S(2)}) async-start(f32[32,4,128]{2,1,0:T(4,128)} %shard_map.150), calls=%async_computation | async-start | bytes 131072 | tf_op jit(solution)/shard_map/all_to_all | solution.py:725
  22.8 5.3 %shard_map.151 = (f32[8,16,16,128]{3,2,1,0:T(8,128)S(1)}, f32[16,16,128]{2,1,0:T(8,128)S(1)}, f32[16,16,128]{2,1,0:T(8,128)S(1)}, f32[16,16,128]{2,1,0:T(8,128)S...) custom-call(f32[8,16,16,128]{3,2,1,0:T(8,128)S(1)} %get-tuple-element.56.w_ref.refs_0_, ...), custom_call_target="tpu_custom_call" | custom-call | bytes 16500000 | tf_op jit(solution)/shard_map/pallas_call | solution.py:300
  28.1 2.2 %all-to-all-done.block_ref = f32[32,4,128]{2,1,0:T(4,128)S(1)} async-done(((f32[32,4,128]{2,1,0:T(4,128)}), f32[32,4,128]{2,1,0:T(4,128)S(1)}, u32[]{:S(2)}, u32[]{:S(2)}) %all-to-all-start) | async-done | bytes 65568 | tf_op jit(solution)/shard_map/all_to_all | solution.py:725
  31.2 2.9 %collective-permute-start.5 = (f32[17,16,128]{2,1,0:T(8,128)S(1)}, f32[17,16,128]{2,1,0:T(8,128)S(1)}, u32[]{:S(2)}, u32[]{:S(2)}) collective-permute-start(f32[17,16,128]{2,1,0:T(8,128)S(1)} %get-tuple-element.66), channel_id=1, source_target_pairs={{0,96},{32,0},{64,32},{96,64},{1,97},{33,1},{65,33},{97,65},{2,98}... | collective-permute-start | bytes 417800 | tf_op jit(solution)/shard_map/ppermute | solution.py:634
  34.1 3.1 %collective-permute-start.8 = (f32[16,16,128]{2,1,0:T(8,128)S(1)}, f32[16,16,128]{2,1,0:T(8,128)S(1)}, u32[]{:S(2)}, u32[]{:S(2)}) collective-permute-start(f32[16,16,128]{2,1,0:T(8,128)S(1)} %get-tuple-element.69), channel_id=1, source_target_pairs={{1,2},{3,4},{5,6},{7,8},{9,10},{11,12},{13,14},{15,16},{17,18},{19... | collective-permute-start | bytes 393224 | tf_op jit(solution)/shard_map/ppermute | solution.py:640
  40.1 1.7 %collective-permute-done.8.refs_5_ = f32[16,16,128]{2,1,0:T(8,128)S(1)} collective-permute-done((f32[16,16,128]{2,1,0:T(8,128)S(1)}, f32[16,16,128]{2,1,0:T(8,128)S(1)}, u32[]{:S(2)}, u32[]{:S(2)}) %collective-permute-start.8) | collective-permute-done | bytes 131104 | tf_op jit(solution)/shard_map/ppermute | solution.py:640
  41.8 5.3 %shard_map.154 = (f32[8,16,16,128]{3,2,1,0:T(8,128)S(1)}, f32[14,16,128]{2,1,0:T(8,128)S(1)}, f32[14,16,128]{2,1,0:T(8,128)S(1)}, f32[14,16,128]{2,1,0:T(8,128)S(1)}, f32[14,16,128]{2,1,0:T(8,128)S(1)}) custom-call(f32[8,16,16,128]{3,2,1,0:T(8,128)S(1)} %get-tuple-element.67.refs_0_, f32[16,16,128]{2,1,0:T(8,128)S(1)} %get-tuple-element.61.refs_1_, ...), custom_call_target="tpu_custom_call" | custom-call | bytes 16500000 | tf_op jit(solution)/shard_map/pallas_call | solution.py:300
  47.2 2.0 %collective-permute-start.9 = (f32[2,16,128]{2,1,0:T(8,128)S(1)}, f32[2,16,128]{2,1,0:T(8,128)S(1)}, u32[]{:S(2)}, u32[]{:S(2)}) collective-permute-start(f32[2,16,128]{2,1,0:T(8,128)S(1)} %get-tuple-element.73.here_ref), channel_id=1, source_target_pairs={{0,2},{1,3},{2,4},{3,5},{4,6},{5,7},{6,8},{7,9},{8,10},{9,11},{10,... | collective-permute-start | bytes 49160 | tf_op jit(solution)/shard_map/ppermute | solution.py:634
  49.2 5.9 %collective-permute-start.12 = (f32[16,16,128]{2,1,0:T(8,128)S(1)}, f32[16,16,128]{2,1,0:T(8,128)S(1)}, u32[]{:S(2)}, u32[]{:S(2)}) collective-permute-start(f32[16,16,128]{2,1,0:T(8,128)S(1)} %get-tuple-element.77), channel_id=1, source_target_pairs={{1,2},{3,4},{5,6},{7,8},{9,10},{11,12},{13,14},{15,16},{17,18},{19... | collective-permute-start | bytes 393224 | tf_op jit(solution)/shard_map/ppermute | solution.py:640
  56.3 3.2 %collective-permute-start.14 = (f32[14,16,128]{2,1,0:T(8,128)S(1)}, f32[14,16,128]{2,1,0:T(8,128)S(1)}, u32[]{:S(2)}, u32[]{:S(2)}) collective-permute-start(f32[14,16,128]{2,1,0:T(8,128)S(1)} %get-tuple-element.82), channel_id=1, source_target_pairs={{0,96},{32,0},{64,32},{96,64},{1,97},{33,1},{65,33},{97,65},{2,98}... | collective-permute-start | bytes 344072 | tf_op jit(solution)/shard_map/ppermute | solution.py:634
  59.6 3.0 %collective-permute-done.13.y_low.refs_2_ = f32[14,16,128]{2,1,0:T(8,128)S(1)} collective-permute-done((f32[14,16,128]{2,1,0:T(8,128)S(1)}, f32[14,16,128]{2,1,0:T(8,128)S(1)}, u32[]{:S(2)}, u32[]{:S(2)}) %collective-permute-start.13) | collective-permute-done | bytes 114720 | tf_op jit(solution)/shard_map/ppermute | solution.py:634
  64.2 10.5 %all_to_all.15.block_ref = f32[32,4,128]{2,1,0:T(4,128)S(1)} all-to-all(f32[32,4,128]{2,1,0:T(4,128)S(1)} %get-tuple-element.83), channel_id=1, replica_groups=mesh['grp'=4,'blk'=32] {'blk'}, dimensions={0} | all-to-all | bytes 131072 | tf_op jit(solution)/shard_map/all_to_all | solution.py:725
  75.7 3.2 %collective-permute-start.16 = (f32[3,16,128]{2,1,0:T(8,128)S(1)}, f32[3,16,128]{2,1,0:T(8,128)S(1)}, u32[]{:S(2)}, u32[]{:S(2)}) collective-permute-start(f32[3,16,128]{2,1,0:T(8,128)S(1)} %get-tuple-element.86), channel_id=1, source_target_pairs={{0,96},{32,0},{64,32},{96,64},{1,97},{33,1},{65,33},{97,65},{2,98}... | collective-permute-start | bytes 73736 | tf_op jit(solution)/shard_map/ppermute | solution.py:634
  78.9 1.8 %collective-permute-start.19 = (f32[2,16,128]{2,1,0:T(8,128)S(1)}, f32[2,16,128]{2,1,0:T(8,128)S(1)}, u32[]{:S(2)}, u32[]{:S(2)}) collective-permute-start(f32[2,16,128]{2,1,0:T(8,128)S(1)} %get-tuple-element.91), channel_id=1, source_target_pairs={{1,2},{3,4},{5,6},{7,8},{9,10},{11,12},{13,14},{15,16},{17,18},{19... | collective-permute-start | bytes 49160 | tf_op jit(solution)/shard_map/ppermute | solution.py:640
  81.9 3.4 %collective-permute-done.19.refs_11_ = f32[2,16,128]{2,1,0:T(8,128)S(1)} collective-permute-done((f32[2,16,128]{2,1,0:T(8,128)S(1)}, f32[2,16,128]{2,1,0:T(8,128)S(1)}, u32[]{:S(2)}, u32[]{:S(2)}) %collective-permute-start.19) | collective-permute-done | bytes 16416 | tf_op jit(solution)/shard_map/ppermute | solution.py:640
  85.4 5.3 %shard_map.159 = (f32[8,16,16,128]{3,2,1,0:T(8,128)S(1)}, f32[16,16,128]{2,1,0:T(8,128)S(1)}, f32[16,16,128]{2,1,0:T(8,128)S(1)}, f32[16,16,128]{2,1,0:T(8,128)S(1)}, f32[16,16,128]{2,1,0:T(8,128)S(1)}) custom-call(f32[8,16,16,128]{3,2,1,0:T(8,128)S(1)} %get-tuple-element.80.w_ref.refs_0_, f32[16,16,128]{2,1,0:T(8,128)S(1)} %get-tuple-element.61.refs_1_, ...), custom_call_target="tpu_custom_call" | custom-call | bytes 16500000 | tf_op jit(solution)/shard_map/pallas_call | solution.py:300
  90.8 5.3 %collective-permute-start.21 = (f32[2,16,128]{2,1,0:T(8,128)S(1)}, f32[2,16,128]{2,1,0:T(8,128)S(1)}, u32[]{:S(2)}, u32[]{:S(2)}) collective-permute-start(f32[2,16,128]{2,1,0:T(8,128)S(1)} %get-tuple-element.94.here_ref), channel_id=1, source_target_pairs={{0,30},{1,31},{2,0},{3,1},{4,2},{5,3},{6,4},{7,5},{8,6},{9,7},{10,... | collective-permute-start | bytes 49160 | tf_op jit(solution)/shard_map/ppermute | solution.py:634
  96.1 1.7 %collective-permute-done.20.m2 = f32[2,16,128]{2,1,0:T(8,128)S(1)} collective-permute-done((f32[2,16,128]{2,1,0:T(8,128)S(1)}, f32[2,16,128]{2,1,0:T(8,128)S(1)}, u32[]{:S(2)}, u32[]{:S(2)}) %collective-permute-start.20) | collective-permute-done | bytes 16416 | tf_op jit(solution)/shard_map/ppermute | solution.py:634
  97.9 3.2 %collective-permute-start.25 = (f32[16,16,128]{2,1,0:T(8,128)S(1)}, f32[16,16,128]{2,1,0:T(8,128)S(1)}, u32[]{:S(2)}, u32[]{:S(2)}) collective-permute-start(f32[16,16,128]{2,1,0:T(8,128)S(1)} %get-tuple-element.103), channel_id=1, source_target_pairs={{0,96},{32,0},{64,32},{96,64},{1,97},{33,1},{65,33},{97,65},{2,98}... | collective-permute-start | bytes 393224 | tf_op jit(solution)/shard_map/ppermute | solution.py:634
  101.1 2.9 %collective-permute-done.23.x_b.refs_5_ = f32[18,16,128]{2,1,0:T(8,128)S(1)} collective-permute-done((f32[18,16,128]{2,1,0:T(8,128)S(1)}, f32[18,16,128]{2,1,0:T(8,128)S(1)}, u32[]{:S(2)}, u32[]{:S(2)}) %collective-permute-start.23) | collective-permute-done | bytes 147488 | tf_op jit(solution)/shard_map/ppermute | solution.py:640
  105.4 4.3 %all-to-all-start.2 = ((f32[32,4,128]{2,1,0:T(4,128)}), f32[32,4,128]{2,1,0:T(4,128)S(1)}, u32[]{:S(2)}, u32[]{:S(2)}) async-start(f32[32,4,128]{2,1,0:T(4,128)} %get-tuple-element.100), calls=%async_computation.2 | async-start | bytes 131072 | tf_op jit(solution)/shard_map/all_to_all | solution.py:725
  111.3 5.0 %shard_map.162.u_ref = f32[8,16,16,128]{3,2,1,0:T(8,128)S(1)} custom-call(f32[8,16,16,128]{3,2,1,0:T(8,128)S(1)} %get-tuple-element.101.refs_0_, f32[16,16,128]{2,1,0:T(8,128)S(1)} %get-tuple-element.61.refs_1_, f32[16,16,128]{2,1,0:T(8,128)S(1)} %collective-permute-done.24.refs_2_, f32[16,16,128]{2,1,0:T(8,128)S(1)} %collective-permute-done.25.refs_3_, ...), custom_call_target="tpu_custom_call" | custom-call | bytes 16500000 | tf_op jit(solution)/shard_map/pallas_call | solution.py:300
  (77 shorter events, 21.1 us)
Async XLA Ops:
  2.1 11.3 %collective-permute-start = (f32[17,16,128]{2,1,0:T(8,128)S(1)}, f32[17,16,128]{2,1,0:T(8,128)S(1)}, u32[]{:S(2)}, u32[]{:S(2)}) collective-permute-start(f32[17,16,128]{2,1,0:T(8,128)S(1)} %get-tuple-element.57), channel_id=1, source_target_pairs={{0,32},{32,64},{64,96},{96,0},{1,33},{33,65},{65,97},{97,1},{2,34}... | collective-permute-start | bytes 417800 | tf_op jit(solution)/shard_map/ppermute | solution.py:634
  3.8 9.6 %collective-permute-start.1 = (f32[17,16,128]{2,1,0:T(8,128)S(1)}, f32[17,16,128]{2,1,0:T(8,128)S(1)}, u32[]{:S(2)}, u32[]{:S(2)}) collective-permute-start(f32[17,16,128]{2,1,0:T(8,128)S(1)} %get-tuple-element.58), channel_id=1, source_target_pairs={{0,96},{32,0},{64,32},{96,64},{1,97},{33,1},{65,33},{97,65},{2,98}... | collective-permute-start | bytes 417800 | tf_op jit(solution)/shard_map/ppermute | solution.py:634
  5.4 8.0 %collective-permute-start.2 = (f32[17,16,128]{2,1,0:T(8,128)S(1)}, f32[17,16,128]{2,1,0:T(8,128)S(1)}, u32[]{:S(2)}, u32[]{:S(2)}) collective-permute-start(f32[17,16,128]{2,1,0:T(8,128)S(1)} %get-tuple-element.59), channel_id=1, source_target_pairs={{0,1},{2,3},{4,5},{6,7},{8,9},{10,11},{12,13},{14,15},{16,17},{18,... | collective-permute-start | bytes 417800 | tf_op jit(solution)/shard_map/ppermute | solution.py:640
  5.4 9.2 %collective-permute-start.3 = (f32[17,16,128]{2,1,0:T(8,128)S(1)}, f32[17,16,128]{2,1,0:T(8,128)S(1)}, u32[]{:S(2)}, u32[]{:S(2)}) collective-permute-start(f32[17,16,128]{2,1,0:T(8,128)S(1)} %get-tuple-element.60), channel_id=1, source_target_pairs={{1,2},{3,4},{5,6},{7,8},{9,10},{11,12},{13,14},{15,16},{17,18},{19... | collective-permute-start | bytes 417800 | tf_op jit(solution)/shard_map/ppermute | solution.py:640
  16.1 14.3 %all-to-all-start = ((f32[32,4,128]{2,1,0:T(4,128)}), f32[32,4,128]{2,1,0:T(4,128)S(1)}, u32[]{:S(2)}, u32[]{:S(2)}) async-start(f32[32,4,128]{2,1,0:T(4,128)} %shard_map.150), calls=%async_computation | async-start | bytes 131072 | tf_op jit(solution)/shard_map/all_to_all | solution.py:725
  30.9 11.0 %collective-permute-start.4 = (f32[17,16,128]{2,1,0:T(8,128)S(1)}, f32[17,16,128]{2,1,0:T(8,128)S(1)}, u32[]{:S(2)}, u32[]{:S(2)}) collective-permute-start(f32[17,16,128]{2,1,0:T(8,128)S(1)} %get-tuple-element.65), channel_id=1, source_target_pairs={{0,32},{32,64},{64,96},{96,0},{1,33},{33,65},{65,97},{97,1},{2,34}... | collective-permute-start | bytes 417800 | tf_op jit(solution)/shard_map/ppermute | solution.py:634
  31.2 10.6 %collective-permute-start.5 = (f32[17,16,128]{2,1,0:T(8,128)S(1)}, f32[17,16,128]{2,1,0:T(8,128)S(1)}, u32[]{:S(2)}, u32[]{:S(2)}) collective-permute-start(f32[17,16,128]{2,1,0:T(8,128)S(1)} %get-tuple-element.66), channel_id=1, source_target_pairs={{0,96},{32,0},{64,32},{96,64},{1,97},{33,1},{65,33},{97,65},{2,98}... | collective-permute-start | bytes 417800 | tf_op jit(solution)/shard_map/ppermute | solution.py:634
  34.1 7.7 %collective-permute-start.8 = (f32[16,16,128]{2,1,0:T(8,128)S(1)}, f32[16,16,128]{2,1,0:T(8,128)S(1)}, u32[]{:S(2)}, u32[]{:S(2)}) collective-permute-start(f32[16,16,128]{2,1,0:T(8,128)S(1)} %get-tuple-element.69), channel_id=1, source_target_pairs={{1,2},{3,4},{5,6},{7,8},{9,10},{11,12},{13,14},{15,16},{17,18},{19... | collective-permute-start | bytes 393224 | tf_op jit(solution)/shard_map/ppermute | solution.py:640
  37.2 9.9 %collective-permute-start.6 = (f32[1,16,128]{2,1,0:T(8,128)S(1)}, f32[1,16,128]{2,1,0:T(8,128)S(1)}, u32[]{:S(2)}, u32[]{:S(2)}) collective-permute-start(f32[1,16,128]{2,1,0:T(8,128)S(1)} %get-tuple-element.64.own), channel_id=1, source_target_pairs={{0,64},{32,96},{64,0},{96,32},{1,65},{33,97},{65,1},{97,33},{2,66}... | collective-permute-start | bytes 24584 | tf_op jit(solution)/shard_map/ppermute | solution.py:634
  47.2 8.0 %collective-permute-start.10 = (f32[2,16,128]{2,1,0:T(8,128)S(1)}, f32[2,16,128]{2,1,0:T(8,128)S(1)}, u32[]{:S(2)}, u32[]{:S(2)}) collective-permute-start(f32[2,16,128]{2,1,0:T(8,128)S(1)} %get-tuple-element.73.here_ref), channel_id=1, source_target_pairs={{0,30},{1,31},{2,0},{3,1},{4,2},{5,3},{6,4},{7,5},{8,6},{9,7},{10,... | collective-permute-start | bytes 49160 | tf_op jit(solution)/shard_map/ppermute | solution.py:634
  47.2 7.9 %collective-permute-start.9 = (f32[2,16,128]{2,1,0:T(8,128)S(1)}, f32[2,16,128]{2,1,0:T(8,128)S(1)}, u32[]{:S(2)}, u32[]{:S(2)}) collective-permute-start(f32[2,16,128]{2,1,0:T(8,128)S(1)} %get-tuple-element.73.here_ref), channel_id=1, source_target_pairs={{0,2},{1,3},{2,4},{3,5},{4,6},{5,7},{6,8},{7,9},{8,10},{9,11},{10,... | collective-permute-start | bytes 49160 | tf_op jit(solution)/shard_map/ppermute | solution.py:634
  49.2 13.4 %collective-permute-start.12 = (f32[16,16,128]{2,1,0:T(8,128)S(1)}, f32[16,16,128]{2,1,0:T(8,128)S(1)}, u32[]{:S(2)}, u32[]{:S(2)}) collective-permute-start(f32[16,16,128]{2,1,0:T(8,128)S(1)} %get-tuple-element.77), channel_id=1, source_target_pairs={{1,2},{3,4},{5,6},{7,8},{9,10},{11,12},{13,14},{15,16},{17,18},{19... | collective-permute-start | bytes 393224 | tf_op jit(solution)/shard_map/ppermute | solution.py:640
  55.1 7.5 %collective-permute-start.11 = (f32[16,16,128]{2,1,0:T(8,128)S(1)}, f32[16,16,128]{2,1,0:T(8,128)S(1)}, u32[]{:S(2)}, u32[]{:S(2)}) collective-permute-start(f32[16,16,128]{2,1,0:T(8,128)S(1)} %get-tuple-element.76), channel_id=1, source_target_pairs={{0,1},{2,3},{4,5},{6,7},{8,9},{10,11},{12,13},{14,15},{16,17},{18,... | collective-permute-start | bytes 393224 | tf_op jit(solution)/shard_map/ppermute | solution.py:640
  56.3 6.3 %collective-permute-start.13 = (f32[14,16,128]{2,1,0:T(8,128)S(1)}, f32[14,16,128]{2,1,0:T(8,128)S(1)}, u32[]{:S(2)}, u32[]{:S(2)}) collective-permute-start(f32[14,16,128]{2,1,0:T(8,128)S(1)} %get-tuple-element.81), channel_id=1, source_target_pairs={{0,32},{32,64},{64,96},{96,0},{1,33},{33,65},{65,97},{97,1},{2,34}... | collective-permute-start | bytes 344072 | tf_op jit(solution)/shard_map/ppermute | solution.py:634
  75.6 9.8 %collective-permute-start.15 = (f32[3,16,128]{2,1,0:T(8,128)S(1)}, f32[3,16,128]{2,1,0:T(8,128)S(1)}, u32[]{:S(2)}, u32[]{:S(2)}) collective-permute-start(f32[3,16,128]{2,1,0:T(8,128)S(1)} %get-tuple-element.85), channel_id=1, source_target_pairs={{0,32},{32,64},{64,96},{96,0},{1,33},{33,65},{65,97},{97,1},{2,34}... | collective-permute-start | bytes 73736 | tf_op jit(solution)/shard_map/ppermute | solution.py:634
  75.7 9.7 %collective-permute-start.16 = (f32[3,16,128]{2,1,0:T(8,128)S(1)}, f32[3,16,128]{2,1,0:T(8,128)S(1)}, u32[]{:S(2)}, u32[]{:S(2)}) collective-permute-start(f32[3,16,128]{2,1,0:T(8,128)S(1)} %get-tuple-element.86), channel_id=1, source_target_pairs={{0,96},{32,0},{64,32},{96,64},{1,97},{33,1},{65,33},{97,65},{2,98}... | collective-permute-start | bytes 73736 | tf_op jit(solution)/shard_map/ppermute | solution.py:634
  78.9 6.5 %collective-permute-start.19 = (f32[2,16,128]{2,1,0:T(8,128)S(1)}, f32[2,16,128]{2,1,0:T(8,128)S(1)}, u32[]{:S(2)}, u32[]{:S(2)}) collective-permute-start(f32[2,16,128]{2,1,0:T(8,128)S(1)} %get-tuple-element.91), channel_id=1, source_target_pairs={{1,2},{3,4},{5,6},{7,8},{9,10},{11,12},{13,14},{15,16},{17,18},{19... | collective-permute-start | bytes 49160 | tf_op jit(solution)/shard_map/ppermute | solution.py:640
  80.7 9.9 %collective-permute-start.17 = (f32[1,16,128]{2,1,0:T(8,128)S(1)}, f32[1,16,128]{2,1,0:T(8,128)S(1)}, u32[]{:S(2)}, u32[]{:S(2)}) collective-permute-start(f32[1,16,128]{2,1,0:T(8,128)S(1)} %get-tuple-element.84.own), channel_id=1, source_target_pairs={{0,64},{32,96},{64,0},{96,32},{1,65},{33,97},{65,1},{97,33},{2,66}... | collective-permute-start | bytes 24584 | tf_op jit(solution)/shard_map/ppermute | solution.py:634
  90.7 7.1 %collective-permute-start.20 = (f32[2,16,128]{2,1,0:T(8,128)S(1)}, f32[2,16,128]{2,1,0:T(8,128)S(1)}, u32[]{:S(2)}, u32[]{:S(2)}) collective-permute-start(f32[2,16,128]{2,1,0:T(8,128)S(1)} %get-tuple-element.94.here_ref), channel_id=1, source_target_pairs={{0,2},{1,3},{2,4},{3,5},{4,6},{5,7},{6,8},{7,9},{8,10},{9,11},{10,... | collective-permute-start | bytes 49160 | tf_op jit(solution)/shard_map/ppermute | solution.py:634
  90.8 7.0 %collective-permute-start.21 = (f32[2,16,128]{2,1,0:T(8,128)S(1)}, f32[2,16,128]{2,1,0:T(8,128)S(1)}, u32[]{:S(2)}, u32[]{:S(2)}) collective-permute-start(f32[2,16,128]{2,1,0:T(8,128)S(1)} %get-tuple-element.94.here_ref), channel_id=1, source_target_pairs={{0,30},{1,31},{2,0},{3,1},{4,2},{5,3},{6,4},{7,5},{8,6},{9,7},{10,... | collective-permute-start | bytes 49160 | tf_op jit(solution)/shard_map/ppermute | solution.py:634
  96.1 7.9 %collective-permute-start.23 = (f32[18,16,128]{2,1,0:T(8,128)S(1)}, f32[18,16,128]{2,1,0:T(8,128)S(1)}, u32[]{:S(2)}, u32[]{:S(2)}) collective-permute-start(f32[18,16,128]{2,1,0:T(8,128)S(1)} %get-tuple-element.98), channel_id=1, source_target_pairs={{1,2},{3,4},{5,6},{7,8},{9,10},{11,12},{13,14},{15,16},{17,18},{19... | collective-permute-start | bytes 442376 | tf_op jit(solution)/shard_map/ppermute | solution.py:640
  97.8 13.5 %collective-permute-start.24 = (f32[16,16,128]{2,1,0:T(8,128)S(1)}, f32[16,16,128]{2,1,0:T(8,128)S(1)}, u32[]{:S(2)}, u32[]{:S(2)}) collective-permute-start(f32[16,16,128]{2,1,0:T(8,128)S(1)} %get-tuple-element.102), channel_id=1, source_target_pairs={{0,32},{32,64},{64,96},{96,0},{1,33},{33,65},{65,97},{97,1},{2,34}... | collective-permute-start | bytes 393224 | tf_op jit(solution)/shard_map/ppermute | solution.py:634
  97.9 13.5 %collective-permute-start.25 = (f32[16,16,128]{2,1,0:T(8,128)S(1)}, f32[16,16,128]{2,1,0:T(8,128)S(1)}, u32[]{:S(2)}, u32[]{:S(2)}) collective-permute-start(f32[16,16,128]{2,1,0:T(8,128)S(1)} %get-tuple-element.103), channel_id=1, source_target_pairs={{0,96},{32,0},{64,32},{96,64},{1,97},{33,1},{65,33},{97,65},{2,98}... | collective-permute-start | bytes 393224 | tf_op jit(solution)/shard_map/ppermute | solution.py:634
  105.4 11.6 %all-to-all-start.2 = ((f32[32,4,128]{2,1,0:T(4,128)}), f32[32,4,128]{2,1,0:T(4,128)S(1)}, u32[]{:S(2)}, u32[]{:S(2)}) async-start(f32[32,4,128]{2,1,0:T(4,128)} %get-tuple-element.100), calls=%async_computation.2 | async-start | bytes 131072 | tf_op jit(solution)/shard_map/all_to_all | solution.py:725
  (12 other events, 54.0 us)

commit v4 on v3

--- a/solution.py
+++ b/solution.py
@@ -314,25 +314,35 @@
     return rows == positions.astype(jnp.int32)
 
 
-def spread(rows, out_ref, first, last):
-    for t in range(SLOTS // CZ):
-        tile = rows[:, t * CZ : (t + 1) * CZ]
-        for j in range(CZ // CAP):
-            moved = tile if j == 0 else pltpu.roll(tile, CZ - CAP * j, 1)
-            out_ref[t * (CZ // CAP) + j, first:last, :] = moved[first:last]
-
-
-def collect(block_ref, rows_ref):
+def turned_segments(tile):
+    tile = jnp.concatenate([tile, tile], axis=0)
     lane = lax.broadcasted_iota(jnp.int32, (8, CZ), 1) // CAP
+    row = lax.broadcasted_iota(jnp.int32, (8, CZ), 0)
+    same = lane == row % 4
+    total = jnp.where(same, tile, 0.0)
+    for d in range(1, 4):
+        moved = jnp.where(same, pltpu.roll(tile, CAP * d, 1), 0.0)
+        total = total + pltpu.roll(moved, 8 - d, 0)
+    return total
+
+
+def spread(rows, out_ref, kept=None):
+    half = lax.broadcasted_iota(jnp.int32, (1, CZ), 1) < 2 * CAP
     per = CZ // CAP
     for t in range(SLOTS // CZ):
-        total = jnp.zeros((8, CZ), F32)
+        tile = turned_segments(rows[0:4, t * CZ : (t + 1) * CZ])
         for j in range(per):
-            block = block_ref[t * per + j]
-            block = jnp.concatenate([block, block], axis=0)
-            moved = block if j == 0 else pltpu.roll(block, CAP * j, 1)
-            total = jnp.where(lane == j, moved, total)
-        rows_ref[:, t * CZ : (t + 1) * CZ] = total
+            block = tile[j : j + 1]
+            if kept is not None:
+                block = jnp.where(half, kept[t * per + j], block)
+            out_ref[t * per + j] = block
+
+
+def collect(block_ref, rows_ref):
+    per = CZ // CAP
+    for t in range(SLOTS // CZ):
+        tile = jnp.concatenate([block_ref[t * per + j] for j in range(per)], axis=0)
+        rows_ref[:, t * CZ : (t + 1) * CZ] = turned_segments(tile)
 
 
 def slot_kernel(owner_ref, rows_ref, out_ref):
@@ -378,7 +388,7 @@
     for v in range(2):
         kept = jnp.where(levels, found[v * CZ : (v + 1) * CZ], 0.0)
         rows[v : v + 1, :] = jnp.sum(kept, axis=0, keepdims=True)
-    spread(rows[...], out_ref, 0, 4)
+    spread(rows[...], out_ref)
 
 
 def deposit(rows, column, stack):
@@ -594,12 +604,7 @@
     weight = jnp.where(upper, found[3:4], found[2:3])
     sub = lax.broadcasted_iota(jnp.int32, (8, SLOTS), 0)
     rows = jnp.where(sub % 2 == 0, voltage, weight)
-    if payload is None:
-        spread(rows, out_block, 0, 4)
-    else:
-        spread(rows, out_block, 2, 4)
-        for owner in range(BLOCKS):
-            out_block[owner, 0:2, :] = payload[owner, 0:2, :]
+    spread(rows, out_block, payload)
 
 
 def thermal_kernel(
@@ -716,7 +721,7 @@
     def payload(w, near, fx, fy):
         return kernel_call(
             functools.partial(payload_kernel, fx, fy),
-            shape(BLOCKS, 4, CZ),
+            shape(BLOCKS, 1, CZ),
             2.0,
             [pltpu.VMEM((CX * CY, 2 * CZ), F32), rows_scratch],
         )(w, *near, slots)
@@ -735,7 +740,7 @@
     def swept(m2, x_a, here, x_b, p2, base_now, column, *payload):
         return kernel_call(
             sweep_kernel,
-            [shape(2, LATS), shape(BLOCKS, 4, CZ), shape(8, LATS), shape(8, LATS)],
+            [shape(2, LATS), shape(BLOCKS, 1, CZ), shape(8, LATS), shape(8, LATS)],
             2.0,
             [pltpu.VMEM((4, 16, LATS), F32), pltpu.VMEM((16, LATS), F32)],
         )(m2, x_a, here, x_b, p2, base_now, column, *payload)

time: 120 us -> 119 us (level)
  no operation moved by 1% of the time
where the time goes in v4:
time: 119 us; the launch traced here: 118 us
  starting transfers between devices  55.7 us (47%)
  Pallas kernels  32.2 us (27%)
  waiting for transfers between devices  16.2 us (14%)
  blocking collectives  10.3 us (9%)
  local copies, waits for them, and re-layouts  2.41 us (2%)
    ppermute x16, starting transfers between devices, shifted(): lax.ppermute(value, axis, [(i, (i + by) % count) for i in range(count)])  25.8 us
    pallas_call x4, Pallas kernels, substep(): return kernel_call(body, outs, 5.0, scratch)(*args)  20.9 us
    ppermute x10, starting transfers between devices, swapped(): return lax.ppermute(value, 'blk', pairs + [(j, i) for i, j in pairs])  18.9 us
    all_to_all x2, starting transfers between devices, exchange(): lax.all_to_all(blocks, 'blk', split_axis=0, concat_axis=0, tiled=True)  11 us
    all_to_all x1, blocking collectives, exchange(): lax.all_to_all(blocks, 'blk', split_axis=0, concat_axis=0, tiled=True)  10.3 us
    ppermute x10, waiting for transfers between devices, swapped(): return lax.ppermute(value, 'blk', pairs + [(j, i) for i, j in pairs])  9.04 us
    ppermute x16, waiting for transfers between devices, shifted(): lax.ppermute(value, axis, [(i, (i + by) % count) for i in range(count)])  4.77 us
    all_to_all x2, waiting for transfers between devices, exchange(): lax.all_to_all(blocks, 'blk', split_axis=0, concat_axis=0, tiled=True)  2.39 us
  transfers between devices with their start and end apart: 28, of which 8 were waited for; matrix products, arithmetic and copies ran while one was open for 0% of the time, Pallas kernels for 21%

profile of v4, /device:TPU:0, one launch (start us, length us, event | category | flops | bytes accessed | tf_op | source)
XLA Modules:
  0.0 118.1 jit_solution(330932627826907344)
XLA Ops:
  2.1 1.7 %collective-permute-start = (f32[17,16,128]{2,1,0:T(8,128)S(1)}, f32[17,16,128]{2,1,0:T(8,128)S(1)}, u32[]{:S(2)}, u32[]{:S(2)}) collective-permute-start(f32[17,16,128]{2,1,0:T(8,128)S(1)} %get-tuple-element.57), channel_id=1, source_target_pairs={{0,32},{32,64},{64,96},{96,0},{1,33},{33,65},{65,97},{97,1},{2,34}... | collective-permute-start | bytes 417800 | tf_op jit(solution)/shard_map/ppermute | solution.py:639
  3.8 1.6 %collective-permute-start.1 = (f32[17,16,128]{2,1,0:T(8,128)S(1)}, f32[17,16,128]{2,1,0:T(8,128)S(1)}, u32[]{:S(2)}, u32[]{:S(2)}) collective-permute-start(f32[17,16,128]{2,1,0:T(8,128)S(1)} %get-tuple-element.58), channel_id=1, source_target_pairs={{0,96},{32,0},{64,32},{96,64},{1,97},{33,1},{65,33},{97,65},{2,98}... | collective-permute-start | bytes 417800 | tf_op jit(solution)/shard_map/ppermute | solution.py:639
  5.4 6.4 %collective-permute-start.3 = (f32[17,16,128]{2,1,0:T(8,128)S(1)}, f32[17,16,128]{2,1,0:T(8,128)S(1)}, u32[]{:S(2)}, u32[]{:S(2)}) collective-permute-start(f32[17,16,128]{2,1,0:T(8,128)S(1)} %get-tuple-element.60), channel_id=1, source_target_pairs={{1,2},{3,4},{5,6},{7,8},{9,10},{11,12},{13,14},{15,16},{17,18},{19... | collective-permute-start | bytes 417800 | tf_op jit(solution)/shard_map/ppermute | solution.py:645
  16.1 6.7 %all-to-all-start = ((f32[32,1,128]{2,1,0:T(1,128)}), f32[32,1,128]{2,1,0:T(1,128)S(1)}, u32[]{:S(2)}, u32[]{:S(2)}) async-start(f32[32,1,128]{2,1,0:T(1,128)} %shard_map.150), calls=%async_computation | async-start | bytes 32768 | tf_op jit(solution)/shard_map/all_to_all | solution.py:730
  22.8 5.3 %shard_map.151 = (f32[8,16,16,128]{3,2,1,0:T(8,128)S(1)}, f32[16,16,128]{2,1,0:T(8,128)S(1)}, f32[16,16,128]{2,1,0:T(8,128)S(1)}, f32[16,16,128]{2,1,0:T(8,128)S...) custom-call(f32[8,16,16,128]{3,2,1,0:T(8,128)S(1)} %get-tuple-element.56.w_ref.refs_0_, ...), custom_call_target="tpu_custom_call" | custom-call | bytes 16500000 | tf_op jit(solution)/shard_map/pallas_call | solution.py:300
  28.1 2.0 %all-to-all-done.block_ref = f32[32,1,128]{2,1,0:T(1,128)S(1)} async-done(((f32[32,1,128]{2,1,0:T(1,128)}), f32[32,1,128]{2,1,0:T(1,128)S(1)}, u32[]{:S(2)}, u32[]{:S(2)}) %all-to-all-start) | async-done | bytes 16416 | tf_op jit(solution)/shard_map/all_to_all | solution.py:730
  31.0 2.9 %collective-permute-start.5 = (f32[17,16,128]{2,1,0:T(8,128)S(1)}, f32[17,16,128]{2,1,0:T(8,128)S(1)}, u32[]{:S(2)}, u32[]{:S(2)}) collective-permute-start(f32[17,16,128]{2,1,0:T(8,128)S(1)} %get-tuple-element.66), channel_id=1, source_target_pairs={{0,96},{32,0},{64,32},{96,64},{1,97},{33,1},{65,33},{97,65},{2,98}... | collective-permute-start | bytes 417800 | tf_op jit(solution)/shard_map/ppermute | solution.py:639
  33.9 3.3 %collective-permute-start.8 = (f32[16,16,128]{2,1,0:T(8,128)S(1)}, f32[16,16,128]{2,1,0:T(8,128)S(1)}, u32[]{:S(2)}, u32[]{:S(2)}) collective-permute-start(f32[16,16,128]{2,1,0:T(8,128)S(1)} %get-tuple-element.69), channel_id=1, source_target_pairs={{1,2},{3,4},{5,6},{7,8},{9,10},{11,12},{13,14},{15,16},{17,18},{19... | collective-permute-start | bytes 393224 | tf_op jit(solution)/shard_map/ppermute | solution.py:645
  41.6 5.3 %shard_map.154 = (f32[8,16,16,128]{3,2,1,0:T(8,128)S(1)}, f32[14,16,128]{2,1,0:T(8,128)S(1)}, f32[14,16,128]{2,1,0:T(8,128)S(1)}, f32[14,16,128]{2,1,0:T(8,128)S(1)}, f32[14,16,128]{2,1,0:T(8,128)S(1)}) custom-call(f32[8,16,16,128]{3,2,1,0:T(8,128)S(1)} %get-tuple-element.67.refs_0_, f32[16,16,128]{2,1,0:T(8,128)S(1)} %get-tuple-element.61.refs_1_, ...), custom_call_target="tpu_custom_call" | custom-call | bytes 16500000 | tf_op jit(solution)/shard_map/pallas_call | solution.py:300
  47.0 2.0 %collective-permute-start.9 = (f32[2,16,128]{2,1,0:T(8,128)S(1)}, f32[2,16,128]{2,1,0:T(8,128)S(1)}, u32[]{:S(2)}, u32[]{:S(2)}) collective-permute-start(f32[2,16,128]{2,1,0:T(8,128)S(1)} %get-tuple-element.73.here_ref), channel_id=1, source_target_pairs={{0,2},{1,3},{2,4},{3,5},{4,6},{5,7},{6,8},{7,9},{8,10},{9,11},{10,... | collective-permute-start | bytes 49160 | tf_op jit(solution)/shard_map/ppermute | solution.py:639
  49.0 6.1 %collective-permute-start.12 = (f32[16,16,128]{2,1,0:T(8,128)S(1)}, f32[16,16,128]{2,1,0:T(8,128)S(1)}, u32[]{:S(2)}, u32[]{:S(2)}) collective-permute-start(f32[16,16,128]{2,1,0:T(8,128)S(1)} %get-tuple-element.77), channel_id=1, source_target_pairs={{1,2},{3,4},{5,6},{7,8},{9,10},{11,12},{13,14},{15,16},{17,18},{19... | collective-permute-start | bytes 393224 | tf_op jit(solution)/shard_map/ppermute | solution.py:645
  56.3 3.2 %collective-permute-start.14 = (f32[14,16,128]{2,1,0:T(8,128)S(1)}, f32[14,16,128]{2,1,0:T(8,128)S(1)}, u32[]{:S(2)}, u32[]{:S(2)}) collective-permute-start(f32[14,16,128]{2,1,0:T(8,128)S(1)} %get-tuple-element.82), channel_id=1, source_target_pairs={{0,96},{32,0},{64,32},{96,64},{1,97},{33,1},{65,33},{97,65},{2,98}... | collective-permute-start | bytes 344072 | tf_op jit(solution)/shard_map/ppermute | solution.py:639
  59.6 3.0 %collective-permute-done.13.y_low.refs_2_ = f32[14,16,128]{2,1,0:T(8,128)S(1)} collective-permute-done((f32[14,16,128]{2,1,0:T(8,128)S(1)}, f32[14,16,128]{2,1,0:T(8,128)S(1)}, u32[]{:S(2)}, u32[]{:S(2)}) %collective-permute-start.13) | collective-permute-done | bytes 114720 | tf_op jit(solution)/shard_map/ppermute | solution.py:639
  64.2 10.3 %all_to_all.15.block_ref = f32[32,1,128]{2,1,0:T(1,128)S(1)} all-to-all(f32[32,1,128]{2,1,0:T(1,128)S(1)} %get-tuple-element.83), channel_id=1, replica_groups=mesh['grp'=4,'blk'=32] {'blk'}, dimensions={0} | all-to-all | bytes 32768 | tf_op jit(solution)/shard_map/all_to_all | solution.py:730
  75.5 3.2 %collective-permute-start.16 = (f32[3,16,128]{2,1,0:T(8,128)S(1)}, f32[3,16,128]{2,1,0:T(8,128)S(1)}, u32[]{:S(2)}, u32[]{:S(2)}) collective-permute-start(f32[3,16,128]{2,1,0:T(8,128)S(1)} %get-tuple-element.86), channel_id=1, source_target_pairs={{0,96},{32,0},{64,32},{96,64},{1,97},{33,1},{65,33},{97,65},{2,98}... | collective-permute-start | bytes 73736 | tf_op jit(solution)/shard_map/ppermute | solution.py:639
  78.7 1.8 %collective-permute-start.19 = (f32[2,16,128]{2,1,0:T(8,128)S(1)}, f32[2,16,128]{2,1,0:T(8,128)S(1)}, u32[]{:S(2)}, u32[]{:S(2)}) collective-permute-start(f32[2,16,128]{2,1,0:T(8,128)S(1)} %get-tuple-element.91), channel_id=1, source_target_pairs={{1,2},{3,4},{5,6},{7,8},{9,10},{11,12},{13,14},{15,16},{17,18},{19... | collective-permute-start | bytes 49160 | tf_op jit(solution)/shard_map/ppermute | solution.py:645
  81.8 3.5 %collective-permute-done.19.refs_11_ = f32[2,16,128]{2,1,0:T(8,128)S(1)} collective-permute-done((f32[2,16,128]{2,1,0:T(8,128)S(1)}, f32[2,16,128]{2,1,0:T(8,128)S(1)}, u32[]{:S(2)}, u32[]{:S(2)}) %collective-permute-start.19) | collective-permute-done | bytes 16416 | tf_op jit(solution)/shard_map/ppermute | solution.py:645
  85.2 5.3 %shard_map.159 = (f32[8,16,16,128]{3,2,1,0:T(8,128)S(1)}, f32[16,16,128]{2,1,0:T(8,128)S(1)}, f32[16,16,128]{2,1,0:T(8,128)S(1)}, f32[16,16,128]{2,1,0:T(8,128)S(1)}, f32[16,16,128]{2,1,0:T(8,128)S(1)}) custom-call(f32[8,16,16,128]{3,2,1,0:T(8,128)S(1)} %get-tuple-element.80.w_ref.refs_0_, f32[16,16,128]{2,1,0:T(8,128)S(1)} %get-tuple-element.61.refs_1_, ...), custom_call_target="tpu_custom_call" | custom-call | bytes 16500000 | tf_op jit(solution)/shard_map/pallas_call | solution.py:300
  90.6 5.3 %collective-permute-start.21 = (f32[2,16,128]{2,1,0:T(8,128)S(1)}, f32[2,16,128]{2,1,0:T(8,128)S(1)}, u32[]{:S(2)}, u32[]{:S(2)}) collective-permute-start(f32[2,16,128]{2,1,0:T(8,128)S(1)} %get-tuple-element.94.here_ref), channel_id=1, source_target_pairs={{0,30},{1,31},{2,0},{3,1},{4,2},{5,3},{6,4},{7,5},{8,6},{9,7},{10,... | collective-permute-start | bytes 49160 | tf_op jit(solution)/shard_map/ppermute | solution.py:639
  96.0 1.7 %collective-permute-done.20.m2 = f32[2,16,128]{2,1,0:T(8,128)S(1)} collective-permute-done((f32[2,16,128]{2,1,0:T(8,128)S(1)}, f32[2,16,128]{2,1,0:T(8,128)S(1)}, u32[]{:S(2)}, u32[]{:S(2)}) %collective-permute-start.20) | collective-permute-done | bytes 16416 | tf_op jit(solution)/shard_map/ppermute | solution.py:639
  97.7 3.2 %collective-permute-start.25 = (f32[16,16,128]{2,1,0:T(8,128)S(1)}, f32[16,16,128]{2,1,0:T(8,128)S(1)}, u32[]{:S(2)}, u32[]{:S(2)}) collective-permute-start(f32[16,16,128]{2,1,0:T(8,128)S(1)} %get-tuple-element.103), channel_id=1, source_target_pairs={{0,96},{32,0},{64,32},{96,64},{1,97},{33,1},{65,33},{97,65},{2,98}... | collective-permute-start | bytes 393224 | tf_op jit(solution)/shard_map/ppermute | solution.py:639
  100.9 2.9 %collective-permute-done.23.x_b.refs_5_ = f32[18,16,128]{2,1,0:T(8,128)S(1)} collective-permute-done((f32[18,16,128]{2,1,0:T(8,128)S(1)}, f32[18,16,128]{2,1,0:T(8,128)S(1)}, u32[]{:S(2)}, u32[]{:S(2)}) %collective-permute-start.23) | collective-permute-done | bytes 147488 | tf_op jit(solution)/shard_map/ppermute | solution.py:645
  105.2 4.3 %all-to-all-start.2 = ((f32[32,1,128]{2,1,0:T(1,128)}), f32[32,1,128]{2,1,0:T(1,128)S(1)}, u32[]{:S(2)}, u32[]{:S(2)}) async-start(f32[32,1,128]{2,1,0:T(1,128)} %get-tuple-element.100), calls=%async_computation.2 | async-start | bytes 32768 | tf_op jit(solution)/shard_map/all_to_all | solution.py:730
  111.2 5.0 %shard_map.162.u_ref = f32[8,16,16,128]{3,2,1,0:T(8,128)S(1)} custom-call(f32[8,16,16,128]{3,2,1,0:T(8,128)S(1)} %get-tuple-element.101.refs_0_, f32[16,16,128]{2,1,0:T(8,128)S(1)} %get-tuple-element.61.refs_1_, f32[16,16,128]{2,1,0:T(8,128)S(1)} %collective-permute-done.24.refs_2_, f32[16,16,128]{2,1,0:T(8,128)S(1)} %collective-permute-done.25.refs_3_, ...), custom_call_target="tpu_custom_call" | custom-call | bytes 16500000 | tf_op jit(solution)/shard_map/pallas_call | solution.py:300
  (77 shorter events, 20.7 us)
Async XLA Ops:
  2.1 11.3 %collective-permute-start = (f32[17,16,128]{2,1,0:T(8,128)S(1)}, f32[17,16,128]{2,1,0:T(8,128)S(1)}, u32[]{:S(2)}, u32[]{:S(2)}) collective-permute-start(f32[17,16,128]{2,1,0:T(8,128)S(1)} %get-tuple-element.57), channel_id=1, source_target_pairs={{0,32},{32,64},{64,96},{96,0},{1,33},{33,65},{65,97},{97,1},{2,34}... | collective-permute-start | bytes 417800 | tf_op jit(solution)/shard_map/ppermute | solution.py:639
  3.8 9.6 %collective-permute-start.1 = (f32[17,16,128]{2,1,0:T(8,128)S(1)}, f32[17,16,128]{2,1,0:T(8,128)S(1)}, u32[]{:S(2)}, u32[]{:S(2)}) collective-permute-start(f32[17,16,128]{2,1,0:T(8,128)S(1)} %get-tuple-element.58), channel_id=1, source_target_pairs={{0,96},{32,0},{64,32},{96,64},{1,97},{33,1},{65,33},{97,65},{2,98}... | collective-permute-start | bytes 417800 | tf_op jit(solution)/shard_map/ppermute | solution.py:639
  5.4 8.0 %collective-permute-start.2 = (f32[17,16,128]{2,1,0:T(8,128)S(1)}, f32[17,16,128]{2,1,0:T(8,128)S(1)}, u32[]{:S(2)}, u32[]{:S(2)}) collective-permute-start(f32[17,16,128]{2,1,0:T(8,128)S(1)} %get-tuple-element.59), channel_id=1, source_target_pairs={{0,1},{2,3},{4,5},{6,7},{8,9},{10,11},{12,13},{14,15},{16,17},{18,... | collective-permute-start | bytes 417800 | tf_op jit(solution)/shard_map/ppermute | solution.py:645
  5.4 9.2 %collective-permute-start.3 = (f32[17,16,128]{2,1,0:T(8,128)S(1)}, f32[17,16,128]{2,1,0:T(8,128)S(1)}, u32[]{:S(2)}, u32[]{:S(2)}) collective-permute-start(f32[17,16,128]{2,1,0:T(8,128)S(1)} %get-tuple-element.60), channel_id=1, source_target_pairs={{1,2},{3,4},{5,6},{7,8},{9,10},{11,12},{13,14},{15,16},{17,18},{19... | collective-permute-start | bytes 417800 | tf_op jit(solution)/shard_map/ppermute | solution.py:645
  16.1 14.0 %all-to-all-start = ((f32[32,1,128]{2,1,0:T(1,128)}), f32[32,1,128]{2,1,0:T(1,128)S(1)}, u32[]{:S(2)}, u32[]{:S(2)}) async-start(f32[32,1,128]{2,1,0:T(1,128)} %shard_map.150), calls=%async_computation | async-start | bytes 32768 | tf_op jit(solution)/shard_map/all_to_all | solution.py:730
  30.6 11.0 %collective-permute-start.4 = (f32[17,16,128]{2,1,0:T(8,128)S(1)}, f32[17,16,128]{2,1,0:T(8,128)S(1)}, u32[]{:S(2)}, u32[]{:S(2)}) collective-permute-start(f32[17,16,128]{2,1,0:T(8,128)S(1)} %get-tuple-element.65), channel_id=1, source_target_pairs={{0,32},{32,64},{64,96},{96,0},{1,33},{33,65},{65,97},{97,1},{2,34}... | collective-permute-start | bytes 417800 | tf_op jit(solution)/shard_map/ppermute | solution.py:639
  31.0 10.6 %collective-permute-start.5 = (f32[17,16,128]{2,1,0:T(8,128)S(1)}, f32[17,16,128]{2,1,0:T(8,128)S(1)}, u32[]{:S(2)}, u32[]{:S(2)}) collective-permute-start(f32[17,16,128]{2,1,0:T(8,128)S(1)} %get-tuple-element.66), channel_id=1, source_target_pairs={{0,96},{32,0},{64,32},{96,64},{1,97},{33,1},{65,33},{97,65},{2,98}... | collective-permute-start | bytes 417800 | tf_op jit(solution)/shard_map/ppermute | solution.py:639
  33.9 7.7 %collective-permute-start.8 = (f32[16,16,128]{2,1,0:T(8,128)S(1)}, f32[16,16,128]{2,1,0:T(8,128)S(1)}, u32[]{:S(2)}, u32[]{:S(2)}) collective-permute-start(f32[16,16,128]{2,1,0:T(8,128)S(1)} %get-tuple-element.69), channel_id=1, source_target_pairs={{1,2},{3,4},{5,6},{7,8},{9,10},{11,12},{13,14},{15,16},{17,18},{19... | collective-permute-start | bytes 393224 | tf_op jit(solution)/shard_map/ppermute | solution.py:645
  37.2 9.7 %collective-permute-start.6 = (f32[1,16,128]{2,1,0:T(8,128)S(1)}, f32[1,16,128]{2,1,0:T(8,128)S(1)}, u32[]{:S(2)}, u32[]{:S(2)}) collective-permute-start(f32[1,16,128]{2,1,0:T(8,128)S(1)} %get-tuple-element.64.own), channel_id=1, source_target_pairs={{0,64},{32,96},{64,0},{96,32},{1,65},{33,97},{65,1},{97,33},{2,66}... | collective-permute-start | bytes 24584 | tf_op jit(solution)/shard_map/ppermute | solution.py:639
  46.9 8.2 %collective-permute-start.10 = (f32[2,16,128]{2,1,0:T(8,128)S(1)}, f32[2,16,128]{2,1,0:T(8,128)S(1)}, u32[]{:S(2)}, u32[]{:S(2)}) collective-permute-start(f32[2,16,128]{2,1,0:T(8,128)S(1)} %get-tuple-element.73.here_ref), channel_id=1, source_target_pairs={{0,30},{1,31},{2,0},{3,1},{4,2},{5,3},{6,4},{7,5},{8,6},{9,7},{10,... | collective-permute-start | bytes 49160 | tf_op jit(solution)/shard_map/ppermute | solution.py:639
  47.0 8.1 %collective-permute-start.9 = (f32[2,16,128]{2,1,0:T(8,128)S(1)}, f32[2,16,128]{2,1,0:T(8,128)S(1)}, u32[]{:S(2)}, u32[]{:S(2)}) collective-permute-start(f32[2,16,128]{2,1,0:T(8,128)S(1)} %get-tuple-element.73.here_ref), channel_id=1, source_target_pairs={{0,2},{1,3},{2,4},{3,5},{4,6},{5,7},{6,8},{7,9},{8,10},{9,11},{10,... | collective-permute-start | bytes 49160 | tf_op jit(solution)/shard_map/ppermute | solution.py:639
  49.0 13.6 %collective-permute-start.12 = (f32[16,16,128]{2,1,0:T(8,128)S(1)}, f32[16,16,128]{2,1,0:T(8,128)S(1)}, u32[]{:S(2)}, u32[]{:S(2)}) collective-permute-start(f32[16,16,128]{2,1,0:T(8,128)S(1)} %get-tuple-element.77), channel_id=1, source_target_pairs={{1,2},{3,4},{5,6},{7,8},{9,10},{11,12},{13,14},{15,16},{17,18},{19... | collective-permute-start | bytes 393224 | tf_op jit(solution)/shard_map/ppermute | solution.py:645
  55.1 7.5 %collective-permute-start.11 = (f32[16,16,128]{2,1,0:T(8,128)S(1)}, f32[16,16,128]{2,1,0:T(8,128)S(1)}, u32[]{:S(2)}, u32[]{:S(2)}) collective-permute-start(f32[16,16,128]{2,1,0:T(8,128)S(1)} %get-tuple-element.76), channel_id=1, source_target_pairs={{0,1},{2,3},{4,5},{6,7},{8,9},{10,11},{12,13},{14,15},{16,17},{18,... | collective-permute-start | bytes 393224 | tf_op jit(solution)/shard_map/ppermute | solution.py:645
  56.3 6.3 %collective-permute-start.13 = (f32[14,16,128]{2,1,0:T(8,128)S(1)}, f32[14,16,128]{2,1,0:T(8,128)S(1)}, u32[]{:S(2)}, u32[]{:S(2)}) collective-permute-start(f32[14,16,128]{2,1,0:T(8,128)S(1)} %get-tuple-element.81), channel_id=1, source_target_pairs={{0,32},{32,64},{64,96},{96,0},{1,33},{33,65},{65,97},{97,1},{2,34}... | collective-permute-start | bytes 344072 | tf_op jit(solution)/shard_map/ppermute | solution.py:639
  75.4 9.8 %collective-permute-start.15 = (f32[3,16,128]{2,1,0:T(8,128)S(1)}, f32[3,16,128]{2,1,0:T(8,128)S(1)}, u32[]{:S(2)}, u32[]{:S(2)}) collective-permute-start(f32[3,16,128]{2,1,0:T(8,128)S(1)} %get-tuple-element.85), channel_id=1, source_target_pairs={{0,32},{32,64},{64,96},{96,0},{1,33},{33,65},{65,97},{97,1},{2,34}... | collective-permute-start | bytes 73736 | tf_op jit(solution)/shard_map/ppermute | solution.py:639
  75.5 9.7 %collective-permute-start.16 = (f32[3,16,128]{2,1,0:T(8,128)S(1)}, f32[3,16,128]{2,1,0:T(8,128)S(1)}, u32[]{:S(2)}, u32[]{:S(2)}) collective-permute-start(f32[3,16,128]{2,1,0:T(8,128)S(1)} %get-tuple-element.86), channel_id=1, source_target_pairs={{0,96},{32,0},{64,32},{96,64},{1,97},{33,1},{65,33},{97,65},{2,98}... | collective-permute-start | bytes 73736 | tf_op jit(solution)/shard_map/ppermute | solution.py:639
  78.7 6.5 %collective-permute-start.19 = (f32[2,16,128]{2,1,0:T(8,128)S(1)}, f32[2,16,128]{2,1,0:T(8,128)S(1)}, u32[]{:S(2)}, u32[]{:S(2)}) collective-permute-start(f32[2,16,128]{2,1,0:T(8,128)S(1)} %get-tuple-element.91), channel_id=1, source_target_pairs={{1,2},{3,4},{5,6},{7,8},{9,10},{11,12},{13,14},{15,16},{17,18},{19... | collective-permute-start | bytes 49160 | tf_op jit(solution)/shard_map/ppermute | solution.py:645
  80.6 10.0 %collective-permute-start.17 = (f32[1,16,128]{2,1,0:T(8,128)S(1)}, f32[1,16,128]{2,1,0:T(8,128)S(1)}, u32[]{:S(2)}, u32[]{:S(2)}) collective-permute-start(f32[1,16,128]{2,1,0:T(8,128)S(1)} %get-tuple-element.84.own), channel_id=1, source_target_pairs={{0,64},{32,96},{64,0},{96,32},{1,65},{33,97},{65,1},{97,33},{2,66}... | collective-permute-start | bytes 24584 | tf_op jit(solution)/shard_map/ppermute | solution.py:639
  90.6 7.1 %collective-permute-start.20 = (f32[2,16,128]{2,1,0:T(8,128)S(1)}, f32[2,16,128]{2,1,0:T(8,128)S(1)}, u32[]{:S(2)}, u32[]{:S(2)}) collective-permute-start(f32[2,16,128]{2,1,0:T(8,128)S(1)} %get-tuple-element.94.here_ref), channel_id=1, source_target_pairs={{0,2},{1,3},{2,4},{3,5},{4,6},{5,7},{6,8},{7,9},{8,10},{9,11},{10,... | collective-permute-start | bytes 49160 | tf_op jit(solution)/shard_map/ppermute | solution.py:639
  90.6 7.0 %collective-permute-start.21 = (f32[2,16,128]{2,1,0:T(8,128)S(1)}, f32[2,16,128]{2,1,0:T(8,128)S(1)}, u32[]{:S(2)}, u32[]{:S(2)}) collective-permute-start(f32[2,16,128]{2,1,0:T(8,128)S(1)} %get-tuple-element.94.here_ref), channel_id=1, source_target_pairs={{0,30},{1,31},{2,0},{3,1},{4,2},{5,3},{6,4},{7,5},{8,6},{9,7},{10,... | collective-permute-start | bytes 49160 | tf_op jit(solution)/shard_map/ppermute | solution.py:639
  96.0 7.9 %collective-permute-start.23 = (f32[18,16,128]{2,1,0:T(8,128)S(1)}, f32[18,16,128]{2,1,0:T(8,128)S(1)}, u32[]{:S(2)}, u32[]{:S(2)}) collective-permute-start(f32[18,16,128]{2,1,0:T(8,128)S(1)} %get-tuple-element.98), channel_id=1, source_target_pairs={{1,2},{3,4},{5,6},{7,8},{9,10},{11,12},{13,14},{15,16},{17,18},{19... | collective-permute-start | bytes 442376 | tf_op jit(solution)/shard_map/ppermute | solution.py:645
  97.7 13.4 %collective-permute-start.24 = (f32[16,16,128]{2,1,0:T(8,128)S(1)}, f32[16,16,128]{2,1,0:T(8,128)S(1)}, u32[]{:S(2)}, u32[]{:S(2)}) collective-permute-start(f32[16,16,128]{2,1,0:T(8,128)S(1)} %get-tuple-element.102), channel_id=1, source_target_pairs={{0,32},{32,64},{64,96},{96,0},{1,33},{33,65},{65,97},{97,1},{2,34}... | collective-permute-start | bytes 393224 | tf_op jit(solution)/shard_map/ppermute | solution.py:639
  97.7 13.4 %collective-permute-start.25 = (f32[16,16,128]{2,1,0:T(8,128)S(1)}, f32[16,16,128]{2,1,0:T(8,128)S(1)}, u32[]{:S(2)}, u32[]{:S(2)}) collective-permute-start(f32[16,16,128]{2,1,0:T(8,128)S(1)} %get-tuple-element.103), channel_id=1, source_target_pairs={{0,96},{32,0},{64,32},{96,64},{1,97},{33,1},{65,33},{97,65},{2,98}... | collective-permute-start | bytes 393224 | tf_op jit(solution)/shard_map/ppermute | solution.py:639
  105.2 11.4 %all-to-all-start.2 = ((f32[32,1,128]{2,1,0:T(1,128)}), f32[32,1,128]{2,1,0:T(1,128)S(1)}, u32[]{:S(2)}, u32[]{:S(2)}) async-start(f32[32,1,128]{2,1,0:T(1,128)} %get-tuple-element.100), calls=%async_computation.2 | async-start | bytes 32768 | tf_op jit(solution)/shard_map/all_to_all | solution.py:730
  (12 other events, 54.5 us)

commit v5 on v4

--- a/solution.py
+++ b/solution.py
@@ -42,8 +42,10 @@
 
 
 def half_slope(before, centre, after, half_limiter):
-    forward = after - centre
-    backward = centre - before
+    return limited(after - centre, centre - before, half_limiter)
+
+
+def limited(forward, backward, half_limiter):
     low = jnp.minimum(backward, 0.0)
     high = jnp.maximum(backward, 0.0)
     return half_limiter * jnp.minimum(jnp.maximum(forward, low), high)
@@ -127,7 +129,7 @@
         for k in range(4):
             refs[0][k] = lims[k]
         refs = refs[1:]
-    ext, lim_ext, turned, lim_turned, across, lx, hx = refs
+    ext, lim_ext, turned, lim_turned, across, lx, hx, fx = refs
     even = core() == 0
     place_a = jnp.where(even, CX + 2, 0)
     place_b = CX + 2 - place_a
@@ -167,6 +169,7 @@
             slope = half_slope(q, r, s, lim[1])
             right.append(r - slope)
             lx[d, f] = r + slope
+            fx[d, f] = s - r
         for f, value in enumerate(face_flux(left, right, d)):
             hx[d, f] = value
 
@@ -175,7 +178,9 @@
         right = []
         for f in range(8):
             after = w[f, i + 3]
-            slope = half_slope(w[f, i + 2], after, w[f, i + 4], lim[i + 2])
+            forward = w[f, i + 4] - after
+            slope = limited(forward, fx[d, f], lim[i + 2])
+            fx[d, f] = forward
             right.append(after - slope)
             lx[d, f] = after + slope
         flux = face_flux(left, right, d)
@@ -283,6 +288,7 @@
         pltpu.VMEM((8, CY + 4, CX, CZ), F32),
         pltpu.VMEM((CY + 2, CX, CZ), F32),
         pltpu.VMEM((8, CX, CY, CZ), F32),
+        pltpu.VMEM((2, 8, CY, CZ), F32),
         pltpu.VMEM((2, 8, CY, CZ), F32),
         pltpu.VMEM((2, 8, CY, CZ), F32),
     ]

time: 119 us -> 119 us (level)
  no operation moved by 1% of the time
where the time goes in v5:
time: 119 us; the launch traced here: 118 us
  starting transfers between devices  55.6 us (47%)
  Pallas kernels  32.1 us (27%)
  waiting for transfers between devices  16.3 us (14%)
  blocking collectives  10.3 us (9%)
  local copies, waits for them, and re-layouts  2.41 us (2%)
    ppermute x16, starting transfers between devices, shifted(): lax.ppermute(value, axis, [(i, (i + by) % count) for i in range(count)])  25.8 us
    pallas_call x4, Pallas kernels, substep(): return kernel_call(body, outs, 5.0, scratch)(*args)  20.7 us
    ppermute x10, starting transfers between devices, swapped(): return lax.ppermute(value, 'blk', pairs + [(j, i) for i, j in pairs])  18.8 us
    all_to_all x2, starting transfers between devices, exchange(): lax.all_to_all(blocks, 'blk', split_axis=0, concat_axis=0, tiled=True)  11 us
    all_to_all x1, blocking collectives, exchange(): lax.all_to_all(blocks, 'blk', split_axis=0, concat_axis=0, tiled=True)  10.3 us
    ppermute x10, waiting for transfers between devices, swapped(): return lax.ppermute(value, 'blk', pairs + [(j, i) for i, j in pairs])  9.09 us
    ppermute x16, waiting for transfers between devices, shifted(): lax.ppermute(value, axis, [(i, (i + by) % count) for i in range(count)])  4.77 us
    all_to_all x2, waiting for transfers between devices, exchange(): lax.all_to_all(blocks, 'blk', split_axis=0, concat_axis=0, tiled=True)  2.47 us
  transfers between devices with their start and end apart: 28, of which 8 were waited for; matrix products, arithmetic and copies ran while one was open for 0% of the time, Pallas kernels for 21%

profile of v5, /device:TPU:0, one launch (start us, length us, event | category | flops | bytes accessed | tf_op | source)
XLA Modules:
  0.0 118.0 jit_solution(13554712882989328659)
XLA Ops:
  2.1 1.7 %collective-permute-start = (f32[17,16,128]{2,1,0:T(8,128)S(1)}, f32[17,16,128]{2,1,0:T(8,128)S(1)}, u32[]{:S(2)}, u32[]{:S(2)}) collective-permute-start(f32[17,16,128]{2,1,0:T(8,128)S(1)} %get-tuple-element.57), channel_id=1, source_target_pairs={{0,32},{32,64},{64,96},{96,0},{1,33},{33,65},{65,97},{97,1},{2,34}... | collective-permute-start | bytes 417800 | tf_op jit(solution)/shard_map/ppermute | solution.py:645
  3.8 1.6 %collective-permute-start.1 = (f32[17,16,128]{2,1,0:T(8,128)S(1)}, f32[17,16,128]{2,1,0:T(8,128)S(1)}, u32[]{:S(2)}, u32[]{:S(2)}) collective-permute-start(f32[17,16,128]{2,1,0:T(8,128)S(1)} %get-tuple-element.58), channel_id=1, source_target_pairs={{0,96},{32,0},{64,32},{96,64},{1,97},{33,1},{65,33},{97,65},{2,98}... | collective-permute-start | bytes 417800 | tf_op jit(solution)/shard_map/ppermute | solution.py:645
  5.4 6.4 %collective-permute-start.3 = (f32[17,16,128]{2,1,0:T(8,128)S(1)}, f32[17,16,128]{2,1,0:T(8,128)S(1)}, u32[]{:S(2)}, u32[]{:S(2)}) collective-permute-start(f32[17,16,128]{2,1,0:T(8,128)S(1)} %get-tuple-element.60), channel_id=1, source_target_pairs={{1,2},{3,4},{5,6},{7,8},{9,10},{11,12},{13,14},{15,16},{17,18},{19... | collective-permute-start | bytes 417800 | tf_op jit(solution)/shard_map/ppermute | solution.py:651
  16.1 6.7 %all-to-all-start = ((f32[32,1,128]{2,1,0:T(1,128)}), f32[32,1,128]{2,1,0:T(1,128)S(1)}, u32[]{:S(2)}, u32[]{:S(2)}) async-start(f32[32,1,128]{2,1,0:T(1,128)} %shard_map.150), calls=%async_computation | async-start | bytes 32768 | tf_op jit(solution)/shard_map/all_to_all | solution.py:736
  22.8 5.2 %shard_map.151 = (f32[8,16,16,128]{3,2,1,0:T(8,128)S(1)}, f32[16,16,128]{2,1,0:T(8,128)S(1)}, f32[16,16,128]{2,1,0:T(8,128)S(1)}, f32[16,16,128]{2,1,0:T(8,128)S...) custom-call(f32[8,16,16,128]{3,2,1,0:T(8,128)S(1)} %get-tuple-element.56.w_ref.refs_0_, ...), custom_call_target="tpu_custom_call" | custom-call | bytes 16500000 | tf_op jit(solution)/shard_map/pallas_call | solution.py:306
  28.0 2.0 %all-to-all-done.block_ref = f32[32,1,128]{2,1,0:T(1,128)S(1)} async-done(((f32[32,1,128]{2,1,0:T(1,128)}), f32[32,1,128]{2,1,0:T(1,128)S(1)}, u32[]{:S(2)}, u32[]{:S(2)}) %all-to-all-start) | async-done | bytes 16416 | tf_op jit(solution)/shard_map/all_to_all | solution.py:736
  31.0 2.9 %collective-permute-start.5 = (f32[17,16,128]{2,1,0:T(8,128)S(1)}, f32[17,16,128]{2,1,0:T(8,128)S(1)}, u32[]{:S(2)}, u32[]{:S(2)}) collective-permute-start(f32[17,16,128]{2,1,0:T(8,128)S(1)} %get-tuple-element.66), channel_id=1, source_target_pairs={{0,96},{32,0},{64,32},{96,64},{1,97},{33,1},{65,33},{97,65},{2,98}... | collective-permute-start | bytes 417800 | tf_op jit(solution)/shard_map/ppermute | solution.py:645
  33.9 3.3 %collective-permute-start.8 = (f32[16,16,128]{2,1,0:T(8,128)S(1)}, f32[16,16,128]{2,1,0:T(8,128)S(1)}, u32[]{:S(2)}, u32[]{:S(2)}) collective-permute-start(f32[16,16,128]{2,1,0:T(8,128)S(1)} %get-tuple-element.69), channel_id=1, source_target_pairs={{1,2},{3,4},{5,6},{7,8},{9,10},{11,12},{13,14},{15,16},{17,18},{19... | collective-permute-start | bytes 393224 | tf_op jit(solution)/shard_map/ppermute | solution.py:651
  41.6 5.2 %shard_map.154 = (f32[8,16,16,128]{3,2,1,0:T(8,128)S(1)}, f32[14,16,128]{2,1,0:T(8,128)S(1)}, f32[14,16,128]{2,1,0:T(8,128)S(1)}, f32[14,16,128]{2,1,0:T(8,128)S(1)}, f32[14,16,128]{2,1,0:T(8,128)S(1)}) custom-call(f32[8,16,16,128]{3,2,1,0:T(8,128)S(1)} %get-tuple-element.67.refs_0_, f32[16,16,128]{2,1,0:T(8,128)S(1)} %get-tuple-element.61.refs_1_, ...), custom_call_target="tpu_custom_call" | custom-call | bytes 16500000 | tf_op jit(solution)/shard_map/pallas_call | solution.py:306
  46.9 2.0 %collective-permute-start.9 = (f32[2,16,128]{2,1,0:T(8,128)S(1)}, f32[2,16,128]{2,1,0:T(8,128)S(1)}, u32[]{:S(2)}, u32[]{:S(2)}) collective-permute-start(f32[2,16,128]{2,1,0:T(8,128)S(1)} %get-tuple-element.73.here_ref), channel_id=1, source_target_pairs={{0,2},{1,3},{2,4},{3,5},{4,6},{5,7},{6,8},{7,9},{8,10},{9,11},{10,... | collective-permute-start | bytes 49160 | tf_op jit(solution)/shard_map/ppermute | solution.py:645
  49.0 6.0 %collective-permute-start.12 = (f32[16,16,128]{2,1,0:T(8,128)S(1)}, f32[16,16,128]{2,1,0:T(8,128)S(1)}, u32[]{:S(2)}, u32[]{:S(2)}) collective-permute-start(f32[16,16,128]{2,1,0:T(8,128)S(1)} %get-tuple-element.77), channel_id=1, source_target_pairs={{1,2},{3,4},{5,6},{7,8},{9,10},{11,12},{13,14},{15,16},{17,18},{19... | collective-permute-start | bytes 393224 | tf_op jit(solution)/shard_map/ppermute | solution.py:651
  56.2 3.2 %collective-permute-start.14 = (f32[14,16,128]{2,1,0:T(8,128)S(1)}, f32[14,16,128]{2,1,0:T(8,128)S(1)}, u32[]{:S(2)}, u32[]{:S(2)}) collective-permute-start(f32[14,16,128]{2,1,0:T(8,128)S(1)} %get-tuple-element.82), channel_id=1, source_target_pairs={{0,96},{32,0},{64,32},{96,64},{1,97},{33,1},{65,33},{97,65},{2,98}... | collective-permute-start | bytes 344072 | tf_op jit(solution)/shard_map/ppermute | solution.py:645
  59.5 3.0 %collective-permute-done.13.y_low.refs_2_ = f32[14,16,128]{2,1,0:T(8,128)S(1)} collective-permute-done((f32[14,16,128]{2,1,0:T(8,128)S(1)}, f32[14,16,128]{2,1,0:T(8,128)S(1)}, u32[]{:S(2)}, u32[]{:S(2)}) %collective-permute-start.13) | collective-permute-done | bytes 114720 | tf_op jit(solution)/shard_map/ppermute | solution.py:645
  64.1 10.3 %all_to_all.15.block_ref = f32[32,1,128]{2,1,0:T(1,128)S(1)} all-to-all(f32[32,1,128]{2,1,0:T(1,128)S(1)} %get-tuple-element.83), channel_id=1, replica_groups=mesh['grp'=4,'blk'=32] {'blk'}, dimensions={0} | all-to-all | bytes 32768 | tf_op jit(solution)/shard_map/all_to_all | solution.py:736
  75.4 3.2 %collective-permute-start.16 = (f32[3,16,128]{2,1,0:T(8,128)S(1)}, f32[3,16,128]{2,1,0:T(8,128)S(1)}, u32[]{:S(2)}, u32[]{:S(2)}) collective-permute-start(f32[3,16,128]{2,1,0:T(8,128)S(1)} %get-tuple-element.86), channel_id=1, source_target_pairs={{0,96},{32,0},{64,32},{96,64},{1,97},{33,1},{65,33},{97,65},{2,98}... | collective-permute-start | bytes 73736 | tf_op jit(solution)/shard_map/ppermute | solution.py:645
  78.6 1.8 %collective-permute-start.19 = (f32[2,16,128]{2,1,0:T(8,128)S(1)}, f32[2,16,128]{2,1,0:T(8,128)S(1)}, u32[]{:S(2)}, u32[]{:S(2)}) collective-permute-start(f32[2,16,128]{2,1,0:T(8,128)S(1)} %get-tuple-element.91), channel_id=1, source_target_pairs={{1,2},{3,4},{5,6},{7,8},{9,10},{11,12},{13,14},{15,16},{17,18},{19... | collective-permute-start | bytes 49160 | tf_op jit(solution)/shard_map/ppermute | solution.py:651
  81.7 3.5 %collective-permute-done.19.refs_11_ = f32[2,16,128]{2,1,0:T(8,128)S(1)} collective-permute-done((f32[2,16,128]{2,1,0:T(8,128)S(1)}, f32[2,16,128]{2,1,0:T(8,128)S(1)}, u32[]{:S(2)}, u32[]{:S(2)}) %collective-permute-start.19) | collective-permute-done | bytes 16416 | tf_op jit(solution)/shard_map/ppermute | solution.py:651
  85.1 5.2 %shard_map.159 = (f32[8,16,16,128]{3,2,1,0:T(8,128)S(1)}, f32[16,16,128]{2,1,0:T(8,128)S(1)}, f32[16,16,128]{2,1,0:T(8,128)S(1)}, f32[16,16,128]{2,1,0:T(8,128)S(1)}, f32[16,16,128]{2,1,0:T(8,128)S(1)}) custom-call(f32[8,16,16,128]{3,2,1,0:T(8,128)S(1)} %get-tuple-element.80.w_ref.refs_0_, f32[16,16,128]{2,1,0:T(8,128)S(1)} %get-tuple-element.61.refs_1_, ...), custom_call_target="tpu_custom_call" | custom-call | bytes 16500000 | tf_op jit(solution)/shard_map/pallas_call | solution.py:306
  90.5 5.3 %collective-permute-start.21 = (f32[2,16,128]{2,1,0:T(8,128)S(1)}, f32[2,16,128]{2,1,0:T(8,128)S(1)}, u32[]{:S(2)}, u32[]{:S(2)}) collective-permute-start(f32[2,16,128]{2,1,0:T(8,128)S(1)} %get-tuple-element.94.here_ref), channel_id=1, source_target_pairs={{0,30},{1,31},{2,0},{3,1},{4,2},{5,3},{6,4},{7,5},{8,6},{9,7},{10,... | collective-permute-start | bytes 49160 | tf_op jit(solution)/shard_map/ppermute | solution.py:645
  95.8 1.7 %collective-permute-done.20.m2 = f32[2,16,128]{2,1,0:T(8,128)S(1)} collective-permute-done((f32[2,16,128]{2,1,0:T(8,128)S(1)}, f32[2,16,128]{2,1,0:T(8,128)S(1)}, u32[]{:S(2)}, u32[]{:S(2)}) %collective-permute-start.20) | collective-permute-done | bytes 16416 | tf_op jit(solution)/shard_map/ppermute | solution.py:645
  97.6 3.2 %collective-permute-start.25 = (f32[16,16,128]{2,1,0:T(8,128)S(1)}, f32[16,16,128]{2,1,0:T(8,128)S(1)}, u32[]{:S(2)}, u32[]{:S(2)}) collective-permute-start(f32[16,16,128]{2,1,0:T(8,128)S(1)} %get-tuple-element.103), channel_id=1, source_target_pairs={{0,96},{32,0},{64,32},{96,64},{1,97},{33,1},{65,33},{97,65},{2,98}... | collective-permute-start | bytes 393224 | tf_op jit(solution)/shard_map/ppermute | solution.py:645
  100.8 2.9 %collective-permute-done.23.x_b.refs_5_ = f32[18,16,128]{2,1,0:T(8,128)S(1)} collective-permute-done((f32[18,16,128]{2,1,0:T(8,128)S(1)}, f32[18,16,128]{2,1,0:T(8,128)S(1)}, u32[]{:S(2)}, u32[]{:S(2)}) %collective-permute-start.23) | collective-permute-done | bytes 147488 | tf_op jit(solution)/shard_map/ppermute | solution.py:651
  105.1 4.3 %all-to-all-start.2 = ((f32[32,1,128]{2,1,0:T(1,128)}), f32[32,1,128]{2,1,0:T(1,128)S(1)}, u32[]{:S(2)}, u32[]{:S(2)}) async-start(f32[32,1,128]{2,1,0:T(1,128)} %get-tuple-element.100), calls=%async_computation.2 | async-start | bytes 32768 | tf_op jit(solution)/shard_map/all_to_all | solution.py:736
  111.0 5.0 %shard_map.162.u_ref = f32[8,16,16,128]{3,2,1,0:T(8,128)S(1)} custom-call(f32[8,16,16,128]{3,2,1,0:T(8,128)S(1)} %get-tuple-element.101.refs_0_, f32[16,16,128]{2,1,0:T(8,128)S(1)} %get-tuple-element.61.refs_1_, f32[16,16,128]{2,1,0:T(8,128)S(1)} %collective-permute-done.24.refs_2_, f32[16,16,128]{2,1,0:T(8,128)S(1)} %collective-permute-done.25.refs_3_, ...), custom_call_target="tpu_custom_call" | custom-call | bytes 16500000 | tf_op jit(solution)/shard_map/pallas_call | solution.py:306
  (77 shorter events, 20.8 us)
Async XLA Ops:
  2.1 11.3 %collective-permute-start = (f32[17,16,128]{2,1,0:T(8,128)S(1)}, f32[17,16,128]{2,1,0:T(8,128)S(1)}, u32[]{:S(2)}, u32[]{:S(2)}) collective-permute-start(f32[17,16,128]{2,1,0:T(8,128)S(1)} %get-tuple-element.57), channel_id=1, source_target_pairs={{0,32},{32,64},{64,96},{96,0},{1,33},{33,65},{65,97},{97,1},{2,34}... | collective-permute-start | bytes 417800 | tf_op jit(solution)/shard_map/ppermute | solution.py:645
  3.8 9.6 %collective-permute-start.1 = (f32[17,16,128]{2,1,0:T(8,128)S(1)}, f32[17,16,128]{2,1,0:T(8,128)S(1)}, u32[]{:S(2)}, u32[]{:S(2)}) collective-permute-start(f32[17,16,128]{2,1,0:T(8,128)S(1)} %get-tuple-element.58), channel_id=1, source_target_pairs={{0,96},{32,0},{64,32},{96,64},{1,97},{33,1},{65,33},{97,65},{2,98}... | collective-permute-start | bytes 417800 | tf_op jit(solution)/shard_map/ppermute | solution.py:645
  5.4 8.0 %collective-permute-start.2 = (f32[17,16,128]{2,1,0:T(8,128)S(1)}, f32[17,16,128]{2,1,0:T(8,128)S(1)}, u32[]{:S(2)}, u32[]{:S(2)}) collective-permute-start(f32[17,16,128]{2,1,0:T(8,128)S(1)} %get-tuple-element.59), channel_id=1, source_target_pairs={{0,1},{2,3},{4,5},{6,7},{8,9},{10,11},{12,13},{14,15},{16,17},{18,... | collective-permute-start | bytes 417800 | tf_op jit(solution)/shard_map/ppermute | solution.py:651
  5.4 9.2 %collective-permute-start.3 = (f32[17,16,128]{2,1,0:T(8,128)S(1)}, f32[17,16,128]{2,1,0:T(8,128)S(1)}, u32[]{:S(2)}, u32[]{:S(2)}) collective-permute-start(f32[17,16,128]{2,1,0:T(8,128)S(1)} %get-tuple-element.60), channel_id=1, source_target_pairs={{1,2},{3,4},{5,6},{7,8},{9,10},{11,12},{13,14},{15,16},{17,18},{19... | collective-permute-start | bytes 417800 | tf_op jit(solution)/shard_map/ppermute | solution.py:651
  16.1 14.0 %all-to-all-start = ((f32[32,1,128]{2,1,0:T(1,128)}), f32[32,1,128]{2,1,0:T(1,128)S(1)}, u32[]{:S(2)}, u32[]{:S(2)}) async-start(f32[32,1,128]{2,1,0:T(1,128)} %shard_map.150), calls=%async_computation | async-start | bytes 32768 | tf_op jit(solution)/shard_map/all_to_all | solution.py:736
  30.6 11.0 %collective-permute-start.4 = (f32[17,16,128]{2,1,0:T(8,128)S(1)}, f32[17,16,128]{2,1,0:T(8,128)S(1)}, u32[]{:S(2)}, u32[]{:S(2)}) collective-permute-start(f32[17,16,128]{2,1,0:T(8,128)S(1)} %get-tuple-element.65), channel_id=1, source_target_pairs={{0,32},{32,64},{64,96},{96,0},{1,33},{33,65},{65,97},{97,1},{2,34}... | collective-permute-start | bytes 417800 | tf_op jit(solution)/shard_map/ppermute | solution.py:645
  31.0 10.6 %collective-permute-start.5 = (f32[17,16,128]{2,1,0:T(8,128)S(1)}, f32[17,16,128]{2,1,0:T(8,128)S(1)}, u32[]{:S(2)}, u32[]{:S(2)}) collective-permute-start(f32[17,16,128]{2,1,0:T(8,128)S(1)} %get-tuple-element.66), channel_id=1, source_target_pairs={{0,96},{32,0},{64,32},{96,64},{1,97},{33,1},{65,33},{97,65},{2,98}... | collective-permute-start | bytes 417800 | tf_op jit(solution)/shard_map/ppermute | solution.py:645
  33.9 7.7 %collective-permute-start.8 = (f32[16,16,128]{2,1,0:T(8,128)S(1)}, f32[16,16,128]{2,1,0:T(8,128)S(1)}, u32[]{:S(2)}, u32[]{:S(2)}) collective-permute-start(f32[16,16,128]{2,1,0:T(8,128)S(1)} %get-tuple-element.69), channel_id=1, source_target_pairs={{1,2},{3,4},{5,6},{7,8},{9,10},{11,12},{13,14},{15,16},{17,18},{19... | collective-permute-start | bytes 393224 | tf_op jit(solution)/shard_map/ppermute | solution.py:651
  37.1 9.7 %collective-permute-start.6 = (f32[1,16,128]{2,1,0:T(8,128)S(1)}, f32[1,16,128]{2,1,0:T(8,128)S(1)}, u32[]{:S(2)}, u32[]{:S(2)}) collective-permute-start(f32[1,16,128]{2,1,0:T(8,128)S(1)} %get-tuple-element.64.own), channel_id=1, source_target_pairs={{0,64},{32,96},{64,0},{96,32},{1,65},{33,97},{65,1},{97,33},{2,66}... | collective-permute-start | bytes 24584 | tf_op jit(solution)/shard_map/ppermute | solution.py:645
  46.9 8.1 %collective-permute-start.10 = (f32[2,16,128]{2,1,0:T(8,128)S(1)}, f32[2,16,128]{2,1,0:T(8,128)S(1)}, u32[]{:S(2)}, u32[]{:S(2)}) collective-permute-start(f32[2,16,128]{2,1,0:T(8,128)S(1)} %get-tuple-element.73.here_ref), channel_id=1, source_target_pairs={{0,30},{1,31},{2,0},{3,1},{4,2},{5,3},{6,4},{7,5},{8,6},{9,7},{10,... | collective-permute-start | bytes 49160 | tf_op jit(solution)/shard_map/ppermute | solution.py:645
  46.9 8.1 %collective-permute-start.9 = (f32[2,16,128]{2,1,0:T(8,128)S(1)}, f32[2,16,128]{2,1,0:T(8,128)S(1)}, u32[]{:S(2)}, u32[]{:S(2)}) collective-permute-start(f32[2,16,128]{2,1,0:T(8,128)S(1)} %get-tuple-element.73.here_ref), channel_id=1, source_target_pairs={{0,2},{1,3},{2,4},{3,5},{4,6},{5,7},{6,8},{7,9},{8,10},{9,11},{10,... | collective-permute-start | bytes 49160 | tf_op jit(solution)/shard_map/ppermute | solution.py:645
  49.0 13.6 %collective-permute-start.12 = (f32[16,16,128]{2,1,0:T(8,128)S(1)}, f32[16,16,128]{2,1,0:T(8,128)S(1)}, u32[]{:S(2)}, u32[]{:S(2)}) collective-permute-start(f32[16,16,128]{2,1,0:T(8,128)S(1)} %get-tuple-element.77), channel_id=1, source_target_pairs={{1,2},{3,4},{5,6},{7,8},{9,10},{11,12},{13,14},{15,16},{17,18},{19... | collective-permute-start | bytes 393224 | tf_op jit(solution)/shard_map/ppermute | solution.py:651
  55.0 7.5 %collective-permute-start.11 = (f32[16,16,128]{2,1,0:T(8,128)S(1)}, f32[16,16,128]{2,1,0:T(8,128)S(1)}, u32[]{:S(2)}, u32[]{:S(2)}) collective-permute-start(f32[16,16,128]{2,1,0:T(8,128)S(1)} %get-tuple-element.76), channel_id=1, source_target_pairs={{0,1},{2,3},{4,5},{6,7},{8,9},{10,11},{12,13},{14,15},{16,17},{18,... | collective-permute-start | bytes 393224 | tf_op jit(solution)/shard_map/ppermute | solution.py:651
  56.2 6.3 %collective-permute-start.13 = (f32[14,16,128]{2,1,0:T(8,128)S(1)}, f32[14,16,128]{2,1,0:T(8,128)S(1)}, u32[]{:S(2)}, u32[]{:S(2)}) collective-permute-start(f32[14,16,128]{2,1,0:T(8,128)S(1)} %get-tuple-element.81), channel_id=1, source_target_pairs={{0,32},{32,64},{64,96},{96,0},{1,33},{33,65},{65,97},{97,1},{2,34}... | collective-permute-start | bytes 344072 | tf_op jit(solution)/shard_map/ppermute | solution.py:645
  75.3 9.8 %collective-permute-start.15 = (f32[3,16,128]{2,1,0:T(8,128)S(1)}, f32[3,16,128]{2,1,0:T(8,128)S(1)}, u32[]{:S(2)}, u32[]{:S(2)}) collective-permute-start(f32[3,16,128]{2,1,0:T(8,128)S(1)} %get-tuple-element.85), channel_id=1, source_target_pairs={{0,32},{32,64},{64,96},{96,0},{1,33},{33,65},{65,97},{97,1},{2,34}... | collective-permute-start | bytes 73736 | tf_op jit(solution)/shard_map/ppermute | solution.py:645
  75.4 9.7 %collective-permute-start.16 = (f32[3,16,128]{2,1,0:T(8,128)S(1)}, f32[3,16,128]{2,1,0:T(8,128)S(1)}, u32[]{:S(2)}, u32[]{:S(2)}) collective-permute-start(f32[3,16,128]{2,1,0:T(8,128)S(1)} %get-tuple-element.86), channel_id=1, source_target_pairs={{0,96},{32,0},{64,32},{96,64},{1,97},{33,1},{65,33},{97,65},{2,98}... | collective-permute-start | bytes 73736 | tf_op jit(solution)/shard_map/ppermute | solution.py:645
  78.6 6.5 %collective-permute-start.19 = (f32[2,16,128]{2,1,0:T(8,128)S(1)}, f32[2,16,128]{2,1,0:T(8,128)S(1)}, u32[]{:S(2)}, u32[]{:S(2)}) collective-permute-start(f32[2,16,128]{2,1,0:T(8,128)S(1)} %get-tuple-element.91), channel_id=1, source_target_pairs={{1,2},{3,4},{5,6},{7,8},{9,10},{11,12},{13,14},{15,16},{17,18},{19... | collective-permute-start | bytes 49160 | tf_op jit(solution)/shard_map/ppermute | solution.py:651
  80.5 9.9 %collective-permute-start.17 = (f32[1,16,128]{2,1,0:T(8,128)S(1)}, f32[1,16,128]{2,1,0:T(8,128)S(1)}, u32[]{:S(2)}, u32[]{:S(2)}) collective-permute-start(f32[1,16,128]{2,1,0:T(8,128)S(1)} %get-tuple-element.84.own), channel_id=1, source_target_pairs={{0,64},{32,96},{64,0},{96,32},{1,65},{33,97},{65,1},{97,33},{2,66}... | collective-permute-start | bytes 24584 | tf_op jit(solution)/shard_map/ppermute | solution.py:645
  90.4 7.1 %collective-permute-start.20 = (f32[2,16,128]{2,1,0:T(8,128)S(1)}, f32[2,16,128]{2,1,0:T(8,128)S(1)}, u32[]{:S(2)}, u32[]{:S(2)}) collective-permute-start(f32[2,16,128]{2,1,0:T(8,128)S(1)} %get-tuple-element.94.here_ref), channel_id=1, source_target_pairs={{0,2},{1,3},{2,4},{3,5},{4,6},{5,7},{6,8},{7,9},{8,10},{9,11},{10,... | collective-permute-start | bytes 49160 | tf_op jit(solution)/shard_map/ppermute | solution.py:645
  90.5 7.0 %collective-permute-start.21 = (f32[2,16,128]{2,1,0:T(8,128)S(1)}, f32[2,16,128]{2,1,0:T(8,128)S(1)}, u32[]{:S(2)}, u32[]{:S(2)}) collective-permute-start(f32[2,16,128]{2,1,0:T(8,128)S(1)} %get-tuple-element.94.here_ref), channel_id=1, source_target_pairs={{0,30},{1,31},{2,0},{3,1},{4,2},{5,3},{6,4},{7,5},{8,6},{9,7},{10,... | collective-permute-start | bytes 49160 | tf_op jit(solution)/shard_map/ppermute | solution.py:645
  95.8 7.9 %collective-permute-start.23 = (f32[18,16,128]{2,1,0:T(8,128)S(1)}, f32[18,16,128]{2,1,0:T(8,128)S(1)}, u32[]{:S(2)}, u32[]{:S(2)}) collective-permute-start(f32[18,16,128]{2,1,0:T(8,128)S(1)} %get-tuple-element.98), channel_id=1, source_target_pairs={{1,2},{3,4},{5,6},{7,8},{9,10},{11,12},{13,14},{15,16},{17,18},{19... | collective-permute-start | bytes 442376 | tf_op jit(solution)/shard_map/ppermute | solution.py:651
  97.6 13.5 %collective-permute-start.24 = (f32[16,16,128]{2,1,0:T(8,128)S(1)}, f32[16,16,128]{2,1,0:T(8,128)S(1)}, u32[]{:S(2)}, u32[]{:S(2)}) collective-permute-start(f32[16,16,128]{2,1,0:T(8,128)S(1)} %get-tuple-element.102), channel_id=1, source_target_pairs={{0,32},{32,64},{64,96},{96,0},{1,33},{33,65},{65,97},{97,1},{2,34}... | collective-permute-start | bytes 393224 | tf_op jit(solution)/shard_map/ppermute | solution.py:645
  97.6 13.5 %collective-permute-start.25 = (f32[16,16,128]{2,1,0:T(8,128)S(1)}, f32[16,16,128]{2,1,0:T(8,128)S(1)}, u32[]{:S(2)}, u32[]{:S(2)}) collective-permute-start(f32[16,16,128]{2,1,0:T(8,128)S(1)} %get-tuple-element.103), channel_id=1, source_target_pairs={{0,96},{32,0},{64,32},{96,64},{1,97},{33,1},{65,33},{97,65},{2,98}... | collective-permute-start | bytes 393224 | tf_op jit(solution)/shard_map/ppermute | solution.py:645
  105.1 11.4 %all-to-all-start.2 = ((f32[32,1,128]{2,1,0:T(1,128)}), f32[32,1,128]{2,1,0:T(1,128)S(1)}, u32[]{:S(2)}, u32[]{:S(2)}) async-start(f32[32,1,128]{2,1,0:T(1,128)} %get-tuple-element.100), calls=%async_computation.2 | async-start | bytes 32768 | tf_op jit(solution)/shard_map/all_to_all | solution.py:736
  (12 other events, 54.3 us)
